TPU v7x, 256 devices: a whole 4x4x8 slice. The times are simulated.
256 devices in a mesh: tm: 16 (over x, y), space: 16 (over z, core).
Axes of the slice: x: 4, y: 4, z: 8, core: 2. Of those that a mesh axis runs over, the one named last changes fastest.
Arguments:
- courant_x: float32 [16, 4, 128, 3072], P('tm', None, 'space'), may hold values from -0.45 to 0.45
- courant_y: float32 [16, 4, 128, 3072], P('tm', None, 'space'), may hold values from -0.45 to 0.45
- model_var: float32 [16, 4, 128, 3072], P('tm', None, 'space'), may hold values from 0.2 to 2
- obs_var: float32 [16, 16384], P('tm', 'space'), may hold values from 0.25 to 4
- obs_brick: int32 [16, 16384], P('tm'), may hold values from 0 to 15
- obs_cell: int32 [16, 16384], P('tm'), may hold values from 0 to 98303
- obs_step: int32 [16, 16384], P('tm'), may hold values from 0 to 1
- dual_state: float32 [16, 4, 128, 3072], P('tm', None, 'space'), may hold values from -6 to 6
- dual_obs: float32 [16, 16384], P('tm', 'space'), may hold values from -6 to 6
- increment: float32 [16, 4, 128, 3072], P('tm', None, 'space'), may hold values from -6 to 6
- resid_model: float32 [16, 4, 128, 3072], P('tm', None, 'space'), may hold values from -6 to 6
- resid_obs: float32 [16, 16384], P('tm', 'space'), may hold values from -6 to 6
- resid_state: float32 [16, 4, 128, 3072], P('tm', None, 'space'), may hold values from -6 to 6
Outputs:
- new_dual_state: float32 [16, 4, 128, 3072], P('tm', None, 'space')
- new_dual_obs: float32 [16, 16384], P('tm', 'space')
- new_increment: float32 [16, 4, 128, 3072], P('tm', None, 'space')
- new_resid_model: float32 [16, 4, 128, 3072], P('tm', None, 'space')
- new_resid_obs: float32 [16, 16384], P('tm', 'space')
- new_resid_state: float32 [16, 4, 128, 3072], P('tm', None, 'space')
Inputs may be any that keep to these rules, and one draw needn't show every extreme that they name: `obs_brick`: index of the brick of 8 rows that holds the observation. `obs_cell`: cell within the brick, levels slowest, then rows, then columns. `obs_step`: 0: taken at the sub-window's start; 1: after its first advection step.
All inputs are finite; a program needn't handle non-finite values.
Results may differ from a plain program's by a relative error of at most 0.00005.
Values sent between devices are 32-bit elements; how exact they have to be, the bound alone decides.
No kernel may reach another device: no remote copies, remote signals or barrier semaphores. Data moves between devices by JAX's collectives and lax.ppermute only.
A program may use at most 128 MiB of HBM per device.

v0:
```python
import jax
import jax.numpy as jnp
from jax import lax
from jax.sharding import PartitionSpec as P


def with_halo(block, sides, width):
    for axis, dim in sides:
        count = lax.axis_size(axis)
        forward = [(i, i + 1) for i in range(count - 1)]
        backward = [(target, source) for source, target in forward]
        low = lax.ppermute(
            lax.slice_in_dim(block, block.shape[dim] - width, None, axis=dim), axis, forward
        )
        high = lax.ppermute(lax.slice_in_dim(block, 0, width, axis=dim), axis, backward)
        block = jnp.concatenate([low, block, high], axis=dim)
    return block


def shifted(block, axis, distance):
    devices = range(lax.axis_size(axis))
    route = [(i - distance, i) for i in devices if i - distance in devices]
    return lax.ppermute(block, axis, route)


def carried_in(part, axis, combine, identity, reverse):
    count = lax.axis_size(axis)
    place = lax.axis_index(axis)
    ahead = count - 1 - place if reverse else place
    gathered = lax.all_gather(part, axis)
    state = jnp.zeros_like(part) + jnp.asarray(identity, part.dtype)

    def one(step, state):
        source = count - 1 - step if reverse else step
        return combine(state, lax.dynamic_index_in_dim(gathered, source, 0, False))

    return lax.fori_loop(0, ahead, one, state)


def weights_of(courant_x, courant_y):
    coef_west = jnp.maximum(courant_x, 0.0)
    coef_east = jnp.maximum(-courant_x, 0.0)
    coef_south = jnp.maximum(courant_y, 0.0)
    coef_north = jnp.maximum(-courant_y, 0.0)
    coef_self = 1.0 - jnp.abs(courant_x) - jnp.abs(courant_y)
    return (coef_self, coef_west, coef_east, coef_south, coef_north)


def step_rows(padded, coeffs):
    coef_self, coef_west, coef_east, coef_south, coef_north = coeffs
    centre = padded[:, 1:-1]
    return (
        coef_self * centre
        + coef_west * jnp.roll(centre, 1, axis=-1)
        + coef_east * jnp.roll(centre, -1, axis=-1)
        + coef_south * padded[:, :-2]
        + coef_north * padded[:, 2:]
    )


def forward_two(state_field, coeffs):

    def one_step(values):
        return step_rows(with_halo(values, (("space", 1),), 1), coeffs)

    after_one = one_step(state_field)
    after_two = one_step(after_one)
    return (after_one, after_two)


def backward_one(values, coeffs):
    coef_self, coef_west, coef_east, coef_south, coef_north = coeffs
    south_part = coef_south * values
    north_part = coef_north * values
    from_above = shifted(south_part[:, :1], "space", -1)
    from_below = shifted(north_part[:, -1:], "space", 1)
    up_part = jnp.concatenate([south_part[:, 1:], from_above], axis=1)
    down_part = jnp.concatenate([from_below, north_part[:, :-1]], axis=1)
    return (
        coef_self * values
        + jnp.roll(coef_west * values, -1, axis=-1)
        + jnp.roll(coef_east * values, 1, axis=-1)
        + up_part
        + down_part
    )


def add_fields(earlier, later):
    return earlier + later


def body(
    courant_x,
    courant_y,
    model_var,
    obs_var,
    obs_brick,
    obs_cell,
    obs_step,
    dual_state,
    dual_obs,
    increment,
    resid_model,
    resid_obs,
    resid_state,
):
    local_x = courant_x[0]
    local_y = courant_y[0]
    coeffs = weights_of(local_x, local_y)
    variance = model_var[0]
    res_model = resid_model[0]
    res_state = resid_state[0]
    blank_field = jnp.zeros_like(res_state)
    dual_step = carried_in(res_state, "tm", add_fields, blank_field, True) + res_state
    source = res_model - variance * dual_step
    incr_step = carried_in(source, "tm", add_fields, blank_field, False) + source
    after_one, after_two = forward_two(incr_step, coeffs)
    carried = shifted(after_two, "tm", 1)
    image_model = variance * dual_step + incr_step - carried
    bricks = obs_brick[0]
    obs_cells = obs_cell[0]
    sections = obs_step[0]
    in_brick = bricks == lax.axis_index("space")
    lanes = 128
    groups = incr_step.size // lanes
    count = obs_cells.shape[0]
    group_id = obs_cells // lanes
    lane_id = obs_cells % lanes
    row_hot = (
        (group_id[:, None] == jnp.arange(groups, dtype=jnp.int32)[None, :]) & in_brick[:, None]
    ).astype(jnp.float32)
    lane_hot = (lane_id[:, None] == jnp.arange(lanes, dtype=jnp.int32)[None, :]).astype(jnp.float32)
    both_fields = jnp.stack(
        [incr_step.reshape(groups, lanes), after_one.reshape(groups, lanes)], axis=1
    ).reshape(groups, 2 * lanes)
    picked = jnp.dot(
        row_hot, both_fields, precision=lax.Precision.HIGHEST, preferred_element_type=jnp.float32
    ).reshape(count, 2, lanes)
    values_two = jnp.sum(picked * lane_hot[:, None, :], axis=-1)
    local_vals = jnp.where(sections == 0, values_two[:, 0], values_two[:, 1])
    observed = lax.psum_scatter(local_vals[None], "space", scatter_dimension=1, tiled=True)
    dual_obs_step = resid_obs / obs_var
    image_obs = obs_var * dual_obs_step + observed
    all_duals = lax.all_gather(dual_obs_step, "space", axis=1, tiled=True)[0]
    owned = jnp.where(in_brick, all_duals, 0.0)
    weights_two = jnp.stack(
        [jnp.where(sections == 0, owned, 0.0), jnp.where(sections == 1, owned, 0.0)], axis=1
    )
    placed = (weights_two[:, :, None] * lane_hot[:, None, :]).reshape(count, 2 * lanes)
    spread = lax.dot_general(
        row_hot,
        placed,
        (((0,), (0,)), ((), ())),
        precision=lax.Precision.HIGHEST,
        preferred_element_type=jnp.float32,
    ).reshape(groups, 2, lanes)
    spread_start = spread[:, 0].reshape(incr_step.shape)
    spread_middle = spread[:, 1].reshape(incr_step.shape)
    next_dual = dual_step - res_state
    carried_back = backward_one(next_dual, coeffs)
    image_state = dual_step + spread_start + backward_one(spread_middle - carried_back, coeffs)
    local_projected = (
        jnp.sum(res_model * image_model)
        + jnp.sum(resid_obs * image_obs)
        + jnp.sum(res_state * image_state)
    )
    local_curvature = (
        jnp.sum(image_model * image_model)
        + jnp.sum(image_obs * image_obs)
        + jnp.sum(image_state * image_state)
    )
    projected, curvature = lax.psum((local_projected, local_curvature), ("tm", "space"))
    step_length = projected / curvature
    return (
        dual_state + step_length * dual_step[None],
        dual_obs + step_length * dual_obs_step,
        increment + step_length * incr_step[None],
        resid_model - step_length * image_model[None],
        resid_obs - step_length * image_obs,
        resid_state - step_length * image_state[None],
    )


def solution(mesh):
    placed = (
        P("tm", None, "space", None),
        P("tm", None, "space", None),
        P("tm", None, "space", None),
        P("tm", "space"),
        P("tm", None),
        P("tm", None),
        P("tm", None),
        P("tm", None, "space", None),
        P("tm", "space"),
        P("tm", None, "space", None),
        P("tm", None, "space", None),
        P("tm", "space"),
        P("tm", None, "space", None),
    )
    return jax.shard_map(
        body,
        mesh=mesh,
        in_specs=placed,
        out_specs=(
            P("tm", None, "space", None),
            P("tm", "space"),
            P("tm", None, "space", None),
            P("tm", None, "space", None),
            P("tm", "space"),
            P("tm", None, "space", None),
        ),
        check_vma=False,
    )
```

profile of v0, /device:TPU:1, one launch (start us, length us, event | category | flops | bytes accessed | tf_op | source)
XLA Modules:
  0.0 476.7 jit_solution(6474550639894338390)
XLA Ops:
  7.3 0.7 all-gather.4.cloned.1.call-update
  8.0 72.7 %all-gather.4.cloned.1.call-done = f32[16,4,8,3072]{3,2,1,0:T(8,128)} async-done(((f32[1,4,8,3072]{3,2,1,0:T(8,128)}), f32[16,4,8,3072]{3,2,1,0:T(8,128)}) %all-gather.4.cloned.1.call-update) | async-done | bytes 6291472 | tf_op jit(solution)/shard_map/all_gather | solution.py:30
  80.8 16.7 %while.22 = (s32[]{:T(128)}, f32[4,8,3072]{2,1,0:T(8,128)S(1)}, s32[]{:T(128)}, f32[16,4,8,3072]{3,2,1,0:T(8,128)}, s32[]{:T(128)}, /*index=5*/s32[]{:T(128)}, s32[]{:T(128)}, s32[]{:T(128)}) while((s32[]{:T(128)}, f32[4,8,3072]{2,1,0:T(8,128)S(1)}, s32[]{:T(128)}, f32[16,4,8,3072]{3,2,1,0:T(8,128)}, s32[]{:T(128)}, /*index=5*/s32[]{:T(128)}, ...), condition=%wide.region_1.2_spmd, body=%wide.region_0.1_spmd.sunk | while | flops 98310 | bytes 1179783 | solution.py:37
  80.8 1.1 bitcast_add_fusion.8
  81.9 1.1 bitcast_add_fusion.8
  83.0 1.1 bitcast_add_fusion.8
  84.1 1.1 bitcast_add_fusion.8
  85.2 1.1 bitcast_add_fusion.8
  86.3 1.1 bitcast_add_fusion.8
  87.4 1.1 bitcast_add_fusion.8
  88.6 1.1 bitcast_add_fusion.8
  89.7 1.1 bitcast_add_fusion.8
  90.8 1.1 bitcast_add_fusion.8
  91.9 1.1 bitcast_add_fusion.8
  93.0 1.1 bitcast_add_fusion.8
  94.1 1.1 bitcast_add_fusion.8
  95.2 1.1 bitcast_add_fusion.8
  96.3 1.1 bitcast_add_fusion.8
  97.4 1.2 bitcast_multiply_fusion.1
  98.7 0.8 bitcast_subtract_fusion.3
  99.6 0.8 compare_reduce_fusion
  100.4 0.7 add_select_fusion.1
  101.1 4.2 fusion.17
  105.9 3.7 collective-permute-start.6
  109.7 53.0 %all-gather.6.cloned.1.call-done = f32[64,8,3072]{2,1,0:T(8,128)} async-done(((f32[4,8,3072]{2,1,0:T(8,128)}), f32[64,8,3072]{2,1,0:T(8,128)}) %all-gather.6.cloned.1.call-update) | async-done | bytes 6291472 | tf_op jit(solution)/shard_map/all_gather | solution.py:30
  163.0 3.7 collective-permute-start
  166.8 1.9 collective-permute-start.1
  169.4 0.8 stack_reshape.6
  170.2 2.0 collective-permute-done.1
  172.8 2.0 bitcast_multiply_fusion.7
  174.8 0.8 slice.172
  176.2 0.9 slice.168
  177.2 0.8 stack_reshape.7
  178.0 1.0 fusion.51
  179.0 0.7 fusion.53
  179.7 1.2 pad_maximum_fusion
  180.9 1.2 copy.23
  182.1 29.5 %fusion.18 = f32[16384,2]{0,1:T(2,128)S(1)} fusion(f32[16384,128]{0,1:T(8,128)} %fusion.17, s32[16384]{0:T(1024)} %get-tuple-element.147, pred[16384]{0:T(1024)(128)(4,1)} %compare_reduce_fusion, f32[768,2,128]{0,2,1:T(8,128)} %copy.23), kind=kOutput, calls=%fused_computation.18 | convolution fusion | flops 38688227328 | bytes 9388032 | tf_op jit(solution)/shard_map/dot_general | solution.py:136
  211.8 4.9 %copy.27 = f32[1,16384]{0,1:T(8,128)} copy(f32[1,16384]{1,0:T(1,128)S(1)} %compare_select_fusion.3) | data formatting | bytes 131072
  216.7 1.9 collective-permute-start.5
  218.7 1.4 slice.170
  220.1 3.6 collective-permute-start.2
  223.7 1.9 collective-permute-start.3
  226.3 73.4 %reduce-scatter.4.cloned.1.call-done = f32[1024,1]{1,0:T(8,128)} async-done(((f32[16384,1]{1,0:T(8,128)}), f32[1024,1]{1,0:T(8,128)}) %reduce-scatter.4.cloned.1.call-update) | async-done | bytes 4112
  299.7 1.2 copy.28
  300.9 1.3 multiply_reduce_fusion.2
  302.2 17.8 %all_gather.15 = f32[1,16384]{1,0:T(1,128)S(1)} all-gather(f32[1,1024]{1,0:T(1,128)S(1)} %get-tuple-element.118), channel_id=1, replica_groups=mesh['tm'=16,'space'=16] {'space'}, dimensions={1}, use_global_device_ids=true | all-gather | bytes 69632 | tf_op jit(solution)/shard_map/all_gather | solution.py:144
  320.3 38.7 %fusion.2 = f32[768,2,128]{2,0,1:T(8,128)} fusion(s32[16384]{0:T(1024)S(1)} %copy-done.14, pred[16384]{0:T(1024)(128)(4,1)S(1)} %copy-done.18, f32[16384,2]{0,1:T(2,128)S(1)} %pad_maximum_fusion.5, f32[16384,128]{0,1:T(8,128)} %fusion.17), kind=kOutput, calls=%fused_computation.5 | convolution fusion | flops 38684065792 | bytes 9388032 | tf_op jit(solution)/shard_map/dot_general | solution.py:150
  359.0 2.0 fusion.50
  361.0 0.8 reshape_squeeze.7
  361.8 1.9 bitcast_multiply_fusion
  363.7 2.5 bitcast_multiply_fusion.6
  366.2 3.2 collective-permute-start.4
  370.1 2.3 collective-permute-start.7
  373.1 3.5 collective-permute-start.8
  376.6 0.8 slice.180
  377.3 0.9 slice.176
  379.0 1.8 reshape_squeeze.6
  380.8 0.7 copy-done.9
  381.5 3.0 multiply_reduce_fusion
  388.4 76.1 %all-reduce = (f32[]{:T(128)}, f32[]{:T(128)}) all-reduce(f32[]{:T(128)S(6)} %add.161, f32[]{:T(128)S(6)} %add.163), channel_id=1, replica_groups=mesh['tm'=16,'space'=16] {'tm','space'}, use_global_device_ids=true, to_apply=%region_9.10 | all-reduce | flops 2 | bytes 16 | tf_op jit(solution)/shard_map/psum | solution.py:172
  465.8 1.0 bitcast_subtract_fusion
  466.7 1.3 multiply_subtract_fusion
  468.1 2.1 bitcast_add_fusion.2
  (72 shorter events, 6.3 us)
Async XLA Ops:
  7.2 91.5 %copy-start.8 = (f32[1,4,8,3072]{3,2,1,0:T(8,128)S(1)}, f32[1,4,8,3072]{3,2,1,0:T(8,128)}, u32[]{:S(2)}) copy-start(f32[1,4,8,3072]{3,2,1,0:T(8,128)} %param.19) | copy-start | bytes 1179652
  7.2 91.5 %copy-start.3 = (f32[1,4,8,3072]{3,2,1,0:T(8,128)S(1)}, f32[1,4,8,3072]{3,2,1,0:T(8,128)}, u32[]{:S(2)}) copy-start(f32[1,4,8,3072]{3,2,1,0:T(8,128)} %param.27) | copy-start | bytes 1179652
  7.2 92.4 %copy-start.10 = (s32[1,16384]{1,0:T(1,128)S(1)}, s32[1,16384]{1,0:T(1,128)}, u32[]{:S(2)}) copy-start(s32[1,16384]{1,0:T(1,128)} %param.21) | copy-start | bytes 196612
  7.2 93.2 %copy-start.13 = (s32[1,16384]{1,0:T(1,128)S(1)}, s32[1,16384]{1,0:T(1,128)}, u32[]{:S(2)}) copy-start(s32[1,16384]{1,0:T(1,128)} %param.22) | copy-start | bytes 196612
  7.2 73.5 %all-gather.4.cloned.1.call-start = ((), (), s32[]{:S(2)}) async-start(), calls=%async_computation.1 | async-start | bytes 6684672 | tf_op jit(solution)/shard_map/all_gather | solution.py:30
  7.9 154.7 %all-gather.6.cloned.1.call-start = ((), (), s32[]{:S(2)}) async-start(), calls=%async_computation.2 | async-start | bytes 6684672 | tf_op jit(solution)/shard_map/all_gather | solution.py:30
  98.6 64.0 %copy-start.5 = (f32[4,8,3072]{2,1,0:T(8,128)}, f32[4,8,3072]{2,1,0:T(8,128)S(1)}, u32[]{:S(2)}) copy-start(f32[4,8,3072]{2,1,0:T(8,128)S(1)} %get-tuple-element.114) | copy-start | bytes 1179652
  99.5 63.2 %copy-start.4 = (f32[4,8,3072]{2,1,0:T(8,128)S(1)}, f32[4,8,3072]{2,1,0:T(8,128)}, u32[]{:S(2)}) copy-start(f32[4,8,3072]{2,1,0:T(8,128)} %bitcast_subtract_fusion.3) | copy-start | bytes 1179652
  99.5 200.1 %reduce-scatter.4.cloned.1.call-start = ((), (), s32[]{:S(2)}) async-start(), calls=%async_computation.3 | async-start | bytes 8912896
  101.1 71.7 %copy-start = (f32[1,4,8,3072]{3,2,1,0:T(8,128)S(1)}, f32[1,4,8,3072]{3,2,1,0:T(8,128)}, u32[]{:S(2)}) copy-start(f32[1,4,8,3072]{3,2,1,0:T(8,128)} %param.18) | copy-start | bytes 1179652
  101.1 71.7 %copy-start.2 = (f32[1,4,8,3072]{3,2,1,0:T(8,128)S(1)}, f32[1,4,8,3072]{3,2,1,0:T(8,128)}, u32[]{:S(2)}) copy-start(f32[1,4,8,3072]{3,2,1,0:T(8,128)} %param.17) | copy-start | bytes 1179652
  105.9 255.9 %collective-permute-start.6 = (f32[4,1,3072]{2,1,0:T(1,128)}, f32[4,1,3072]{2,1,0:T(1,128)}, u32[]{:S(2)}, u32[]{:S(2)}) collective-permute-start(f32[4,1,3072]{2,1,0:T(1,128)} %slice.174), channel_id=1, source_target_pairs={{0,1},{1,2},{2,3},{3,4},{4,5},{5,6},{6,7},{7,8},{8,9},{9,10},{10,1... | collective-permute-start | bytes 147464 | tf_op jit(solution)/shard_map/ppermute | solution.py:23
  163.0 7.2 %collective-permute-start = (f32[4,1,3072]{2,1,0:T(1,128)S(1)}, f32[4,1,3072]{2,1,0:T(1,128)S(1)}, u32[]{:S(2)}, u32[]{:S(2)}) collective-permute-start(f32[4,1,3072]{2,1,0:T(1,128)S(1)} %get-tuple-element.143), channel_id=1, source_target_pairs={{0,1},{1,2},{2,3},{3,4},{4,5},{5,6},{6,7},{7,8},{8,9},{9,10},{10,1... | collective-permute-start | bytes 147464 | tf_op jit(solution)/shard_map/ppermute | solution.py:12
  166.8 5.4 %collective-permute-start.1 = (f32[4,1,3072]{2,1,0:T(1,128)S(1)}, f32[4,1,3072]{2,1,0:T(1,128)S(1)}, u32[]{:S(2)}, u32[]{:S(2)}) collective-permute-start(f32[4,1,3072]{2,1,0:T(1,128)S(1)} %get-tuple-element.144), channel_id=1, source_target_pairs={{1,0},{2,1},{3,2},{4,3},{5,4},{6,5},{7,6},{8,7},{9,8},{10,9},{11,1... | collective-permute-start | bytes 147464 | tf_op jit(solution)/shard_map/ppermute | solution.py:15
  170.2 2.0 copy-start.15
  172.2 0.6 copy-start.16
  182.1 29.5 %copy-start.12 = (s32[1,16384]{1,0:T(1,128)S(1)}, s32[1,16384]{1,0:T(1,128)}, u32[]{:S(2)}) copy-start(s32[1,16384]{1,0:T(1,128)} %param.23) | copy-start | bytes 196612
  211.7 89.2 %copy-start.19 = (f32[1,1024]{1,0:T(1,128)S(1)}, f32[1,1024]{1,0:T(1,128)}, u32[]{:S(2)}) copy-start(f32[1,1024]{1,0:T(1,128)} %param.28) | copy-start | bytes 12292
  211.8 89.2 %copy-start.20 = (f32[1,1024]{1,0:T(1,128)S(1)}, f32[1,1024]{1,0:T(1,128)}, u32[]{:S(2)}) copy-start(f32[1,1024]{1,0:T(1,128)} %param.20) | copy-start | bytes 12292
  211.8 108.2 %copy-start.11 = (s32[1,16384]{1,0:T(1,128)S(1)}, s32[1,16384]{1,0:T(1,128)}, u32[]{:S(2)}) copy-start(s32[1,16384]{1,0:T(1,128)} %param.21) | copy-start | bytes 196612
  211.8 108.5 %copy-start.14 = (s32[16384]{0:T(1024)S(1)}, s32[16384]{0:T(1024)}, u32[]{:S(2)}) copy-start(s32[16384]{0:T(1024)} %get-tuple-element.147) | copy-start | bytes 196612
  211.8 108.5 %copy-start.18 = (pred[16384]{0:T(1024)(128)(4,1)S(1)}, pred[16384]{0:T(1024)(128)(4,1)}, u32[]{:S(2)}) copy-start(pred[16384]{0:T(1024)(128)(4,1)} %compare_reduce_fusion) | copy-start | bytes 49156
  216.7 145.1 %collective-permute-start.5 = (f32[4,1,3072]{2,1,0:T(1,128)}, f32[4,1,3072]{2,1,0:T(1,128)}, u32[]{:S(2)}, u32[]{:S(2)}) collective-permute-start(f32[4,1,3072]{2,1,0:T(1,128)} %slice.173), channel_id=1, source_target_pairs={{1,0},{2,1},{3,2},{4,3},{5,4},{6,5},{7,6},{8,7},{9,8},{10,9},{11,1... | collective-permute-start | bytes 147464 | tf_op jit(solution)/shard_map/ppermute | solution.py:23
  220.1 143.6 %collective-permute-start.2 = (f32[4,1,3072]{2,1,0:T(1,128)}, f32[4,1,3072]{2,1,0:T(1,128)}, u32[]{:S(2)}, u32[]{:S(2)}) collective-permute-start(f32[4,1,3072]{2,1,0:T(1,128)} %get-tuple-element.137), channel_id=1, source_target_pairs={{0,1},{1,2},{2,3},{3,4},{4,5},{5,6},{6,7},{7,8},{8,9},{9,10},{10,1... | collective-permute-start | bytes 147464 | tf_op jit(solution)/shard_map/ppermute | solution.py:12
  223.7 140.0 %collective-permute-start.3 = (f32[4,1,3072]{2,1,0:T(1,128)}, f32[4,1,3072]{2,1,0:T(1,128)}, u32[]{:S(2)}, u32[]{:S(2)}) collective-permute-start(f32[4,1,3072]{2,1,0:T(1,128)} %get-tuple-element.138), channel_id=1, source_target_pairs={{1,0},{2,1},{3,2},{4,3},{5,4},{6,5},{7,6},{8,7},{9,8},{10,9},{11,1... | collective-permute-start | bytes 147464 | tf_op jit(solution)/shard_map/ppermute | solution.py:15
  302.2 18.1 %copy-start.17 = (f32[1,1024]{1,0:T(1,128)}, f32[1,1024]{1,0:T(1,128)S(1)}, u32[]{:S(2)}) copy-start(f32[1,1024]{1,0:T(1,128)S(1)} %get-tuple-element.118) | copy-start | bytes 12292
  359.0 22.5 %copy-start.1 = (f32[1,4,8,3072]{3,2,1,0:T(8,128)S(1)}, f32[1,4,8,3072]{3,2,1,0:T(8,128)}, u32[]{:S(2)}) copy-start(f32[1,4,8,3072]{3,2,1,0:T(8,128)} %param.29) | copy-start | bytes 1179652
  363.7 8.8 %copy-start.6 = (f32[4,8,3072]{2,1,0:T(8,128)}, f32[4,8,3072]{2,1,0:T(8,128)S(1)}, u32[]{:S(2)}) copy-start(f32[4,8,3072]{2,1,0:T(8,128)S(1)} %get-tuple-element.112) | copy-start | bytes 1179652
  366.2 12.1 %copy-start.7 = (f32[4,8,3072]{2,1,0:T(8,128)}, f32[4,8,3072]{2,1,0:T(8,128)S(1)}, u32[]{:S(2)}) copy-start(f32[4,8,3072]{2,1,0:T(8,128)S(1)} %get-tuple-element.123) | copy-start | bytes 1179652
  366.2 14.6 %collective-permute-start.4 = (f32[4,8,3072]{2,1,0:T(8,128)}, f32[4,8,3072]{2,1,0:T(8,128)S(1)}, u32[]{:S(2)}, u32[]{:S(2)}) collective-permute-start(f32[4,8,3072]{2,1,0:T(8,128)} %get-tuple-element.129), channel_id=1, source_target_pairs={{0,16},{16,32},{32,48},{48,64},{64,80},{80,96},{96,112},{112,128},... | collective-permute-start | bytes 1179656 | tf_op jit(solution)/shard_map/ppermute | solution.py:23
  370.1 10.7 %collective-permute-start.7 = (f32[4,1,3072]{2,1,0:T(1,128)}, f32[4,1,3072]{2,1,0:T(1,128)}, u32[]{:S(2)}, u32[]{:S(2)}) collective-permute-start(f32[4,1,3072]{2,1,0:T(1,128)} %slice.181), channel_id=1, source_target_pairs={{1,0},{2,1},{3,2},{4,3},{5,4},{6,5},{7,6},{8,7},{9,8},{10,9},{11,1... | collective-permute-start | bytes 147464 | tf_op jit(solution)/shard_map/ppermute | solution.py:23
  373.1 7.7 %collective-permute-start.8 = (f32[4,1,3072]{2,1,0:T(1,128)}, f32[4,1,3072]{2,1,0:T(1,128)}, u32[]{:S(2)}, u32[]{:S(2)}) collective-permute-start(f32[4,1,3072]{2,1,0:T(1,128)} %slice.182), channel_id=1, source_target_pairs={{0,1},{1,2},{2,3},{3,4},{4,5},{5,6},{6,7},{7,8},{8,9},{9,10},{10,1... | collective-permute-start | bytes 147464 | tf_op jit(solution)/shard_map/ppermute | solution.py:23
  380.8 0.7 copy-start.9
Sparse Core Ops, SparseCore 0:
  10.5 70.1 all-gather.3
  99.7 62.9 all-gather.5
  216.9 82.7 reduce-scatter.3
where the time goes:
time: 478 us; the launch traced here: 477 us
  waiting for transfers between devices  202 us (42%)
  blocking collectives  93.8 us (20%)
  matrix products  68.2 us (14%)
  other arithmetic  40.6 us (8%)
  local copies, waits for them, and re-layouts  26.5 us (6%)
  starting transfers between devices  26 us (5%)
  between operations  19.3 us (4%)
    all_gather x2, waiting for transfers between devices, carried_in(): gathered = lax.all_gather(part, axis)  126 us
    psum x1, blocking collectives, body(): lax.psum((local_projected, local_curvature), ('tm', 'space'))  76.1 us
    unnamed x4, waiting for transfers between devices  74.1 us
    dot_general x1, matrix products, body(): lax.dot_general(row_hot, placed, (((0,), (0,)), ((), ())), precision=lax....  38.7 us
    dot_general x1, matrix products, body(): jnp.dot(row_hot, both_fields, precision=lax.Precision.HIGHEST, preferred_...  29.5 us
    all_gather x1, blocking collectives, body(): all_duals = lax.all_gather(dual_obs_step, 'space', axis=1, tiled=True)[0]  17.8 us
    add x15, other arithmetic, add_fields(): return earlier + later  16.2 us
    ppermute x5, starting transfers between devices, shifted(): return lax.ppermute(block, axis, route)  14.7 us
  transfers between devices with their start and end apart: 12, of which 4 were waited for; matrix products, arithmetic and copies ran while one was open for 22% of the time, Pallas kernels for 0%

commit v1 on v0

v1 whole, which is shorter than its diff:
```python
import functools

import jax
import jax.numpy as jnp
from jax import lax
from jax.experimental import pallas as pl
from jax.experimental.pallas import tpu as pltpu
from jax.sharding import PartitionSpec as P

LANES = 128
SLOTS = 128
BLOCK = 1024
MIB = 1024 * 1024


def params(mib):
    return pltpu.CompilerParams(vmem_limit_bytes=mib * MIB)


def cost(flops, touched):
    return pl.CostEstimate(flops=flops, bytes_accessed=touched, transcendentals=0)


VMEM = pl.BlockSpec(memory_space=pltpu.VMEM)
SMEM = pl.BlockSpec(memory_space=pltpu.SMEM)


def f32(*shape):
    return jax.ShapeDtypeStruct(shape, jnp.float32)


def i32(*shape):
    return jax.ShapeDtypeStruct(shape, jnp.int32)


def pack_kernel(parts, rs_ref, rm_ref, mv_ref, out_ref):
    levels, rows, columns = rs_ref.shape
    per_level = parts // levels
    width = columns // per_level
    for level in range(levels):
        for piece in range(per_level):
            part = level * per_level + piece
            cols = slice(piece * width, (piece + 1) * width)
            for place, ref in enumerate((rs_ref, rm_ref, mv_ref)):
                out_ref[part, rows * place : rows * (place + 1), :] = ref[level, :, cols]


def scan_kernel(in_ref, out_ref):
    steps = in_ref.shape[0]
    rows = in_ref.shape[1] // 3
    later = jnp.zeros((rows, in_ref.shape[2]), jnp.float32)
    for t in reversed(range(steps)):
        out_ref[t, rows : 2 * rows, :] = later
        later = later + in_ref[t, 0:rows, :]
        out_ref[t, 0:rows, :] = (
            in_ref[t, rows : 2 * rows, :] - in_ref[t, 2 * rows : 3 * rows, :] * later
        )
    total = jnp.zeros((rows, in_ref.shape[2]), jnp.float32)
    for t in range(steps):
        total = total + out_ref[t, 0:rows, :]
        out_ref[t, 0:rows, :] = total


def edge_kernel(levels, back_ref, up_ref, down_ref):
    parts, _, width = back_ref.shape
    per_level = parts // levels
    for part in range(parts):
        level, piece = part // per_level, part % per_level
        cols = slice(piece * width, (piece + 1) * width)
        for field in range(2):
            base = 8 * field
            for out_ref, rows in ((up_ref, (7, 6)), (down_ref, (0, 1))):
                for place, row in enumerate(rows):
                    at = base + 4 * place + level
                    out_ref[at : at + 1, cols] = back_ref[part, base + row : base + row + 1, :]


def courant_edge_kernel(cx_ref, cy_ref, up_ref, down_ref):
    levels = cx_ref.shape[0]
    for level in range(levels):
        for out_ref, rows in ((up_ref, (7, 6)), (down_ref, (0, 1))):
            first, second = rows
            out_ref[level : level + 1, :] = cx_ref[level, first : first + 1, :]
            out_ref[4 + level : 5 + level, :] = cy_ref[level, first : first + 1, :]
            out_ref[8 + level : 9 + level, :] = cy_ref[level, second : second + 1, :]
            out_ref[12 + level : 13 + level, :] = cy_ref[level, second : second + 1, :]


def place_kernel(columns, at_ref, brick_ref, cell_ref, step_ref, rank_ref, code_ref, passes_ref,
                 brick_s, cell_s, step_s):
    blocks = rank_ref.shape[0]
    here = at_ref[0]
    lane_groups = columns // LANES
    for k in range(blocks):
        cols = slice(k * BLOCK, (k + 1) * BLOCK)
        brick_s[k : k + 1, :] = brick_ref[0:1, cols]
        cell_s[k : k + 1, :] = cell_ref[0:1, cols]
        step_s[k : k + 1, :] = step_ref[0:1, cols]
    brick, cell, step = brick_s[...], cell_s[...], step_s[...]
    line = ((cell >> 10) * 171) >> 9
    level, row = line >> 3, line & 7
    column = cell - line * columns
    group, lane = column >> 7, column & 127
    own = brick == here
    below = (brick == here - 1) & (row == 7) & (step == 1)
    above = (brick == here + 1) & (row == 0) & (step == 1)
    halo_base = 4 * lane_groups * 8
    own_group = (level * lane_groups + group) * 8 + row
    halo_group = halo_base + group * 8 + level + jnp.where(above, 4, 0)
    code_ref[...] = jnp.where(own, own_group, halo_group) * 256 + step * LANES + lane
    inside = own | below | above
    count = inside.astype(jnp.int32)
    lanes = lax.broadcasted_iota(jnp.int32, count.shape, 1)
    shift = 1
    while shift < BLOCK:
        count = count + jnp.where(lanes >= shift, pltpu.roll(count, shift, 1), 0)
        shift *= 2
    rank_ref[...] = jnp.where(inside, count - 1, -1)
    passes_ref[0] = (jnp.max(count) + SLOTS - 1) // SLOTS


def slot_codes(rank_row, code_row, first):
    slot = lax.broadcasted_iota(jnp.int32, (SLOTS, BLOCK), 0) + first
    held = jnp.broadcast_to(rank_row, (SLOTS, BLOCK)) == slot
    code = jnp.max(
        jnp.where(held, jnp.broadcast_to(code_row, (SLOTS, BLOCK)), -1), axis=1, keepdims=True
    )
    return held, code


def split_two(x):
    high = x.astype(jnp.bfloat16)
    low = (x - high.astype(jnp.float32)).astype(jnp.bfloat16)
    return high, low


def spread_kernel(at_ref, passes_ref, rank_ref, code_ref, duals_ref, start_ref, middle_ref, edge_ref,
                  total, hot_s, high_s, low_s):
    blocks = rank_ref.shape[0]
    groups = total.shape[0]
    here = at_ref[0]
    levels, _, columns = start_ref.shape
    lane_groups = columns // LANES
    together = min(4, blocks)
    total[...] = jnp.zeros_like(total)
    eye = (lax.broadcasted_iota(jnp.int32, (SLOTS, SLOTS), 0)
           == lax.broadcasted_iota(jnp.int32, (SLOTS, SLOTS), 1))
    group_id = lax.broadcasted_iota(jnp.int32, (groups, SLOTS), 0)
    column_id = lax.broadcasted_iota(jnp.int32, (SLOTS, 2 * LANES), 1)

    def one_pass(number, carry):
        first = number * SLOTS

        def some_blocks(q, carry):
            for j in range(together):
                k = q * together + j
                held, code = slot_codes(rank_ref[pl.ds(k, 1), :], code_ref[pl.ds(k, 1), :], first)
                dual_row = duals_ref[pl.ds(lax.bitwise_xor(k, here), 1), BLOCK : 2 * BLOCK]
                dual = jnp.sum(
                    jnp.where(held, jnp.broadcast_to(dual_row, (SLOTS, BLOCK)), 0.0),
                    axis=1, keepdims=True,
                )
                group = jnp.max(
                    jnp.where(eye, jnp.broadcast_to(code >> 8, (SLOTS, SLOTS)), -1),
                    axis=0, keepdims=True,
                )
                hot_s[:, j * SLOTS : (j + 1) * SLOTS] = (
                    (group_id == jnp.broadcast_to(group, (groups, SLOTS)))
                    .astype(jnp.float32).astype(jnp.bfloat16)
                )
                placed = jnp.where(
                    column_id == jnp.broadcast_to(code & 255, (SLOTS, 2 * LANES)),
                    jnp.broadcast_to(dual, (SLOTS, 2 * LANES)), 0.0,
                )
                high, low = split_two(placed)
                high_s[j * SLOTS : (j + 1) * SLOTS, :] = high
                low_s[j * SLOTS : (j + 1) * SLOTS, :] = low
            total[...] += jnp.dot(
                hot_s[...], high_s[...], preferred_element_type=jnp.float32
            ) + jnp.dot(hot_s[...], low_s[...], preferred_element_type=jnp.float32)
            return carry

        return lax.fori_loop(0, blocks // together, some_blocks, carry)

    lax.fori_loop(0, passes_ref[0], one_pass, 0)
    for level in range(levels):
        for g in range(lane_groups):
            at = (level * lane_groups + g) * 8
            cols = slice(g * LANES, (g + 1) * LANES)
            start_ref[level, :, cols] = total[at : at + 8, 0:LANES]
            middle_ref[level, :, cols] = total[at : at + 8, LANES : 2 * LANES]
    base = levels * lane_groups * 8
    for g in range(lane_groups):
        edge_ref[:, g * LANES : (g + 1) * LANES] = total[
            base + 8 * g : base + 8 * g + 8, LANES : 2 * LANES
        ]


def west_of(v):
    return pltpu.roll(v, 1, 1)


def east_of(v):
    return pltpu.roll(v, v.shape[1] - 1, 1)


def weights_of(cx, cy):
    west, east = jnp.maximum(cx, 0.0), jnp.maximum(-cx, 0.0)
    south, north = jnp.maximum(cy, 0.0), jnp.maximum(-cy, 0.0)
    return 1.0 - jnp.abs(cx) - jnp.abs(cy), west, east, south, north


def forward(v, below, above, coeffs):
    own, west, east, south, north = coeffs
    return own * v + west * west_of(v) + east * east_of(v) + south * below + north * above


def adjoint(v, from_above, from_below, coeffs):
    own, west, east, _, _ = coeffs
    return own * v + east_of(west * v) + west_of(east * v) + from_above + from_below


def row_below(v, edge, first):
    return jnp.where(first, jnp.broadcast_to(edge, v.shape), pltpu.roll(v, 1, 0))


def row_above(v, edge, last):
    return jnp.where(last, jnp.broadcast_to(edge, v.shape), pltpu.roll(v, v.shape[0] - 1, 0))


def stacked(low, high):
    return jnp.concatenate([low, high], axis=0)


def image_kernel(where_ref, passes_ref, back_ref, up_ref, down_ref, below_ref, above_ref, cx_ref, cy_ref,
                 cup_ref, cdown_ref, cbelow_ref, cabove_ref, start_ref, middle_ref, edge_ref,
                 rs_ref, rm_ref, rm_next_ref, rank_ref, code_ref, obs_ref,
                 next_ref, state_ref, sent_ref, fields, hot_s, found):
    levels, rows, columns = cx_ref.shape
    parts, _, width = back_ref.shape
    per_level = parts // levels
    blocks = rank_ref.shape[0]
    lane_groups = columns // LANES
    window, windows, here = where_ref[0], where_ref[1], where_ref[2]

    cx_edge = stacked(cbelow_ref[0:4, :], cabove_ref[0:4, :])
    cy_edge = stacked(cbelow_ref[4:8, :], cabove_ref[4:8, :])
    cy_edge_below = stacked(cbelow_ref[8:12, :], cup_ref[4:8, :])
    cy_edge_above = stacked(cdown_ref[4:8, :], cabove_ref[8:12, :])
    edge_coeffs = weights_of(cx_edge, cy_edge)
    incr_edge = stacked(below_ref[0:4, :], above_ref[0:4, :])
    one_edge = forward(
        incr_edge,
        stacked(below_ref[4:8, :], up_ref[0:4, :]),
        stacked(down_ref[0:4, :], above_ref[4:8, :]),
        edge_coeffs,
    )
    dual_edge = stacked(below_ref[8:12, :], above_ref[8:12, :])
    dual_below = stacked(below_ref[12:16, :], up_ref[8:12, :])
    dual_above = stacked(down_ref[8:12, :], above_ref[12:16, :])
    kept_edge = edge_ref[...] - adjoint(
        dual_edge,
        jnp.maximum(cy_edge_above, 0.0) * dual_above,
        jnp.maximum(-cy_edge_below, 0.0) * dual_below,
        edge_coeffs,
    )
    edge_north, edge_south = edge_coeffs[4], edge_coeffs[3]
    dual_flux = jnp.where(
        lax.broadcasted_iota(jnp.int32, cx_edge.shape, 0) < 4, edge_north, edge_south
    )
    kept_flux = dual_flux * kept_edge
    dual_flux = dual_flux * dual_edge

    row_id = lax.broadcasted_iota(jnp.int32, (rows, columns), 0)
    first, last = row_id == 0, row_id == rows - 1
    projected = jnp.zeros((rows, columns), jnp.float32)
    curvature = jnp.zeros((rows, columns), jnp.float32)
    has_next = jnp.where(window < windows - 1, 1.0, 0.0)
    is_first = jnp.where(window == 0, 1.0, 0.0)
    for level in range(levels):
        pieces = range(level * per_level, (level + 1) * per_level)
        incr = jnp.concatenate([back_ref[p, 0:rows, :] for p in pieces], axis=1)
        next_dual = jnp.concatenate([back_ref[p, rows : 2 * rows, :] for p in pieces], axis=1)
        coeffs = weights_of(cx_ref[level], cy_ref[level])
        south, north = coeffs[3], coeffs[4]
        low, high = slice(level, level + 1), slice(4 + level, 5 + level)
        after_one = forward(
            incr,
            row_below(incr, incr_edge[low], first),
            row_above(incr, incr_edge[high], last),
            coeffs,
        )
        after_two = forward(
            after_one,
            row_below(after_one, one_edge[low], first),
            row_above(after_one, one_edge[high], last),
            coeffs,
        )
        rm_next = rm_next_ref[level]
        image_next = (rm_next + incr - after_two) * has_next
        next_ref[level] = image_next
        back_one = adjoint(
            next_dual,
            row_above(south * next_dual, dual_flux[high], last),
            row_below(north * next_dual, dual_flux[low], first),
            coeffs,
        )
        kept = middle_ref[level] - back_one
        rs, rm = rs_ref[level], rm_ref[level]
        image_state = (next_dual + rs) + start_ref[level] + adjoint(
            kept,
            row_above(south * kept, kept_flux[high], last),
            row_below(north * kept, kept_flux[low], first),
            coeffs,
        )
        state_ref[level] = image_state
        at_first = is_first * rm * rm
        projected += rm_next * image_next + rs * image_state + at_first
        curvature += image_next * image_next + image_state * image_state + at_first
        for g in range(lane_groups):
            at = (level * lane_groups + g) * 8
            cols = slice(g * LANES, (g + 1) * LANES)
            fields[at : at + 8, 0:LANES] = incr[:, cols]
            fields[at : at + 8, LANES : 2 * LANES] = after_one[:, cols]

    high_fields, low_fields = split_two(fields[...])
    groups = levels * lane_groups * 8
    group_id = lax.broadcasted_iota(jnp.int32, (SLOTS, groups), 1)
    column_id = lax.broadcasted_iota(jnp.int32, (SLOTS, 2 * LANES), 1)
    together = min(4, blocks)
    found[...] = jnp.zeros_like(found)

    def one_pass(number, carry):
        first_slot = number * SLOTS

        def some_blocks(q, carry):
            columns_of, helds = [], []
            for j in range(together):
                k = q * together + j
                held, code = slot_codes(
                    rank_ref[pl.ds(k, 1), :], code_ref[pl.ds(k, 1), :], first_slot
                )
                hot_s[j * SLOTS : (j + 1) * SLOTS, :] = (
                    (group_id == jnp.broadcast_to(code >> 8, (SLOTS, groups)))
                    .astype(jnp.float32).astype(jnp.bfloat16)
                )
                columns_of.append(code & 255)
                helds.append(held)
            picked = jnp.dot(
                hot_s[...], high_fields, preferred_element_type=jnp.float32
            ) + jnp.dot(hot_s[...], low_fields, preferred_element_type=jnp.float32)
            for j in range(together):
                k = q * together + j
                value = jnp.sum(
                    jnp.where(
                        column_id == jnp.broadcast_to(columns_of[j], (SLOTS, 2 * LANES)),
                        picked[j * SLOTS : (j + 1) * SLOTS, :], 0.0,
                    ),
                    axis=1, keepdims=True,
                )
                found[pl.ds(k, 1), :] += jnp.sum(
                    jnp.where(helds[j], jnp.broadcast_to(value, (SLOTS, BLOCK)), 0.0),
                    axis=0, keepdims=True,
                )
            return carry

        return lax.fori_loop(0, blocks // together, some_blocks, carry)

    lax.fori_loop(0, passes_ref[0], one_pass, 0)

    observed = found[...]
    sent_ref[:, 0:BLOCK] = observed
    resid = jnp.concatenate(
        [obs_ref[pl.ds(lax.bitwise_xor(k, here), 1), 0:BLOCK] for k in range(blocks)], axis=0
    )
    own = (rank_ref[...] >= 0) & (code_ref[...] < groups * 256)
    image_obs = jnp.where(own, resid + observed, 0.0)
    all_projected = jnp.sum(projected) + jnp.sum(resid * image_obs)
    all_curvature = jnp.sum(curvature) + jnp.sum(image_obs * image_obs)
    lane = lax.broadcasted_iota(jnp.int32, (blocks, LANES), 1)
    sent_ref[:, BLOCK : BLOCK + LANES] = jnp.where(
        lane == 0, all_projected, jnp.where(lane == 1, all_curvature, 0.0)
    )


def gather_kernel(got_ref, observed_ref, sums_ref):
    total = jnp.sum(got_ref[...], axis=0, keepdims=True)
    observed_ref[...] = total[:, 0:BLOCK]
    sums_ref[...] = jnp.broadcast_to(total[:, BLOCK : BLOCK + LANES], sums_ref.shape)


def update_kernel(where_ref, sums_ref, ds_ref, inc_ref, rm_ref, rs_ref, back_ref, image_ref, state_ref,
                  do_ref, ro_ref, ov_ref, observed_ref,
                  ds_out, do_out, inc_out, rm_out, ro_out, rs_out):
    sums = jnp.sum(sums_ref[...], axis=0, keepdims=True)
    lane = lax.broadcasted_iota(jnp.int32, sums.shape, 1)
    projected = jnp.sum(jnp.where(lane == 0, sums, 0.0), axis=1, keepdims=True)
    curvature = jnp.sum(jnp.where(lane == 1, sums, 0.0), axis=1, keepdims=True)
    step = projected / curvature
    rows = rs_ref.shape[1]
    parts, _, width = back_ref.shape
    wide = jnp.broadcast_to(step, (rows, width))
    starts = where_ref[0] == 0
    for piece in range(parts):
        cols = slice(piece * width, (piece + 1) * width)
        dual = back_ref[piece, rows : 2 * rows, :] + rs_ref[0, :, cols]
        ds_out[0, :, cols] = ds_ref[0, :, cols] + wide * dual
        inc_out[0, :, cols] = inc_ref[0, :, cols] + wide * back_ref[piece, 0:rows, :]
        rm = rm_ref[0, :, cols]
        image = jnp.where(starts, rm, image_ref[0, :, cols])
        rm_out[0, :, cols] = rm - wide * image
        rs_out[0, :, cols] = rs_ref[0, :, cols] - wide * state_ref[0, :, cols]

    @pl.when(pl.program_id(0) == 0)
    def _():
        narrow = jnp.broadcast_to(step, ro_ref.shape)
        ro, ov = ro_ref[...], ov_ref[...]
        dual = ro / ov
        do_out[...] = do_ref[...] + narrow * dual
        ro_out[...] = ro - narrow * (ov * dual + observed_ref[...])


def body(windows, bricks, courant_x, courant_y, model_var, obs_var, obs_brick, obs_cell, obs_step,
         dual_state, dual_obs, increment, resid_model, resid_obs, resid_state):
    cx, cy, mv = courant_x[0], courant_y[0], model_var[0]
    ds, inc, rm, rs = dual_state[0], increment[0], resid_model[0], resid_state[0]
    levels, rows, columns = rs.shape
    per_level = windows // levels
    width = columns // per_level
    blocks = bricks
    groups = levels * (columns // LANES) * 8
    halo_groups = groups + (columns // LANES) * 8
    field_bytes = 4 * levels * rows * columns
    here = lax.axis_index("space").astype(jnp.int32)
    window = lax.axis_index("tm").astype(jnp.int32)
    where = jnp.stack([window, jnp.int32(windows), here])
    at = here[None]

    upward = [(i, i + 1) for i in range(bricks - 1)]
    downward = [(i + 1, i) for i in range(bricks - 1)]

    packed = pl.pallas_call(
        functools.partial(pack_kernel, windows),
        out_shape=f32(windows, 3 * rows, width),
        in_specs=[VMEM] * 3,
        out_specs=VMEM,
        compiler_params=params(32),
        cost_estimate=cost(0, 6 * field_bytes),
        name="pack",
    )(rs, rm, mv)
    windows_of = lax.all_to_all(packed, "tm", 0, 0)

    rm_next = lax.ppermute(rm, "tm", [(i + 1, i) for i in range(windows - 1)])
    obs_all = jnp.concatenate([resid_obs, resid_obs / obs_var], axis=1)
    distance = 1
    while distance < bricks:
        other = lax.ppermute(obs_all, "space", [(i, i ^ distance) for i in range(bricks)])
        obs_all = jnp.concatenate([obs_all, other], axis=0)
        distance *= 2
    cup, cdown = pl.pallas_call(
        courant_edge_kernel,
        out_shape=(f32(16, columns), f32(16, columns)),
        in_specs=[VMEM] * 2,
        out_specs=(VMEM, VMEM),
        compiler_params=params(32),
        cost_estimate=cost(0, 3 * field_bytes),
        name="courant_edges",
    )(cx, cy)
    cbelow = lax.ppermute(cup, "space", upward)
    cabove = lax.ppermute(cdown, "space", downward)
    rank, code, passes = pl.pallas_call(
        functools.partial(place_kernel, columns),
        out_shape=(i32(blocks, BLOCK), i32(blocks, BLOCK), i32(1)),
        in_specs=[SMEM, VMEM, VMEM, VMEM],
        out_specs=(VMEM, VMEM, SMEM),
        scratch_shapes=[pltpu.VMEM((blocks, BLOCK), jnp.int32)] * 3,
        compiler_params=params(32),
        cost_estimate=cost(0, 2 * field_bytes),
        name="places",
    )(at, obs_brick, obs_cell, obs_step)
    together = min(4, blocks)
    spread_start, spread_middle, spread_edge = pl.pallas_call(
        spread_kernel,
        out_shape=(f32(levels, rows, columns), f32(levels, rows, columns), f32(8, columns)),
        in_specs=[SMEM, SMEM, VMEM, VMEM, VMEM],
        out_specs=(VMEM, VMEM, VMEM),
        scratch_shapes=[
            pltpu.VMEM((halo_groups, 2 * LANES), jnp.float32),
            pltpu.VMEM((halo_groups, together * SLOTS), jnp.bfloat16),
            pltpu.VMEM((together * SLOTS, 2 * LANES), jnp.bfloat16),
            pltpu.VMEM((together * SLOTS, 2 * LANES), jnp.bfloat16),
        ],
        compiler_params=params(40),
        cost_estimate=cost(4 * blocks * SLOTS * halo_groups * 2 * LANES, 3 * field_bytes),
        name="spread",
    )(at, passes, rank, code, obs_all)

    summed = pl.pallas_call(
        scan_kernel,
        out_shape=f32(windows, 2 * rows, width),
        in_specs=[VMEM],
        out_specs=VMEM,
        compiler_params=params(32),
        cost_estimate=cost(0, 5 * field_bytes),
        name="scan",
    )(windows_of)
    back = lax.all_to_all(summed, "tm", 0, 0)
    up, down = pl.pallas_call(
        functools.partial(edge_kernel, levels),
        out_shape=(f32(16, columns), f32(16, columns)),
        in_specs=[VMEM],
        out_specs=(VMEM, VMEM),
        compiler_params=params(32),
        cost_estimate=cost(0, 3 * field_bytes),
        name="edges",
    )(back)
    below = lax.ppermute(up, "space", upward)
    above = lax.ppermute(down, "space", downward)

    image_next, image_state, sent = pl.pallas_call(
        image_kernel,
        out_shape=(
            f32(levels, rows, columns), f32(levels, rows, columns), f32(blocks, BLOCK + LANES),
        ),
        in_specs=[SMEM, SMEM] + [VMEM] * 20,
        out_specs=(VMEM, VMEM, VMEM),
        scratch_shapes=[
            pltpu.VMEM((groups, 2 * LANES), jnp.float32),
            pltpu.VMEM((together * SLOTS, groups), jnp.bfloat16),
            pltpu.VMEM((blocks, BLOCK), jnp.float32),
        ],
        compiler_params=params(40),
        cost_estimate=cost(4 * blocks * SLOTS * groups * 2 * LANES, 14 * field_bytes),
        name="images",
    )(where, passes, back, up, down, below, above, cx, cy, cup, cdown, cbelow, cabove,
      spread_start, spread_middle, spread_edge, rs, rm, rm_next, rank, code, obs_all)

    image_model = lax.ppermute(image_next, "tm", [(i, i + 1) for i in range(windows - 1)])
    got = lax.all_to_all(sent, "space", 0, 0, tiled=True)
    observed, sums = pl.pallas_call(
        gather_kernel,
        out_shape=(f32(1, BLOCK), f32(windows, LANES)),
        in_specs=[VMEM],
        out_specs=(VMEM, VMEM),
        cost_estimate=cost(0, 200000),
        name="first_sums",
    )(got)
    all_sums = lax.all_to_all(sums, "tm", 0, 0, tiled=True)

    field = pl.BlockSpec((1, rows, columns), lambda l: (l, 0, 0))
    whole = lambda *shape: pl.BlockSpec(shape, lambda l: (0,) * len(shape))
    count = resid_obs.shape[1]
    new_ds, new_do, new_inc, new_rm, new_ro, new_rs = pl.pallas_call(
        update_kernel,
        grid=(levels,),
        out_shape=(
            f32(levels, rows, columns), f32(1, count), f32(levels, rows, columns),
            f32(levels, rows, columns), f32(1, count), f32(levels, rows, columns),
        ),
        in_specs=[
            SMEM, whole(windows, LANES), field, field, field, field,
            pl.BlockSpec((per_level, 2 * rows, width), lambda l: (l, 0, 0)), field, field,
            whole(1, count), whole(1, count), whole(1, count), whole(1, count),
        ],
        out_specs=(field, whole(1, count), field, field, whole(1, count), field),
        compiler_params=params(32),
        cost_estimate=cost(0, 12 * field_bytes),
        name="updates",
    )(where, all_sums, ds, inc, rm, rs, back, image_model, image_state,
      dual_obs, resid_obs, obs_var, observed)
    return new_ds[None], new_do, new_inc[None], new_rm[None], new_ro, new_rs[None]


def solution(mesh):
    field = P("tm", None, "space", None)
    obs = P("tm", "space")
    shared = P("tm", None)
    return jax.shard_map(
        functools.partial(body, mesh.shape["tm"], mesh.shape["space"]),
        mesh=mesh,
        in_specs=(
            field, field, field, obs, shared, shared, shared,
            field, obs, field, field, obs, field,
        ),
        out_specs=(field, obs, field, field, obs, field),
        check_vma=False,
    )
```

time: 478 us -> 129 us (0.27)
  waiting for transfers between devices: 202 us -> 17.2 us
  matrix products: 68.2 us -> 0 us
  blocking collectives: 93.8 us -> 26.9 us
  other arithmetic: 40.6 us -> 0.19 us
  Pallas kernels: 0 us -> 24 us
  between operations: 19.3 us -> 0.99 us
  starting transfers between devices: 26 us -> 44.3 us
  local copies, waits for them, and re-layouts: 26.5 us -> 14.5 us
    all_gather x2 -> x0, waiting for transfers between devices: 126 us -> none  [carried_in(): gathered = lax.all_gather(part, axis)]
    psum x1 -> x0, blocking collectives: 76.1 us -> none  [body(): lax.psum((local_projected, local_curvature), ('tm', 'space'))]
    unnamed x4 -> x0, waiting for transfers between devices: 74.1 us -> none
    dot_general x2 -> x0, matrix products: 68.2 us -> none  [the longest x1 38.7 us: body(): lax.dot_general(row_hot, placed, (((0,), (0,)), ((), ())), precision=lax....]
    all_to_all x0 -> x2, blocking collectives: none -> 26.9 us  [the longest x1 13.6 us: body(): got = lax.all_to_all(sent, 'space', 0, 0, tiled=True)]
    pallas_call x0 -> x9, Pallas kernels: none -> 24 us  [the longest x1 9.39 us: body(): pl.pallas_call(image_kernel, out_shape=(f32(levels, rows, columns), f32(l...]
    add x17 -> x0, other arithmetic: 18.4 us -> none  [the longest x15 16.2 us: add_fields(): return earlier + later]
    all_gather x1 -> x0, blocking collectives: 17.8 us -> none  [body(): all_duals = lax.all_gather(dual_obs_step, 'space', axis=1, tiled=True)[0]]
  transfers between devices with their start and end apart: 12 -> 12, of which waited for: 4 -> 3; matrix products, arithmetic and copies ran while one was open for 22% -> 2% of each run, Pallas kernels for 0% -> 9%
where the time goes in v1:
time: 129 us; the launch traced here: 128 us
  starting transfers between devices  44.3 us (34%)
  blocking collectives  26.9 us (21%)
  Pallas kernels  24 us (19%)
  waiting for transfers between devices  17.2 us (13%)
  local copies, waits for them, and re-layouts  14.5 us (11%)
    all_to_all x1, waiting for transfers between devices, body(): windows_of = lax.all_to_all(packed, 'tm', 0, 0)  15.7 us
    all_to_all x1, blocking collectives, body(): got = lax.all_to_all(sent, 'space', 0, 0, tiled=True)  13.6 us
    all_to_all x1, blocking collectives, body(): all_sums = lax.all_to_all(sums, 'tm', 0, 0, tiled=True)  13.3 us
    unnamed x65, local copies, waits for them, and re-layouts  12.8 us
    ppermute x4, starting transfers between devices, body(): lax.ppermute(obs_all, 'space', [(i, i ^ distance) for i in range(bricks)])  11.7 us
    pallas_call x1, Pallas kernels, body(): pl.pallas_call(image_kernel, out_shape=(f32(levels, rows, columns), f32(l...  9.39 us
    ppermute x1, starting transfers between devices, body(): cbelow = lax.ppermute(cup, 'space', upward)  8.15 us
    all_to_all x1, starting transfers between devices, body(): windows_of = lax.all_to_all(packed, 'tm', 0, 0)  7.72 us
  transfers between devices with their start and end apart: 12, of which 3 were waited for; matrix products, arithmetic and copies ran while one was open for 2% of the time, Pallas kernels for 9%

profile of v1, /device:TPU:1, one launch (start us, length us, event | category | flops | bytes accessed | tf_op | source)
XLA Modules:
  0.0 128.0 jit_solution(12613688291883938118)
XLA Ops:
  0.6 0.0 copy-start
  0.6 1.0 copy-done
  1.6 1.0 copy-done.2
  2.6 1.0 copy-done.4
  3.6 1.1 pack.1
  4.8 7.7 %all-to-all-start = ((f32[16,24,768]{2,1,0:T(8,128)}), f32[16,24,768]{2,1,0:T(8,128)S(1)}, u32[]{:S(2)}, u32[]{:S(2)}) async-start(f32[16,24,768]{2,1,0:T(8,128)} %pack.1), calls=%async_computation | async-start | bytes 2359296 | tf_op jit(solution)/shard_map/all_to_all | solution.py:451
  12.5 0.0 copy-start.31
  12.6 1.0 collective-permute-start.4
  13.6 15.7 %all-to-all-done.in_ref = f32[16,24,768]{2,1,0:T(8,128)S(1)} async-done(((f32[16,24,768]{2,1,0:T(8,128)}), f32[16,24,768]{2,1,0:T(8,128)S(1)}, u32[]{:S(2)}, u32[]{:S(2)}) %all-to-all-start) | async-done | bytes 1179680 | tf_op jit(solution)/shard_map/all_to_all | solution.py:451
  29.3 1.0 scan.1
  30.3 4.3 %all-to-all-start.1 = ((f32[16,16,768]{2,1,0:T(8,128)}), f32[16,16,768]{2,1,0:T(8,128)S(1)}, u32[]{:S(2)}, u32[]{:S(2)}) async-start(f32[16,16,768]{2,1,0:T(8,128)} %scan.1), calls=%async_computation.1 | async-start | bytes 1572864 | tf_op jit(solution)/shard_map/all_to_all | solution.py:507
  34.6 0.0 copy-start.12
  34.7 0.0 copy-start.13
  34.7 0.0 copy-start.14
  34.7 0.0 collective-permute-done.4
  34.7 1.7 %collective-permute-start.5 = (f32[2,2048]{1,0:T(2,128)S(1)}, f32[2,2048]{1,0:T(2,128)S(1)}, u32[]{:S(2)}, u32[]{:S(2)}) collective-permute-start(f32[2,2048]{1,0:T(2,128)S(1)} %pad_maximum_fusion.2), channel_id=1, source_target_pairs={{0,2},{1,3},{2,0},{3,1},{4,6},{5,7},{6,4},{7,5},{8,10},{9,11},{10,... | collective-permute-start | bytes 49160 | tf_op jit(solution)/shard_map/ppermute | solution.py:457
  36.5 1.1 collective-permute-done.5
  37.6 3.1 %collective-permute-start.6 = (f32[4,2048]{1,0:T(4,128)S(1)}, f32[4,2048]{1,0:T(4,128)S(1)}, u32[]{:S(2)}, u32[]{:S(2)}) collective-permute-start(f32[4,2048]{1,0:T(4,128)S(1)} %pad_maximum_fusion.1), channel_id=1, source_target_pairs={{0,4},{1,5},{2,6},{3,7},{4,0},{5,1},{6,2},{7,3},{8,12},{9,13},{10,... | collective-permute-start | bytes 98312 | tf_op jit(solution)/shard_map/ppermute | solution.py:457
  40.7 1.3 %collective-permute-start.8 = (f32[4,8,3072]{2,1,0:T(8,128)S(1)}, f32[4,8,3072]{2,1,0:T(8,128)S(1)}, u32[]{:S(2)}, u32[]{:S(2)}) collective-permute-start(f32[4,8,3072]{2,1,0:T(8,128)S(1)} %bitcast.25), channel_id=1, source_target_pairs={{16,0},{32,16},{48,32},{64,48},{80,64},{96,80},{112,96},{128,112},... | collective-permute-start | bytes 1179656 | tf_op jit(solution)/shard_map/ppermute | solution.py:453
  42.0 0.3 collective-permute-done.6
  42.3 5.9 %collective-permute-start.7 = (f32[8,2048]{1,0:T(8,128)S(1)}, f32[8,2048]{1,0:T(8,128)}, u32[]{:S(2)}, u32[]{:S(2)}) collective-permute-start(f32[8,2048]{1,0:T(8,128)S(1)} %pad_maximum_fusion), channel_id=1, source_target_pairs={{0,8},{1,9},{2,10},{3,11},{4,12},{5,13},{6,14},{7,15},{8,0},{9,1},... | collective-permute-start | bytes 196616 | tf_op jit(solution)/shard_map/ppermute | solution.py:457
  48.2 0.1 courant_edges.1
  48.3 0.0 copy-start.20
  48.3 0.0 copy-start.22
  48.3 8.2 %collective-permute-start.2 = (f32[16,3072]{1,0:T(8,128)S(1)}, f32[16,3072]{1,0:T(8,128)S(1)}, u32[]{:S(2)}, u32[]{:S(2)}) collective-permute-start(f32[16,3072]{1,0:T(8,128)S(1)} %get-tuple-element.30.cup_ref), channel_id=1, source_target_pairs={{0,1},{1,2},{2,3},{3,4},{4,5},{5,6},{6,7},{7,8},{8,9},{9,10},{10,1... | collective-permute-start | bytes 589832 | tf_op jit(solution)/shard_map/ppermute | solution.py:469
  56.5 1.9 %collective-permute-start.3 = (f32[16,3072]{1,0:T(8,128)S(1)}, f32[16,3072]{1,0:T(8,128)}, u32[]{:S(2)}, u32[]{:S(2)}) collective-permute-start(f32[16,3072]{1,0:T(8,128)S(1)} %get-tuple-element.31.cdown_ref), channel_id=1, source_target_pairs={{1,0},{2,1},{3,2},{4,3},{5,4},{6,5},{7,6},{8,7},{9,8},{10,9},{11,1... | collective-permute-start | bytes 589832 | tf_op jit(solution)/shard_map/ppermute | solution.py:470
  58.4 0.0 all-to-all-done.1.back_ref
  58.5 0.9 edges.1
  59.3 3.6 %collective-permute-start = (f32[16,3072]{1,0:T(8,128)}, f32[16,3072]{1,0:T(8,128)}, u32[]{:S(2)}, u32[]{:S(2)}) collective-permute-start(f32[16,3072]{1,0:T(8,128)} %get-tuple-element.28.up_ref), channel_id=1, source_target_pairs={{0,1},{1,2},{2,3},{3,4},{4,5},{5,6},{6,7},{7,8},{8,9},{9,10},{10,1... | collective-permute-start | bytes 589832 | tf_op jit(solution)/shard_map/ppermute | solution.py:517
  63.0 0.0 collective-permute-done.7
  63.0 1.9 %collective-permute-start.1 = (f32[16,3072]{1,0:T(8,128)}, f32[16,3072]{1,0:T(8,128)}, u32[]{:S(2)}, u32[]{:S(2)}) collective-permute-start(f32[16,3072]{1,0:T(8,128)} %get-tuple-element.29.down_ref), channel_id=1, source_target_pairs={{1,0},{2,1},{3,2},{4,3},{5,4},{6,5},{7,6},{8,7},{9,8},{10,9},{11,1... | collective-permute-start | bytes 589832 | tf_op jit(solution)/shard_map/ppermute | solution.py:518
  64.9 0.1 pad_add_fusion.where_ref
  65.0 1.3 %places.1 = (s32[16,1024]{1,0:T(8,128)S(1)}, s32[16,1024]{1,0:T(8,128)S(1)}, s32[1]{0:T(128)}) custom-call(s32[1]{0:T(128)} %bitcast.1.at_ref, s32[1,16384]{1,0:T(1,128)S(1)} %copy-done.12, s32[1,16384]{1,0:T(1,128)S(1)} %copy-done.13, s32[1,16384]{1,0:T(1,128)S(1)} %copy-done.14), custom_call_target="tpu_custom_call" | custom-call | bytes 786432 | tf_op jit(solution)/shard_map/places/pallas_call | solution.py:471
  66.3 0.0 copy-start.28
  66.4 0.6 copy-done.28
  67.0 1.6 %concatenate.22.duals_ref.obs_ref = f32[16,2048]{1,0:T(8,128)S(1)} concatenate(f32[1,2048]{1,0:T(1,128)} %copy-done.31, f32[1,2048]{1,0:T(1,128)S(1)} %collective-permute-done.4, f32[2,2048]{1,0:T(2,128)S(1)} %collective-permute-done.5, f32[4,2048]{1,0:T(4,128)S(1)} %collective-permute-done.6, f32[8,2048]{1,0:T(8,128)} %collective-permute-done.7), dimensions={0} | concatenate | bytes 262144 | tf_op jit(solution)/shard_map/concatenate | solution.py:458
  68.6 0.9 copy-done.29
  69.5 6.2 %spread.1 = (f32[4,8,3072]{2,1,0:T(8,128)S(1)}, f32[4,8,3072]{2,1,0:T(8,128)S(1)}, f32[8,3072]{1,0:T(8,128)S(1)}) custom-call(s32[1]{0:T(128)} %bitcast.1.at_ref, s32[1]{0:T(128)} %get-tuple-element.27.passes_ref, s32[16,1024]{1,0:T(8,128)S(1)} %get-tuple-element.32.rank_ref, s32[16,1024]{1,0:T(8,128)S(1)} %copy-done.29, ...), custom_call_target="tpu_custom_call" | custom-call | flops 2013265920 | bytes 1179648 | tf_op jit(solution)/shard_map/spread/pallas_call | solution.py:482
  75.7 0.0 collective-permute-done.2.cbelow_ref
  75.7 0.7 copy-done.24
  76.4 0.0 collective-permute-done.3.cabove_ref
  76.4 0.0 collective-permute-done.8.rm_next_ref
  76.4 0.7 copy-done.18
  77.1 0.0 collective-permute-done.below_ref
  77.2 0.0 collective-permute-done.1.above_ref
  77.2 0.0 copy-done.1
  77.2 0.9 copy-done.11
  78.1 1.0 copy-done.19
  79.1 0.9 copy-done.21
  80.0 0.9 copy-done.23
  80.9 0.9 copy-done.25
  81.9 0.8 copy-done.27
  82.7 9.4 %images.1 = (f32[4,8,3072]{2,1,0:T(8,128)}, f32[4,8,3072]{2,1,0:T(8,128)S(1)}, f32[16,1152]{1,0:T(8,128)S(1)}) custom-call(s32[3]{0:T(128)S(1)} %pad_add_fusion.where_ref, s32[1]{0:T(128)} %get-tuple-element.27.passes_ref, f32[16,16,768]{2,1,0:T(8,128)S(1)} %all-to-all-done.1.back_ref, f32[16,3072]{1,0:T(8,128)} %get-tuple-element.28.up_ref, ...), custom_call_target="tpu_custom_call" | custom-call | flops 1610612736 | bytes 5505024 | tf_op jit(solution)/shard_map/images/pallas_call | solution.py:520
  92.1 3.6 %collective-permute-start.9 = (f32[4,8,3072]{2,1,0:T(8,128)}, f32[4,8,3072]{2,1,0:T(8,128)S(1)}, u32[]{:S(2)}, u32[]{:S(2)}) collective-permute-start(f32[4,8,3072]{2,1,0:T(8,128)} %get-tuple-element.39), channel_id=1, source_target_pairs={{0,16},{16,32},{32,48},{48,64},{64,80},{80,96},{96,112},{112,128},... | collective-permute-start | bytes 1179656 | tf_op jit(solution)/shard_map/ppermute | solution.py:538
  95.7 0.1 copy.19
  95.7 13.6 %all_to_all.32 = f32[16,1,1152]{2,1,0:T(1,128)S(1)} all-to-all(f32[16,1,1152]{2,1,0:T(1,128)S(1)} %copy.19), channel_id=1, replica_groups=mesh['tm'=16,'space'=16] {'space'}, dimensions={0} | all-to-all | bytes 147456 | tf_op jit(solution)/shard_map/all_to_all | solution.py:539
  109.4 0.6 copy.23
  110.0 1.5 %first_sums.1 = (f32[1,1024]{1,0:T(1,128)}, f32[16,128]{1,0:T(8,128)}) custom-call(f32[16,1152]{1,0:T(8,128)} %bitcast.37), custom_call_target="tpu_custom_call" | custom-call | bytes 200000 | tf_op jit(solution)/shard_map/first_sums/pallas_call | solution.py:540
  111.5 13.3 %all_to_all.33 = f32[16,1,128]{2,1,0:T(1,128)S(1)} all-to-all(f32[16,1,128]{2,1,0:T(1,128)} %bitcast.38), channel_id=1, replica_groups=mesh['tm'=16,'space'=16] {'tm'}, dimensions={0} | all-to-all | bytes 16384 | tf_op jit(solution)/shard_map/all_to_all | solution.py:548
  124.8 0.0 collective-permute-done.9.image_ref
  124.8 0.0 copy-done.7
  124.8 0.0 copy-start.17
  124.8 0.7 copy-done.17
  125.5 2.5 %updates.1 = (f32[4,8,3072]{2,1,0:T(8,128)}, f32[1,1024]{1,0:T(1,128)}, f32[4,8,3072]{2,1,0:T(8,128)}, f32[4,8,3072]{2,1,0:T(8,128)}, f32[1,1024]{1,0:T(1,128)}, /*index=5*/f32[4,8,3072]{2,1,0:T(8,128)}) custom-call(s32[3]{0:T(128)S(1)} %pad_add_fusion.where_ref, f32[16,128]{1,0:T(8,128)S(1)} %bitcast.36, f32[4,8,3072]{2,1,0:T(8,128)S(1)} %bitcast.33, ...), custom_call_target="tpu_custom_call" | custom-call | bytes 4718592 | tf_op jit(solution)/shard_map/updates/pallas_call | solution.py:553
  (44 shorter events, 0.2 us)
Async XLA Ops:
  0.6 1.0 copy-start
  1.6 1.0 copy-start.2
  2.6 1.0 copy-start.4
  4.8 7.7 %copy-start.9 = (f32[1,1024]{1,0:T(1,128)S(1)}, f32[1,1024]{1,0:T(1,128)}, u32[]{:S(2)}) copy-start(f32[1,1024]{1,0:T(1,128)} %ro_ref.1) | copy-start | bytes 12292
  4.8 7.7 %copy-start.15 = (f32[1,1024]{1,0:T(1,128)S(1)}, f32[1,1024]{1,0:T(1,128)}, u32[]{:S(2)}) copy-start(f32[1,1024]{1,0:T(1,128)} %ov_ref.1) | copy-start | bytes 12292
  4.8 24.5 %all-to-all-start = ((f32[16,24,768]{2,1,0:T(8,128)}), f32[16,24,768]{2,1,0:T(8,128)S(1)}, u32[]{:S(2)}, u32[]{:S(2)}) async-start(f32[16,24,768]{2,1,0:T(8,128)} %pack.1), calls=%async_computation | async-start | bytes 2359296 | tf_op jit(solution)/shard_map/all_to_all | solution.py:451
  12.5 22.2 %copy-start.31 = (f32[1,2048]{1,0:T(1,128)}, f32[1,2048]{1,0:T(1,128)S(1)}, u32[]{:S(2)}) copy-start(f32[1,2048]{1,0:T(1,128)S(1)} %pad_maximum_fusion.3) | copy-start | bytes 24580
  12.6 22.1 %collective-permute-start.4 = (f32[1,2048]{1,0:T(1,128)S(1)}, f32[1,2048]{1,0:T(1,128)S(1)}, u32[]{:S(2)}, u32[]{:S(2)}) collective-permute-start(f32[1,2048]{1,0:T(1,128)S(1)} %pad_maximum_fusion.3), channel_id=1, source_target_pairs={{0,1},{1,0},{2,3},{3,2},{4,5},{5,4},{6,7},{7,6},{8,9},{9,8},{10,11... | collective-permute-start | bytes 24584 | tf_op jit(solution)/shard_map/ppermute | solution.py:457
  30.3 10.4 %copy-start.3 = (f32[1,4,8,3072]{3,2,1,0:T(8,128)S(1)}, f32[1,4,8,3072]{3,2,1,0:T(8,128)}, u32[]{:S(2)}) copy-start(f32[1,4,8,3072]{3,2,1,0:T(8,128)} %param.23) | copy-start | bytes 1179652
  30.3 17.9 %copy-start.5 = (f32[1,4,8,3072]{3,2,1,0:T(8,128)S(1)}, f32[1,4,8,3072]{3,2,1,0:T(8,128)}, u32[]{:S(2)}) copy-start(f32[1,4,8,3072]{3,2,1,0:T(8,128)} %param.13) | copy-start | bytes 1179652
  30.3 17.9 %copy-start.6 = (f32[1,4,8,3072]{3,2,1,0:T(8,128)S(1)}, f32[1,4,8,3072]{3,2,1,0:T(8,128)}, u32[]{:S(2)}) copy-start(f32[1,4,8,3072]{3,2,1,0:T(8,128)} %param.14) | copy-start | bytes 1179652
  30.3 28.1 %all-to-all-start.1 = ((f32[16,16,768]{2,1,0:T(8,128)}), f32[16,16,768]{2,1,0:T(8,128)S(1)}, u32[]{:S(2)}, u32[]{:S(2)}) async-start(f32[16,16,768]{2,1,0:T(8,128)} %scan.1), calls=%async_computation.1 | async-start | bytes 1572864 | tf_op jit(solution)/shard_map/all_to_all | solution.py:507
  34.6 30.3 %copy-start.12 = (s32[1,16384]{1,0:T(1,128)S(1)}, s32[1,16384]{1,0:T(1,128)}, u32[]{:S(2)}) copy-start(s32[1,16384]{1,0:T(1,128)} %brick_ref.1) | copy-start | bytes 196612
  34.7 30.3 %copy-start.13 = (s32[1,16384]{1,0:T(1,128)S(1)}, s32[1,16384]{1,0:T(1,128)}, u32[]{:S(2)}) copy-start(s32[1,16384]{1,0:T(1,128)} %cell_ref.1) | copy-start | bytes 196612
  34.7 30.3 %copy-start.14 = (s32[1,16384]{1,0:T(1,128)S(1)}, s32[1,16384]{1,0:T(1,128)}, u32[]{:S(2)}) copy-start(s32[1,16384]{1,0:T(1,128)} %step_ref.1) | copy-start | bytes 196612
  34.7 2.9 %collective-permute-start.5 = (f32[2,2048]{1,0:T(2,128)S(1)}, f32[2,2048]{1,0:T(2,128)S(1)}, u32[]{:S(2)}, u32[]{:S(2)}) collective-permute-start(f32[2,2048]{1,0:T(2,128)S(1)} %pad_maximum_fusion.2), channel_id=1, source_target_pairs={{0,2},{1,3},{2,0},{3,1},{4,6},{5,7},{6,4},{7,5},{8,10},{9,11},{10,... | collective-permute-start | bytes 49160 | tf_op jit(solution)/shard_map/ppermute | solution.py:457
  37.6 4.7 %collective-permute-start.6 = (f32[4,2048]{1,0:T(4,128)S(1)}, f32[4,2048]{1,0:T(4,128)S(1)}, u32[]{:S(2)}, u32[]{:S(2)}) collective-permute-start(f32[4,2048]{1,0:T(4,128)S(1)} %pad_maximum_fusion.1), channel_id=1, source_target_pairs={{0,4},{1,5},{2,6},{3,7},{4,0},{5,1},{6,2},{7,3},{8,12},{9,13},{10,... | collective-permute-start | bytes 98312 | tf_op jit(solution)/shard_map/ppermute | solution.py:457
  40.7 35.7 %collective-permute-start.8 = (f32[4,8,3072]{2,1,0:T(8,128)S(1)}, f32[4,8,3072]{2,1,0:T(8,128)S(1)}, u32[]{:S(2)}, u32[]{:S(2)}) collective-permute-start(f32[4,8,3072]{2,1,0:T(8,128)S(1)} %bitcast.25), channel_id=1, source_target_pairs={{16,0},{32,16},{48,32},{64,48},{80,64},{96,80},{112,96},{128,112},... | collective-permute-start | bytes 1179656 | tf_op jit(solution)/shard_map/ppermute | solution.py:453
  42.3 20.6 %collective-permute-start.7 = (f32[8,2048]{1,0:T(8,128)S(1)}, f32[8,2048]{1,0:T(8,128)}, u32[]{:S(2)}, u32[]{:S(2)}) collective-permute-start(f32[8,2048]{1,0:T(8,128)S(1)} %pad_maximum_fusion), channel_id=1, source_target_pairs={{0,8},{1,9},{2,10},{3,11},{4,12},{5,13},{6,14},{7,15},{8,0},{9,1},... | collective-permute-start | bytes 196616 | tf_op jit(solution)/shard_map/ppermute | solution.py:457
  48.3 27.3 %copy-start.20 = (f32[16,3072]{1,0:T(8,128)}, f32[16,3072]{1,0:T(8,128)S(1)}, u32[]{:S(2)}) copy-start(f32[16,3072]{1,0:T(8,128)S(1)} %get-tuple-element.30.cup_ref) | copy-start | bytes 589828
  48.3 27.3 %copy-start.22 = (f32[16,3072]{1,0:T(8,128)}, f32[16,3072]{1,0:T(8,128)S(1)}, u32[]{:S(2)}) copy-start(f32[16,3072]{1,0:T(8,128)S(1)} %get-tuple-element.31.cdown_ref) | copy-start | bytes 589828
  48.3 27.4 %collective-permute-start.2 = (f32[16,3072]{1,0:T(8,128)S(1)}, f32[16,3072]{1,0:T(8,128)S(1)}, u32[]{:S(2)}, u32[]{:S(2)}) collective-permute-start(f32[16,3072]{1,0:T(8,128)S(1)} %get-tuple-element.30.cup_ref), channel_id=1, source_target_pairs={{0,1},{1,2},{2,3},{3,4},{4,5},{5,6},{6,7},{7,8},{8,9},{9,10},{10,1... | collective-permute-start | bytes 589832 | tf_op jit(solution)/shard_map/ppermute | solution.py:469
  56.5 19.9 %collective-permute-start.3 = (f32[16,3072]{1,0:T(8,128)S(1)}, f32[16,3072]{1,0:T(8,128)}, u32[]{:S(2)}, u32[]{:S(2)}) collective-permute-start(f32[16,3072]{1,0:T(8,128)S(1)} %get-tuple-element.31.cdown_ref), channel_id=1, source_target_pairs={{1,0},{2,1},{3,2},{4,3},{5,4},{6,5},{7,6},{8,7},{9,8},{10,9},{11,1... | collective-permute-start | bytes 589832 | tf_op jit(solution)/shard_map/ppermute | solution.py:470
  59.3 17.8 %collective-permute-start = (f32[16,3072]{1,0:T(8,128)}, f32[16,3072]{1,0:T(8,128)}, u32[]{:S(2)}, u32[]{:S(2)}) collective-permute-start(f32[16,3072]{1,0:T(8,128)} %get-tuple-element.28.up_ref), channel_id=1, source_target_pairs={{0,1},{1,2},{2,3},{3,4},{4,5},{5,6},{6,7},{7,8},{8,9},{9,10},{10,1... | collective-permute-start | bytes 589832 | tf_op jit(solution)/shard_map/ppermute | solution.py:517
  63.0 14.2 %collective-permute-start.1 = (f32[16,3072]{1,0:T(8,128)}, f32[16,3072]{1,0:T(8,128)}, u32[]{:S(2)}, u32[]{:S(2)}) collective-permute-start(f32[16,3072]{1,0:T(8,128)} %get-tuple-element.29.down_ref), channel_id=1, source_target_pairs={{1,0},{2,1},{3,2},{4,3},{5,4},{6,5},{7,6},{8,7},{9,8},{10,9},{11,1... | collective-permute-start | bytes 589832 | tf_op jit(solution)/shard_map/ppermute | solution.py:518
  66.3 0.6 copy-start.28
  67.0 8.7 %copy-start.26 = (s32[16,1024]{1,0:T(8,128)}, s32[16,1024]{1,0:T(8,128)S(1)}, u32[]{:S(2)}) copy-start(s32[16,1024]{1,0:T(8,128)S(1)} %get-tuple-element.32.rank_ref) | copy-start | bytes 196612
  68.6 7.1 %copy-start.10 = (f32[16,2048]{1,0:T(8,128)}, f32[16,2048]{1,0:T(8,128)S(1)}, u32[]{:S(2)}) copy-start(f32[16,2048]{1,0:T(8,128)S(1)} %concatenate.22.duals_ref.obs_ref) | copy-start | bytes 393220
  68.6 0.9 copy-start.29
  69.5 7.7 %copy-start.1 = (f32[1,4,8,3072]{3,2,1,0:T(8,128)S(1)}, f32[1,4,8,3072]{3,2,1,0:T(8,128)}, u32[]{:S(2)}) copy-start(f32[1,4,8,3072]{3,2,1,0:T(8,128)} %param.25) | copy-start | bytes 1179652
  69.5 7.7 %copy-start.30 = (s32[16,1024]{1,0:T(8,128)S(1)}, s32[16,1024]{1,0:T(8,128)}, u32[]{:S(2)}) copy-start(s32[16,1024]{1,0:T(8,128)} %copy-done.28) | copy-start | bytes 196612
  75.7 0.7 copy-start.24
  76.4 0.7 copy-start.18
  77.2 0.9 copy-start.11
  78.1 1.0 copy-start.19
  79.1 0.9 copy-start.21
  80.0 0.9 copy-start.23
  80.9 0.9 copy-start.25
  81.9 0.8 copy-start.27
  82.7 42.1 %copy-start.7 = (f32[1,4,8,3072]{3,2,1,0:T(8,128)S(1)}, f32[1,4,8,3072]{3,2,1,0:T(8,128)}, u32[]{:S(2)}) copy-start(f32[1,4,8,3072]{3,2,1,0:T(8,128)} %param.20) | copy-start | bytes 1179652
  82.7 42.1 %copy-start.8 = (f32[1,4,8,3072]{3,2,1,0:T(8,128)S(1)}, f32[1,4,8,3072]{3,2,1,0:T(8,128)}, u32[]{:S(2)}) copy-start(f32[1,4,8,3072]{3,2,1,0:T(8,128)} %param.22) | copy-start | bytes 1179652
  82.7 42.1 %copy-start.16 = (f32[1,1024]{1,0:T(1,128)S(1)}, f32[1,1024]{1,0:T(1,128)}, u32[]{:S(2)}) copy-start(f32[1,1024]{1,0:T(1,128)} %do_ref.1) | copy-start | bytes 12292
  92.1 32.7 %collective-permute-start.9 = (f32[4,8,3072]{2,1,0:T(8,128)}, f32[4,8,3072]{2,1,0:T(8,128)S(1)}, u32[]{:S(2)}, u32[]{:S(2)}) collective-permute-start(f32[4,8,3072]{2,1,0:T(8,128)} %get-tuple-element.39), channel_id=1, source_target_pairs={{0,16},{16,32},{32,48},{48,64},{64,80},{80,96},{96,112},{112,128},... | collective-permute-start | bytes 1179656 | tf_op jit(solution)/shard_map/ppermute | solution.py:538
  124.8 0.7 copy-start.17

commit v2 on v1

v2 whole, which is shorter than its diff:
```python
import functools

import jax
import jax.numpy as jnp
from jax import lax
from jax.experimental import pallas as pl
from jax.experimental.pallas import tpu as pltpu
from jax.sharding import PartitionSpec as P

LANES = 128
SLOTS = 64
BLOCK = 512
CHUNK = 1024
MIB = 1024 * 1024


def params(mib):
    return pltpu.CompilerParams(vmem_limit_bytes=mib * MIB)


def cost(flops, touched):
    return pl.CostEstimate(flops=flops, bytes_accessed=touched, transcendentals=0)


VMEM = pl.BlockSpec(memory_space=pltpu.VMEM)
SMEM = pl.BlockSpec(memory_space=pltpu.SMEM)
ANY = pl.BlockSpec(memory_space=pl.ANY)
HBM = pl.BlockSpec(memory_space=pltpu.HBM)


def f32(*shape):
    return jax.ShapeDtypeStruct(shape, jnp.float32)


def i32(*shape):
    return jax.ShapeDtypeStruct(shape, jnp.int32)


def b16(*shape):
    return jax.ShapeDtypeStruct(shape, jnp.bfloat16)


def pack_kernel(parts, rs_ref, rm_ref, mv_ref, out_ref):
    levels, rows, columns = rs_ref.shape
    per_level = parts // levels
    width = columns // per_level
    for part in range(parts):
        level, piece = part // per_level, part % per_level
        cols = slice(piece * width, (piece + 1) * width)
        for place, ref in enumerate((rs_ref, rm_ref, mv_ref)):
            out_ref[part, rows * place : rows * (place + 1), :] = ref[level, :, cols]


def scan_kernel(in_ref, *rest):
    out_ref = rest[-1]
    steps = in_ref.shape[0]
    rows = in_ref.shape[1] // 3
    later = jnp.zeros((rows, in_ref.shape[2]), jnp.float32)
    for t in reversed(range(steps)):
        out_ref[t, rows : 2 * rows, :] = later
        later = later + in_ref[t, 0:rows, :]
        out_ref[t, 0:rows, :] = (
            in_ref[t, rows : 2 * rows, :] - in_ref[t, 2 * rows : 3 * rows, :] * later
        )
    total = jnp.zeros((rows, in_ref.shape[2]), jnp.float32)
    for t in range(steps):
        total = total + out_ref[t, 0:rows, :]
        out_ref[t, 0:rows, :] = total


def edge_kernel(levels, back_ref, rows_ref, up_ref, down_ref, rows_s):
    parts, both, width = back_ref.shape
    rows = both // 2
    per_level = parts // levels
    for part in range(parts):
        level, piece = part // per_level, part % per_level
        cols = slice(piece * width, (piece + 1) * width)
        for place, row in enumerate((rows - 1, 0, rows - 2, 1)):
            for field in range(2):
                at = 16 * field + 4 * place + level
                row_at = rows * field + row
                rows_s[at : at + 1, cols] = back_ref[part, row_at : row_at + 1, :]
    incr, incr_in, dual, dual_in = (rows_s[8 * i : 8 * i + 8, :] for i in range(4))
    cx, cy, cy_in, middle = (rows_ref[8 * i : 8 * i + 8, :] for i in range(4))
    own, west, east, south, north = weights_of(cx, cy)
    is_up = lax.broadcasted_iota(jnp.int32, cx.shape, 0) < 4
    inner, outer = jnp.where(is_up, south, north), jnp.where(is_up, north, south)
    one = own * incr + west * west_of(incr) + east * east_of(incr) + inner * incr_in
    from_in = jnp.maximum(jnp.where(is_up, -cy_in, cy_in), 0.0) * dual_in
    kept = middle - (own * dual + east_of(west * dual) + west_of(east * dual) + from_in)
    for place, value in enumerate((incr, one, outer, outer * kept, outer * dual)):
        up_ref[4 * place : 4 * place + 4, :] = value[0:4]
        down_ref[4 * place : 4 * place + 4, :] = value[4:8]


def slots_held(rank_ref, k, half, first):
    slot = lax.broadcasted_iota(jnp.int32, (SLOTS, BLOCK), 0) + first
    row = rank_ref[pl.ds(k, 1), half * BLOCK : (half + 1) * BLOCK]
    return jnp.broadcast_to(row, (SLOTS, BLOCK)) == slot


def build_slots(rank_ref, code_ref, first, hot_ref, cols_ref, finish=None):
    groups = hot_ref.shape[1]
    group_id = lax.broadcasted_iota(jnp.int32, (SLOTS, groups), 1)

    def one_chunk(k, carry):
        for half in range(CHUNK // BLOCK):
            held = slots_held(rank_ref, k, half, first)
            row = code_ref[pl.ds(k, 1), half * BLOCK : (half + 1) * BLOCK]
            code = jnp.max(
                jnp.where(held, jnp.broadcast_to(row, (SLOTS, BLOCK)), -1), axis=1, keepdims=True
            )
            at = pl.ds(pl.multiple_of(k * (CHUNK // BLOCK * SLOTS) + half * SLOTS, SLOTS), SLOTS)
            hot_ref[at, :] = (
                (group_id == jnp.broadcast_to(code >> 8, (SLOTS, groups)))
                .astype(jnp.float32).astype(jnp.bfloat16)
            )
            cols_ref[at, :] = jnp.broadcast_to(code & 255, (SLOTS, LANES))
        if finish is not None:
            finish(k)
        return carry

    lax.fori_loop(0, rank_ref.shape[0], one_chunk, 0)


def place_kernel(columns, at_ref, brick_ref, cell_ref, step_ref,
                 rank_ref, code_ref, hot_ref, cols_ref, passes_ref,
                 brick_s, cell_s, step_s, hot_s, cols_s, sems):
    chunks = rank_ref.shape[0]
    here = at_ref[0]
    lane_groups = columns // LANES
    for k in range(chunks):
        cols = slice(k * CHUNK, (k + 1) * CHUNK)
        brick_s[k : k + 1, :] = brick_ref[0:1, cols]
        cell_s[k : k + 1, :] = cell_ref[0:1, cols]
        step_s[k : k + 1, :] = step_ref[0:1, cols]
    brick, cell, step = brick_s[...], cell_s[...], step_s[...]
    line = ((cell >> 10) * 171) >> 9
    level, row = line >> 3, line & 7
    column = cell - line * columns
    group, lane = column >> 7, column & 127
    code_ref[...] = ((level * lane_groups + group) * 8 + row) * 256 + step * LANES + lane
    inside = brick == here
    count = inside.astype(jnp.int32)
    lanes = lax.broadcasted_iota(jnp.int32, count.shape, 1) & (BLOCK - 1)
    shift = 1
    while shift < BLOCK:
        count = count + jnp.where(lanes >= shift, pltpu.roll(count, shift, 1), 0)
        shift *= 2
    rank_ref[...] = jnp.where(inside, count - 1, -1)
    passes_ref[0] = (jnp.max(count) + SLOTS - 1) // SLOTS
    per_chunk = CHUNK // BLOCK * SLOTS

    def copies(k):
        at = pl.ds(pl.multiple_of(k * per_chunk, per_chunk), per_chunk)
        return (
            pltpu.make_async_copy(hot_s.at[at, :], hot_ref.at[at, :], sems.at[k, 0]),
            pltpu.make_async_copy(cols_s.at[at, :], cols_ref.at[at, :], sems.at[k, 1]),
        )

    def finish(k):
        for copy in copies(k):
            copy.start()

    build_slots(rank_ref, code_ref, 0, hot_s, cols_s, finish)
    for k in range(chunks):
        for copy in copies(k):
            copy.wait()


def in_column(cols, values, which):
    lane = lax.broadcasted_iota(jnp.int32, cols.shape, 1) + which * LANES
    return jnp.where(cols == lane, values, 0.0)


def split_two(x):
    high = x.astype(jnp.bfloat16)
    low = (x - high.astype(jnp.float32)).astype(jnp.bfloat16)
    return high, low


def spread_kernel(at_ref, passes_ref, rank_ref, code_ref, hot_hbm, cols_hbm, near_ref, far_ref, cx_ref, cy_ref,
                  start_ref, middle_ref, rows_ref, resid_ref,
                  total, hot_ref, cols_ref, again_hot, again_cols, high_s, low_s, duals_s, sems):
    chunks = rank_ref.shape[0]
    here = at_ref[0]
    levels, rows, columns = start_ref.shape
    lane_groups = columns // LANES
    cols_copy = pltpu.make_async_copy(cols_hbm, cols_ref, sems.at[0])
    hot_copy = pltpu.make_async_copy(hot_hbm, hot_ref, sems.at[1])
    cols_copy.start()
    hot_copy.start()
    for i in range(chunks):
        half = chunks // 2
        row = near_ref[i : i + 1, :] if i < half else far_ref[i - half : i - half + 1, :]
        at = pl.ds(lax.bitwise_xor(jnp.int32(i), here), 1)
        resid_ref[at, :] = row[:, 0:CHUNK]
        duals_s[at, :] = row[:, CHUNK : 2 * CHUNK]
    for level in range(levels):
        for place, row in enumerate((rows - 1, 0)):
            at = 4 * place + level
            rows_ref[at : at + 1, :] = cx_ref[level, row : row + 1, :]
            rows_ref[8 + at : 9 + at, :] = cy_ref[level, row : row + 1, :]
            inner = row - 1 if place == 0 else row + 1
            rows_ref[16 + at : 17 + at, :] = cy_ref[level, inner : inner + 1, :]
    cols_copy.wait()

    def add_up(first, hot, cols_ref, ready):
        def one_chunk(k, carry):
            for half in range(CHUNK // BLOCK):
                held = slots_held(rank_ref, k, half, first)
                row = duals_s[pl.ds(k, 1), half * BLOCK : (half + 1) * BLOCK]
                dual = jnp.sum(
                    jnp.where(held, jnp.broadcast_to(row, (SLOTS, BLOCK)), 0.0),
                    axis=1, keepdims=True,
                )
                at = pl.ds(pl.multiple_of(k * (CHUNK // BLOCK * SLOTS) + half * SLOTS, SLOTS), SLOTS)
                wide = jnp.broadcast_to(dual, (SLOTS, LANES))
                for which in range(2):
                    high, low = split_two(in_column(cols_ref[at, :], wide, which))
                    high_s[at, which * LANES : (which + 1) * LANES] = high
                    low_s[at, which * LANES : (which + 1) * LANES] = low
            return carry

        lax.fori_loop(0, chunks, one_chunk, 0)
        if ready is not None:
            ready.wait()
        over_slots = (((0,), (0,)), ((), ()))
        both = lax.dot_general(
            high_s[...], hot[...], over_slots, preferred_element_type=jnp.float32
        ) + lax.dot_general(
            low_s[...], hot[...], over_slots, preferred_element_type=jnp.float32
        )
        return both.T

    total[...] = add_up(0, hot_ref, cols_ref, hot_copy)

    def one_more(number, carry):
        build_slots(rank_ref, code_ref, number * SLOTS, again_hot, again_cols)
        total[...] += add_up(number * SLOTS, again_hot, again_cols, None)
        return carry

    lax.fori_loop(1, passes_ref[0], one_more, 0)
    for level in range(levels):
        for g in range(lane_groups):
            at = (level * lane_groups + g) * 8
            cols = slice(g * LANES, (g + 1) * LANES)
            start_ref[level, :, cols] = total[at : at + 8, 0:LANES]
            middle_ref[level, :, cols] = total[at : at + 8, LANES : 2 * LANES]
    for level in range(levels):
        for place, row in enumerate((rows - 1, 0)):
            at = 24 + 4 * place + level
            rows_ref[at : at + 1, :] = middle_ref[level, row : row + 1, :]


def west_of(v):
    return pltpu.roll(v, 1, 1)


def east_of(v):
    return pltpu.roll(v, v.shape[1] - 1, 1)


def weights_of(cx, cy):
    west, east = jnp.maximum(cx, 0.0), jnp.maximum(-cx, 0.0)
    south, north = jnp.maximum(cy, 0.0), jnp.maximum(-cy, 0.0)
    return 1.0 - jnp.abs(cx) - jnp.abs(cy), west, east, south, north


def forward(v, below, above, coeffs):
    own, west, east, south, north = coeffs
    return own * v + west * west_of(v) + east * east_of(v) + south * below + north * above


def adjoint(v, from_above, from_below, coeffs):
    own, west, east, _, _ = coeffs
    return own * v + east_of(west * v) + west_of(east * v) + from_above + from_below


def row_below(v, edge, first):
    return jnp.where(first, jnp.broadcast_to(edge, v.shape), pltpu.roll(v, 1, 0))


def row_above(v, edge, last):
    return jnp.where(last, jnp.broadcast_to(edge, v.shape), pltpu.roll(v, v.shape[0] - 1, 0))


def image_kernel(where_ref, passes_ref, back_hbm, below_hbm, above_hbm, cx_hbm, cy_hbm,
                 start_hbm, middle_hbm, rs_hbm, rm_hbm, rm_next_hbm, hot_hbm, cols_hbm,
                 rank_ref, code_ref, resid_ref, next_ref, state_ref, sent_ref,
                 back_ref, below_ref, above_ref, cx_ref, cy_ref, start_ref, middle_ref, rs_ref, rm_ref, rm_next_ref,
                 hot_ref, cols_ref, fields, again_hot, again_cols, found, sems, hot_sems):
    levels, rows, columns = cx_ref.shape
    parts, _, width = back_ref.shape
    per_level = parts // levels
    chunks = rank_ref.shape[0]
    lane_groups = columns // LANES
    window, windows = where_ref[0], where_ref[1]

    edges = [
        pltpu.make_async_copy(below_hbm, below_ref, hot_sems.at[0]),
        pltpu.make_async_copy(above_hbm, above_ref, hot_sems.at[1]),
    ]
    loads = []
    for level in range(levels):
        pieces = pl.ds(level * per_level, per_level)
        pairs = [(back_hbm.at[pieces], back_ref.at[pieces])] + [
            (a.at[level], b.at[level])
            for a, b in (
                (cx_hbm, cx_ref), (cy_hbm, cy_ref), (rm_next_hbm, rm_next_ref), (start_hbm, start_ref),
                (middle_hbm, middle_ref), (rs_hbm, rs_ref), (rm_hbm, rm_ref),
            )
        ]
        loads.append([
            pltpu.make_async_copy(a, b, sems.at[level, i]) for i, (a, b) in enumerate(pairs)
        ])
    look = [
        pltpu.make_async_copy(hot_hbm, hot_ref, hot_sems.at[2]),
        pltpu.make_async_copy(cols_hbm, cols_ref, hot_sems.at[3]),
    ]
    for copy in loads[0] + edges + loads[1] + loads[2] + loads[3] + look:
        copy.start()
    for copy in edges:
        copy.wait()

    row_id = lax.broadcasted_iota(jnp.int32, (rows, columns), 0)
    first, last = row_id == 0, row_id == rows - 1
    projected = jnp.zeros((rows, columns), jnp.float32)
    curvature = jnp.zeros((rows, columns), jnp.float32)
    has_next = jnp.where(window < windows - 1, 1.0, 0.0)
    is_first = jnp.where(window == 0, 1.0, 0.0)
    for level in range(levels):
        for copy in loads[level]:
            copy.wait()
        pieces = range(level * per_level, (level + 1) * per_level)
        incr = jnp.concatenate([back_ref[p, 0:rows, :] for p in pieces], axis=1)
        next_dual = jnp.concatenate([back_ref[p, rows : 2 * rows, :] for p in pieces], axis=1)
        coeffs = weights_of(cx_ref[level], cy_ref[level])
        south, north = coeffs[3], coeffs[4]
        low, high = (
            [ref[4 * i + level : 4 * i + level + 1, :] for i in range(5)] for ref in (below_ref, above_ref)
        )
        after_one = forward(
            incr,
            row_below(incr, low[0], first),
            row_above(incr, high[0], last),
            coeffs,
        )
        after_two = forward(
            after_one,
            row_below(after_one, low[1] + low[2] * incr[0:1], first),
            row_above(after_one, high[1] + high[2] * incr[rows - 1 :], last),
            coeffs,
        )
        rm_next = rm_next_ref[level]
        image_next = (rm_next + incr - after_two) * has_next
        next_ref[level] = image_next
        south_dual, north_dual = south * next_dual, north * next_dual
        back_one = adjoint(
            next_dual,
            row_above(south_dual, high[4], last),
            row_below(north_dual, low[4], first),
            coeffs,
        )
        kept = middle_ref[level] - back_one
        rs, rm = rs_ref[level], rm_ref[level]
        image_state = (next_dual + rs) + start_ref[level] + adjoint(
            kept,
            row_above(south * kept, high[3] - high[2] * north_dual[rows - 1 :], last),
            row_below(north * kept, low[3] - low[2] * south_dual[0:1], first),
            coeffs,
        )
        state_ref[level] = image_state
        at_first = is_first * rm * rm
        projected += rm_next * image_next + rs * image_state + at_first
        curvature += image_next * image_next + image_state * image_state + at_first
        for g in range(lane_groups):
            at = (level * lane_groups + g) * 8
            cols = slice(g * LANES, (g + 1) * LANES)
            fields[at : at + 8, 0:LANES] = incr[:, cols]
            fields[at : at + 8, LANES : 2 * LANES] = after_one[:, cols]

    high_fields, low_fields = split_two(fields[...])
    groups = levels * lane_groups * 8
    per_chunk = CHUNK // BLOCK * SLOTS

    def look_up(first, hot, cols_ref, fresh):
        def some_chunks(q, carry):
            rows_at = pl.ds(pl.multiple_of(q * 4 * per_chunk, 4 * per_chunk), 4 * per_chunk)
            picks = hot[rows_at, :]
            picked = jnp.dot(
                picks, high_fields, preferred_element_type=jnp.float32
            ) + jnp.dot(picks, low_fields, preferred_element_type=jnp.float32)
            cols = cols_ref[rows_at, :]
            value = jnp.sum(
                in_column(cols, picked[:, 0:LANES], 0)
                + in_column(cols, picked[:, LANES : 2 * LANES], 1),
                axis=1, keepdims=True,
            )
            for j in range(4):
                k = q * 4 + j
                for half in range(CHUNK // BLOCK):
                    at = j * per_chunk + half * SLOTS
                    held = slots_held(rank_ref, k, half, first)
                    line = jnp.sum(
                        jnp.where(
                            held, jnp.broadcast_to(value[at : at + SLOTS], (SLOTS, BLOCK)), 0.0
                        ),
                        axis=0, keepdims=True,
                    )
                    lanes = slice(half * BLOCK, (half + 1) * BLOCK)
                    if fresh:
                        found[pl.ds(k, 1), lanes] = line
                    else:
                        found[pl.ds(k, 1), lanes] += line
            return carry

        lax.fori_loop(0, chunks // 4, some_chunks, 0)

    for copy in look:
        copy.wait()
    look_up(0, hot_ref, cols_ref, True)

    def one_more(number, carry):
        build_slots(rank_ref, code_ref, number * SLOTS, again_hot, again_cols)
        look_up(number * SLOTS, again_hot, again_cols, False)
        return carry

    lax.fori_loop(1, passes_ref[0], one_more, 0)

    observed = found[...]
    resid = resid_ref[...]
    image_obs = jnp.where(rank_ref[...] >= 0, resid + observed, 0.0)
    all_projected = jnp.sum(projected) + jnp.sum(resid * image_obs)
    all_curvature = jnp.sum(curvature) + jnp.sum(image_obs * image_obs)
    lane = lax.broadcasted_iota(jnp.int32, (1, LANES), 1)
    sums = jnp.where(lane == 0, all_projected, jnp.where(lane == 1, all_curvature, 0.0))
    for k in range(chunks):
        sent_ref[k, :, 0:CHUNK] = found[k : k + 1, :]
        sent_ref[k, :, CHUNK : CHUNK + LANES] = sums


def gather_kernel(got_ref, observed_ref, sums_ref):
    total = got_ref[0]
    for k in range(1, got_ref.shape[0]):
        total = total + got_ref[k]
    observed_ref[...] = total[:, 0:CHUNK]
    for k in range(sums_ref.shape[0]):
        sums_ref[k] = total[:, CHUNK : CHUNK + LANES]


def update_kernel(where_ref, sums_ref, ds_ref, inc_ref, rm_ref, rs_ref, back_ref, image_ref, state_ref,
                  do_ref, ro_ref, ov_ref, observed_ref,
                  ds_out, do_out, inc_out, rm_out, ro_out, rs_out, ds_s, inc_s, rm_s, rs_s, sems):
    sums = sums_ref[0]
    for k in range(1, sums_ref.shape[0]):
        sums = sums + sums_ref[k]
    lane = lax.broadcasted_iota(jnp.int32, sums.shape, 1)
    projected = jnp.sum(jnp.where(lane == 0, sums, 0.0), axis=1, keepdims=True)
    curvature = jnp.sum(jnp.where(lane == 1, sums, 0.0), axis=1, keepdims=True)
    step = projected / curvature
    levels, rows, columns = rs_ref.shape
    parts, _, width = back_ref.shape
    per_level = parts // levels
    wide = jnp.broadcast_to(step, (rows, width))
    starts = where_ref[0] == 0
    copies = []
    for level in range(levels):
        for piece in range(per_level):
            part = level * per_level + piece
            cols = slice(piece * width, (piece + 1) * width)
            rs, rm = rs_ref[level, :, cols], rm_ref[level, :, cols]
            dual = back_ref[part, rows : 2 * rows, :] + rs
            ds_s[level, :, cols] = ds_ref[level, :, cols] + wide * dual
            inc_s[level, :, cols] = inc_ref[level, :, cols] + wide * back_ref[part, 0:rows, :]
            image = jnp.where(starts, rm, image_ref[level, :, cols])
            rm_s[level, :, cols] = rm - wide * image
            rs_s[level, :, cols] = rs - wide * state_ref[level, :, cols]
        pairs = ((ds_s, ds_out), (inc_s, inc_out), (rm_s, rm_out), (rs_s, rs_out))
        for place, (held, out) in enumerate(pairs):
            copies.append(pltpu.make_async_copy(held.at[level], out.at[level], sems.at[level, place]))
            copies[-1].start()
    narrow = jnp.broadcast_to(step, ro_ref.shape)
    ro, ov = ro_ref[...], ov_ref[...]
    dual = ro / ov
    do_out[...] = do_ref[...] + narrow * dual
    ro_out[...] = ro - narrow * (ov * dual + observed_ref[...])
    for copy in copies:
        copy.wait()


def body(windows, bricks, courant_x, courant_y, model_var, obs_var, obs_brick, obs_cell, obs_step,
         dual_state, dual_obs, increment, resid_model, resid_obs, resid_state):
    cx, cy, mv = courant_x[0], courant_y[0], model_var[0]
    ds, inc, rm, rs = dual_state[0], increment[0], resid_model[0], resid_state[0]
    levels, rows, columns = rs.shape
    per_level = windows // levels
    width = columns // per_level
    blocks = bricks
    groups = levels * (columns // LANES) * 8
    field_bytes = 4 * levels * rows * columns
    here = lax.axis_index("space").astype(jnp.int32)
    window = lax.axis_index("tm").astype(jnp.int32)
    where = jnp.stack([window, jnp.int32(windows), here])
    at = here[None]

    upward = [(i, i + 1) for i in range(bricks - 1)]
    downward = [(i + 1, i) for i in range(bricks - 1)]

    packed = pl.pallas_call(
        functools.partial(pack_kernel, windows),
        out_shape=f32(windows, 3 * rows, width),
        in_specs=[VMEM] * 3,
        out_specs=VMEM,
        compiler_params=params(60),
        cost_estimate=cost(0, 6 * field_bytes),
        name="pack",
    )(rs, rm, mv)
    windows_of = lax.all_to_all(packed, "tm", 0, 0)

    rm_next = lax.ppermute(rm, "tm", [(i + 1, i) for i in range(windows - 1)])
    near = jnp.concatenate([resid_obs, resid_obs / obs_var], axis=1)
    distance = 1
    while distance < bricks // 2:
        other = lax.ppermute(near, "space", [(i, i ^ distance) for i in range(bricks)])
        near = jnp.concatenate([near, other], axis=0)
        distance *= 2
    far = lax.ppermute(near, "space", [(i, i ^ distance) for i in range(bricks)])
    slots = blocks * (CHUNK // BLOCK) * SLOTS
    rank, code, hot, slot_cols, passes = pl.pallas_call(
        functools.partial(place_kernel, columns),
        out_shape=(
            i32(blocks, CHUNK), i32(blocks, CHUNK), b16(slots, groups), i32(slots, LANES), i32(1),
        ),
        in_specs=[SMEM, VMEM, VMEM, VMEM],
        out_specs=(VMEM, VMEM, HBM, HBM, SMEM),
        scratch_shapes=[pltpu.VMEM((blocks, CHUNK), jnp.int32)] * 3
        + [
            pltpu.VMEM((slots, groups), jnp.bfloat16), pltpu.VMEM((slots, LANES), jnp.int32),
            pltpu.SemaphoreType.DMA((blocks, 2)),
        ],
        compiler_params=params(60),
        cost_estimate=cost(0, 8 * field_bytes),
        name="places",
    )(at, obs_brick, obs_cell, obs_step)
    slot_scratch = [
        pltpu.VMEM((slots, groups), jnp.bfloat16), pltpu.VMEM((slots, LANES), jnp.int32),
    ]
    spread_start, spread_middle, edge_rows, resid_all = pl.pallas_call(
        spread_kernel,
        out_shape=(
            f32(levels, rows, columns), f32(levels, rows, columns), f32(32, columns),
            f32(blocks, CHUNK),
        ),
        in_specs=[SMEM, SMEM, VMEM, VMEM, HBM, HBM] + [VMEM] * 4,
        out_specs=(VMEM,) * 4,
        scratch_shapes=[
            pltpu.VMEM((groups, 2 * LANES), jnp.float32),
            *slot_scratch,
            *slot_scratch,
            pltpu.VMEM((slots, 2 * LANES), jnp.bfloat16),
            pltpu.VMEM((slots, 2 * LANES), jnp.bfloat16),
            pltpu.VMEM((blocks, CHUNK), jnp.float32),
            pltpu.SemaphoreType.DMA((2,)),
        ],
        compiler_params=params(60),
        cost_estimate=cost(4 * slots * groups * 2 * LANES, 16 * field_bytes),
        name="spread",
    )(at, passes, rank, code, hot, slot_cols, near, far, cx, cy)

    summed = pl.pallas_call(
        scan_kernel,
        out_shape=f32(windows, 2 * rows, width),
        in_specs=[VMEM, ANY, ANY],
        out_specs=VMEM,
        compiler_params=params(4),
        cost_estimate=cost(0, 5 * field_bytes),
        name="scan",
    )(windows_of, code, near)
    back = lax.all_to_all(summed, "tm", 0, 0)
    up, down = pl.pallas_call(
        functools.partial(edge_kernel, levels),
        out_shape=(f32(24, columns), f32(24, columns)),
        in_specs=[VMEM, VMEM],
        out_specs=(VMEM, VMEM),
        scratch_shapes=[pltpu.VMEM((32, columns), jnp.float32)],
        compiler_params=params(6),
        cost_estimate=cost(0, 3 * field_bytes),
        name="edges",
    )(back, edge_rows)
    below = lax.ppermute(up, "space", upward)
    above = lax.ppermute(down, "space", downward)

    image_next, image_state, sent = pl.pallas_call(
        image_kernel,
        out_shape=(
            f32(levels, rows, columns), f32(levels, rows, columns), f32(blocks, 1, CHUNK + LANES),
        ),
        in_specs=[SMEM, SMEM] + [HBM] * 12 + [VMEM] * 3,
        out_specs=(VMEM, VMEM, VMEM),
        scratch_shapes=[
            pltpu.VMEM((windows, 2 * rows, width), jnp.float32),
            pltpu.VMEM((24, columns), jnp.float32),
            pltpu.VMEM((24, columns), jnp.float32),
            *[pltpu.VMEM((levels, rows, columns), jnp.float32)] * 7,
            *slot_scratch,
            pltpu.VMEM((groups, 2 * LANES), jnp.float32),
            *slot_scratch,
            pltpu.VMEM((blocks, CHUNK), jnp.float32),
            pltpu.SemaphoreType.DMA((levels, 8)),
            pltpu.SemaphoreType.DMA((4,)),
        ],
        compiler_params=params(60),
        cost_estimate=cost(4 * slots * groups * 2 * LANES, 24 * field_bytes),
        name="images",
    )(where, passes, back, below, above, cx, cy, spread_start, spread_middle, rs, rm, rm_next,
      hot, slot_cols, rank, code, resid_all)

    image_model = lax.ppermute(image_next, "tm", [(i, i + 1) for i in range(windows - 1)])
    got = lax.all_to_all(sent, "space", 0, 0)
    observed, sums = pl.pallas_call(
        gather_kernel,
        out_shape=(f32(1, CHUNK), f32(windows, 1, LANES)),
        in_specs=[VMEM],
        out_specs=(VMEM, VMEM),
        compiler_params=params(4),
        cost_estimate=cost(0, 200000),
        name="first_sums",
    )(got)
    all_sums = lax.all_to_all(sums, "tm", 0, 0)

    count = resid_obs.shape[1]
    held = pltpu.VMEM((levels, rows, columns), jnp.float32)
    new_ds, new_do, new_inc, new_rm, new_ro, new_rs = pl.pallas_call(
        update_kernel,
        out_shape=(
            f32(levels, rows, columns), f32(1, count), f32(levels, rows, columns),
            f32(levels, rows, columns), f32(1, count), f32(levels, rows, columns),
        ),
        in_specs=[SMEM] + [VMEM] * 12,
        out_specs=(ANY, VMEM, ANY, ANY, VMEM, ANY),
        scratch_shapes=[held] * 4 + [pltpu.SemaphoreType.DMA((levels, 4))],
        compiler_params=params(8),
        cost_estimate=cost(0, 12 * field_bytes),
        name="updates",
    )(where, all_sums, ds, inc, rm, rs, back, image_model, image_state,
      dual_obs, resid_obs, obs_var, observed)
    return new_ds[None], new_do, new_inc[None], new_rm[None], new_ro, new_rs[None]


def solution(mesh):
    field = P("tm", None, "space", None)
    obs = P("tm", "space")
    shared = P("tm", None)
    return jax.shard_map(
        functools.partial(body, mesh.shape["tm"], mesh.shape["space"]),
        mesh=mesh,
        in_specs=(
            field, field, field, obs, shared, shared, shared,
            field, obs, field, field, obs, field,
        ),
        out_specs=(field, obs, field, field, obs, field),
        check_vma=False,
    )
```

time: 129 us -> 115 us (0.89)
  local copies, waits for them, and re-layouts: 14.5 us -> 5.63 us
  waiting for transfers between devices: 17.2 us -> 10 us
  Pallas kernels: 24 us -> 30.7 us
  starting transfers between devices: 44.3 us -> 37.7 us
  blocking collectives: 26.9 us -> 28.8 us
    all_to_all x1, waiting for transfers between devices: 15.7 us -> 1.85 us  [body(): windows_of = lax.all_to_all(packed, 'tm', 0, 0)]
    ppermute x6 -> x4, starting transfers between devices: 21.8 us -> 11.9 us  [body(): lax.ppermute(near, 'space', [(i, i ^ distance) for i in range(bricks)])]
    unnamed x65 -> x38, local copies, waits for them, and re-layouts: 12.8 us -> 5.63 us
    pallas_call x1, Pallas kernels: 1.34 us -> 6.69 us  [body(): pl.pallas_call(functools.partial(place_kernel, columns), out_shape=(i32(b...]
    ppermute x1, waiting for transfers between devices: 0.01 us -> 4.39 us  [body(): above = lax.ppermute(down, 'space', downward)]
    ppermute x1, starting transfers between devices: 3.63 us -> 6.17 us  [body(): below = lax.ppermute(up, 'space', upward)]
    pallas_call x4 -> x3, Pallas kernels: 4.97 us -> 2.89 us  [the longest x1 2.54 us: body(): pl.pallas_call(update_kernel, out_shape=(f32(levels, rows, columns), f32(...]
    all_to_all x2, blocking collectives: 26.9 us -> 28.8 us  [the longest x1 16.3 us: body(): got = lax.all_to_all(sent, 'space', 0, 0)]
  transfers between devices with their start and end apart: 12 -> 10, of which waited for: 3 -> 6; matrix products, arithmetic and copies ran while one was open for 2% -> 1% of each run, Pallas kernels for 9% -> 13%
where the time goes in v2:
time: 115 us; the launch traced here: 114 us
  starting transfers between devices  37.7 us (33%)
  Pallas kernels  30.7 us (27%)
  blocking collectives  28.8 us (25%)
  waiting for transfers between devices  10 us (9%)
  local copies, waits for them, and re-layouts  5.63 us (5%)
    all_to_all x1, blocking collectives, body(): got = lax.all_to_all(sent, 'space', 0, 0)  16.3 us
    all_to_all x1, blocking collectives, body(): all_sums = lax.all_to_all(sums, 'tm', 0, 0)  12.5 us
    ppermute x4, starting transfers between devices, body(): lax.ppermute(near, 'space', [(i, i ^ distance) for i in range(bricks)])  11.9 us
    pallas_call x1, Pallas kernels, body(): pl.pallas_call(image_kernel, out_shape=(f32(levels, rows, columns), f32(l...  9.87 us
    pallas_call x1, Pallas kernels, body(): pl.pallas_call(spread_kernel, out_shape=(f32(levels, rows, columns), f32(...  7.93 us
    all_to_all x1, starting transfers between devices, body(): windows_of = lax.all_to_all(packed, 'tm', 0, 0)  7.72 us
    pallas_call x1, Pallas kernels, body(): pl.pallas_call(functools.partial(place_kernel, columns), out_shape=(i32(b...  6.69 us
    ppermute x1, starting transfers between devices, body(): below = lax.ppermute(up, 'space', upward)  6.17 us
  transfers between devices with their start and end apart: 10, of which 6 were waited for; matrix products, arithmetic and copies ran while one was open for 1% of the time, Pallas kernels for 13%

profile of v2, /device:TPU:1, one launch (start us, length us, event | category | flops | bytes accessed | tf_op | source)
XLA Modules:
  0.0 114.5 jit_solution(9719489678803506639)
XLA Ops:
  0.6 2.3 %pack.1 = f32[16,24,768]{2,1,0:T(8,128)} custom-call(f32[4,8,3072]{2,1,0:T(8,128)} %bitcast.13, f32[4,8,3072]{2,1,0:T(8,128)} %bitcast.16, f32[4,8,3072]{2,1,0:T(8,128)} %bitcast.26), custom_call_target="tpu_custom_call" | custom-call | bytes 2359296 | tf_op jit(solution)/shard_map/pack/pallas_call | solution.py:510
  3.0 0.0 copy-start.11
  3.0 0.0 copy-start.12
  3.0 7.7 %all-to-all-start = ((f32[16,24,768]{2,1,0:T(8,128)}), f32[16,24,768]{2,1,0:T(8,128)S(1)}, u32[]{:S(2)}, u32[]{:S(2)}) async-start(f32[16,24,768]{2,1,0:T(8,128)} %pack.1), calls=%async_computation | async-start | bytes 2359296 | tf_op jit(solution)/shard_map/all_to_all | solution.py:519
  10.7 0.0 copy-done.11
  10.7 0.0 copy-done.12
  10.8 1.0 collective-permute-start
  11.8 0.8 collective-permute-done
  12.6 1.7 %collective-permute-start.1 = (f32[2,2048]{1,0:T(2,128)S(1)}, f32[2,2048]{1,0:T(2,128)S(1)}, u32[]{:S(2)}, u32[]{:S(2)}) collective-permute-start(f32[2,2048]{1,0:T(2,128)S(1)} %pad_maximum_fusion.2), channel_id=1, source_target_pairs={{0,2},{1,3},{2,0},{3,1},{4,6},{5,7},{6,4},{7,5},{8,10},{9,11},{10,... | collective-permute-start | bytes 49160 | tf_op jit(solution)/shard_map/ppermute | solution.py:525
  14.4 1.4 %collective-permute-done.1 = f32[2,2048]{1,0:T(2,128)S(1)} collective-permute-done((f32[2,2048]{1,0:T(2,128)S(1)}, f32[2,2048]{1,0:T(2,128)S(1)}, u32[]{:S(2)}, u32[]{:S(2)}) %collective-permute-start.1) | collective-permute-done | bytes 16416 | tf_op jit(solution)/shard_map/ppermute | solution.py:525
  15.8 3.1 %collective-permute-start.2 = (f32[4,2048]{1,0:T(4,128)S(1)}, f32[4,2048]{1,0:T(4,128)S(1)}, u32[]{:S(2)}, u32[]{:S(2)}) collective-permute-start(f32[4,2048]{1,0:T(4,128)S(1)} %pad_maximum_fusion.1), channel_id=1, source_target_pairs={{0,4},{1,5},{2,6},{3,7},{4,0},{5,1},{6,2},{7,3},{8,12},{9,13},{10,... | collective-permute-start | bytes 98312 | tf_op jit(solution)/shard_map/ppermute | solution.py:525
  18.9 6.7 %places.1 = (s32[16,1024]{1,0:T(8,128)}, s32[16,1024]{1,0:T(8,128)}, bf16[2048,768]{1,0:T(8,128)(2,1)}, s32[2048,128]{1,0:T(8,128)}, s32[1]{0:T(128)}) custom-call(s32[1]{0:T(128)} %bitcast.1.at_ref, s32[1,16384]{1,0:T(1,128)} %brick_ref.1, s32[1,16384]{1,0:T(1,128)} %cell_ref.1, s32[1,16384]{1,0:T(1,128)} %step_ref.1), custom_call_target="tpu_custom_call" | custom-call | bytes 3145728 | tf_op jit(solution)/shard_map/places/pallas_call | solution.py:530
  25.6 0.0 collective-permute-done.2
  25.7 0.0 copy-start.10
  25.7 1.8 %all-to-all-done.in_ref = f32[16,24,768]{2,1,0:T(8,128)S(1)} async-done(((f32[16,24,768]{2,1,0:T(8,128)}), f32[16,24,768]{2,1,0:T(8,128)S(1)}, u32[]{:S(2)}, u32[]{:S(2)}) %all-to-all-start) | async-done | bytes 1179680 | tf_op jit(solution)/shard_map/all_to_all | solution.py:519
  27.5 0.8 copy-done.9
  28.4 1.0 scan.1
  29.3 0.0 copy-start.3
  29.3 5.2 %all-to-all-start.1 = ((f32[16,16,768]{2,1,0:T(8,128)}), f32[16,16,768]{2,1,0:T(8,128)S(1)}, u32[]{:S(2)}, u32[]{:S(2)}) async-start(f32[16,16,768]{2,1,0:T(8,128)} %scan.1), calls=%async_computation.1 | async-start | bytes 1572864 | tf_op jit(solution)/shard_map/all_to_all | solution.py:580
  34.6 0.0 copy-done.10
  34.6 6.1 %collective-permute-start.3 = (f32[8,2048]{1,0:T(8,128)S(1)}, f32[8,2048]{1,0:T(8,128)S(1)}, u32[]{:S(2)}, u32[]{:S(2)}) collective-permute-start(f32[8,2048]{1,0:T(8,128)S(1)} %pad_maximum_fusion.rest_1_.near_ref), channel_id=1, source_target_pairs={{0,8},{1,9},{2,10},{3,11},{4,12},{5,13},{6,14},{7,15},{8,0},{9,1},... | collective-permute-start | bytes 196616 | tf_op jit(solution)/shard_map/ppermute | solution.py:528
  40.7 0.0 copy-done.3
  40.7 1.3 %collective-permute-start.6 = (f32[4,8,3072]{2,1,0:T(8,128)S(1)}, f32[4,8,3072]{2,1,0:T(8,128)S(1)}, u32[]{:S(2)}, u32[]{:S(2)}) collective-permute-start(f32[4,8,3072]{2,1,0:T(8,128)S(1)} %bitcast.18), channel_id=1, source_target_pairs={{16,0},{32,16},{48,32},{64,48},{80,64},{96,80},{112,96},{128,112},... | collective-permute-start | bytes 1179656 | tf_op jit(solution)/shard_map/ppermute | solution.py:521
  42.0 0.4 collective-permute-done.3.far_ref
  42.4 0.0 copy-start.18
  42.4 0.6 copy-done.18
  43.0 7.9 %spread.1 = (f32[4,8,3072]{2,1,0:T(8,128)}, f32[4,8,3072]{2,1,0:T(8,128)}, f32[32,3072]{1,0:T(8,128)}, f32[16,1024]{1,0:T(8,128)}) custom-call(s32[1]{0:T(128)} %bitcast.1.at_ref, s32[1]{0:T(128)} %get-tuple-element.28.passes_ref, s32[16,1024]{1,0:T(8,128)} %get-tuple-element.30.rank_ref, s32[16,1024]{1,0:T(8,128)} %get-tuple-element.29.rest_0_.code_ref, ...), custom_call_target="tpu_custom_call" | custom-call | flops 1610612736 | bytes 6291456 | tf_op jit(solution)/shard_map/spread/pallas_call | solution.py:549
  51.0 0.0 all-to-all-done.1.back_ref.back_hbm
  51.0 0.0 copy-start
  51.0 0.0 copy-start.5
  51.0 1.3 %copy-done.5 = f32[32,3072]{1,0:T(8,128)S(1)} copy-done((f32[32,3072]{1,0:T(8,128)S(1)}, f32[32,3072]{1,0:T(8,128)}, u32[]{:S(2)}) %copy-start.5) | copy-done | bytes 393240
  52.3 0.3 edges.1
  52.6 6.2 %collective-permute-start.4 = (f32[24,3072]{1,0:T(8,128)S(1)}, f32[24,3072]{1,0:T(8,128)S(1)}, u32[]{:S(2)}, u32[]{:S(2)}) collective-permute-start(f32[24,3072]{1,0:T(8,128)S(1)} %get-tuple-element.34), channel_id=1, source_target_pairs={{0,1},{1,2},{2,3},{3,4},{4,5},{5,6},{6,7},{7,8},{8,9},{9,10},{10,1... | collective-permute-start | bytes 884744 | tf_op jit(solution)/shard_map/ppermute | solution.py:591
  58.8 1.9 %collective-permute-start.5 = (f32[24,3072]{1,0:T(8,128)S(1)}, f32[24,3072]{1,0:T(8,128)S(1)}, u32[]{:S(2)}, u32[]{:S(2)}) collective-permute-start(f32[24,3072]{1,0:T(8,128)S(1)} %get-tuple-element.35), channel_id=1, source_target_pairs={{1,0},{2,1},{3,2},{4,3},{5,4},{6,5},{7,6},{8,7},{9,8},{10,9},{11,1... | collective-permute-start | bytes 884744 | tf_op jit(solution)/shard_map/ppermute | solution.py:592
  60.7 0.6 pad_add_fusion.where_ref
  61.3 0.0 collective-permute-done.6.rm_next_hbm
  61.3 0.0 copy-start.15
  61.3 1.1 collective-permute-done.4.below_hbm
  62.4 0.0 copy-start.16
  62.4 4.4 %collective-permute-done.5.above_hbm = f32[24,3072]{1,0:T(8,128)S(1)} collective-permute-done((f32[24,3072]{1,0:T(8,128)S(1)}, f32[24,3072]{1,0:T(8,128)S(1)}, u32[]{:S(2)}, u32[]{:S(2)}) %collective-permute-start.5) | collective-permute-done | bytes 294944 | tf_op jit(solution)/shard_map/ppermute | solution.py:592
  66.8 0.0 copy-start.17
  66.8 0.0 copy-done
  66.8 0.0 copy-done.15
  66.8 0.0 copy-done.16
  66.8 0.7 copy-done.17
  67.6 0.0 copy-start.2
  67.6 0.0 copy-start.4
  67.6 0.0 copy-start.13
  67.6 0.0 copy-start.14
  67.6 9.9 %images.1 = (f32[4,8,3072]{2,1,0:T(8,128)}, f32[4,8,3072]{2,1,0:T(8,128)}, f32[16,1,1152]{2,1,0:T(1,128)}) custom-call(s32[3]{0:T(128)} %pad_add_fusion.where_ref, s32[1]{0:T(128)} %get-tuple-element.28.passes_ref, f32[16,16,768]{2,1,0:T(8,128)} %copy-done, f32[24,3072]{1,0:T(8,128)} %copy-done.16, f32[24,3072]{1,0:T(8,128)} %copy-done.17, ...), custom_call_target="tpu_custom_call" | custom-call | flops 1610612736 | bytes 9437184 | tf_op jit(solution)/shard_map/images/pallas_call | solution.py:594
  77.5 3.5 %collective-permute-start.7 = (f32[4,8,3072]{2,1,0:T(8,128)}, f32[4,8,3072]{2,1,0:T(8,128)S(1)}, u32[]{:S(2)}, u32[]{:S(2)}) collective-permute-start(f32[4,8,3072]{2,1,0:T(8,128)} %get-tuple-element.41), channel_id=1, source_target_pairs={{0,16},{16,32},{32,48},{48,64},{64,80},{80,96},{96,112},{112,128},... | collective-permute-start | bytes 1179656 | tf_op jit(solution)/shard_map/ppermute | solution.py:619
  80.9 16.3 %all_to_all.20.got_ref = f32[16,1,1152]{2,1,0:T(1,128)S(1)} all-to-all(f32[16,1,1152]{2,1,0:T(1,128)} %get-tuple-element.39), channel_id=1, replica_groups=mesh['tm'=16,'space'=16] {'space'}, dimensions={0} | all-to-all | bytes 147456 | tf_op jit(solution)/shard_map/all_to_all | solution.py:620
  97.3 12.5 %all_to_all.21.sums_ref = f32[16,1,128]{2,1,0:T(1,128)S(1)} all-to-all(f32[16,1,128]{2,1,0:T(1,128)S(1)} %get-tuple-element.40), channel_id=1, replica_groups=mesh['tm'=16,'space'=16] {'tm'}, dimensions={0} | all-to-all | bytes 16384 | tf_op jit(solution)/shard_map/all_to_all | solution.py:630
  109.7 0.0 collective-permute-done.7.image_ref
  109.7 0.0 copy-done.2
  109.7 0.0 copy-done.4
  109.7 0.0 copy-done.6
  109.8 0.0 copy-done.7
  109.8 0.0 copy-done.13
  109.8 0.0 copy-done.14
  109.8 0.0 copy-start.1
  109.8 1.1 copy-done.1
  110.9 1.0 copy-done.8
  111.9 2.5 %updates.1 = (f32[4,8,3072]{2,1,0:T(8,128)}, f32[1,1024]{1,0:T(1,128)}, f32[4,8,3072]{2,1,0:T(8,128)}, f32[4,8,3072]{2,1,0:T(8,128)}, f32[1,1024]{1,0:T(1,128)}, /*index=5*/f32[4,8,3072]{2,1,0:T(8,128)}) custom-call(s32[3]{0:T(128)S(1)} %copy-done.13, f32[16,1,128]{2,1,0:T(1,128)S(1)} %all_to_all.21.sums_ref, f32[4,8,3072]{2,1,0:T(8,128)S(1)} %bitcast.20, ...), custom_call_target="tpu_custom_call" | custom-call | bytes 4718592 | tf_op jit(solution)/shard_map/updates/pallas_call | solution.py:634
  (10 shorter events, 0.1 us)
Async XLA Ops:
  3.0 7.7 %copy-start.11 = (f32[1,1024]{1,0:T(1,128)S(1)}, f32[1,1024]{1,0:T(1,128)}, u32[]{:S(2)}) copy-start(f32[1,1024]{1,0:T(1,128)} %ro_ref.1) | copy-start | bytes 12292
  3.0 7.7 %copy-start.12 = (f32[1,1024]{1,0:T(1,128)S(1)}, f32[1,1024]{1,0:T(1,128)}, u32[]{:S(2)}) copy-start(f32[1,1024]{1,0:T(1,128)} %ov_ref.1) | copy-start | bytes 12292
  3.0 24.5 %all-to-all-start = ((f32[16,24,768]{2,1,0:T(8,128)}), f32[16,24,768]{2,1,0:T(8,128)S(1)}, u32[]{:S(2)}, u32[]{:S(2)}) async-start(f32[16,24,768]{2,1,0:T(8,128)} %pack.1), calls=%async_computation | async-start | bytes 2359296 | tf_op jit(solution)/shard_map/all_to_all | solution.py:519
  10.8 1.9 %collective-permute-start = (f32[1,2048]{1,0:T(1,128)S(1)}, f32[1,2048]{1,0:T(1,128)S(1)}, u32[]{:S(2)}, u32[]{:S(2)}) collective-permute-start(f32[1,2048]{1,0:T(1,128)S(1)} %pad_maximum_fusion.3), channel_id=1, source_target_pairs={{0,1},{1,0},{2,3},{3,2},{4,5},{5,4},{6,7},{7,6},{8,9},{9,8},{10,11... | collective-permute-start | bytes 24584 | tf_op jit(solution)/shard_map/ppermute | solution.py:525
  12.6 3.1 %collective-permute-start.1 = (f32[2,2048]{1,0:T(2,128)S(1)}, f32[2,2048]{1,0:T(2,128)S(1)}, u32[]{:S(2)}, u32[]{:S(2)}) collective-permute-start(f32[2,2048]{1,0:T(2,128)S(1)} %pad_maximum_fusion.2), channel_id=1, source_target_pairs={{0,2},{1,3},{2,0},{3,1},{4,6},{5,7},{6,4},{7,5},{8,10},{9,11},{10,... | collective-permute-start | bytes 49160 | tf_op jit(solution)/shard_map/ppermute | solution.py:525
  15.8 9.8 %collective-permute-start.2 = (f32[4,2048]{1,0:T(4,128)S(1)}, f32[4,2048]{1,0:T(4,128)S(1)}, u32[]{:S(2)}, u32[]{:S(2)}) collective-permute-start(f32[4,2048]{1,0:T(4,128)S(1)} %pad_maximum_fusion.1), channel_id=1, source_target_pairs={{0,4},{1,5},{2,6},{3,7},{4,0},{5,1},{6,2},{7,3},{8,12},{9,13},{10,... | collective-permute-start | bytes 98312 | tf_op jit(solution)/shard_map/ppermute | solution.py:525
  25.7 8.9 %copy-start.10 = (f32[8,2048]{1,0:T(8,128)}, f32[8,2048]{1,0:T(8,128)S(1)}, u32[]{:S(2)}) copy-start(f32[8,2048]{1,0:T(8,128)S(1)} %pad_maximum_fusion.rest_1_.near_ref) | copy-start | bytes 196612
  27.5 0.8 copy-start.9
  29.3 11.4 %copy-start.3 = (f32[1,4,8,3072]{3,2,1,0:T(8,128)S(1)}, f32[1,4,8,3072]{3,2,1,0:T(8,128)}, u32[]{:S(2)}) copy-start(f32[1,4,8,3072]{3,2,1,0:T(8,128)} %param.23) | copy-start | bytes 1179652
  29.3 21.6 %all-to-all-start.1 = ((f32[16,16,768]{2,1,0:T(8,128)}), f32[16,16,768]{2,1,0:T(8,128)S(1)}, u32[]{:S(2)}, u32[]{:S(2)}) async-start(f32[16,16,768]{2,1,0:T(8,128)} %scan.1), calls=%async_computation.1 | async-start | bytes 1572864 | tf_op jit(solution)/shard_map/all_to_all | solution.py:580
  34.6 7.8 %collective-permute-start.3 = (f32[8,2048]{1,0:T(8,128)S(1)}, f32[8,2048]{1,0:T(8,128)S(1)}, u32[]{:S(2)}, u32[]{:S(2)}) collective-permute-start(f32[8,2048]{1,0:T(8,128)S(1)} %pad_maximum_fusion.rest_1_.near_ref), channel_id=1, source_target_pairs={{0,8},{1,9},{2,10},{3,11},{4,12},{5,13},{6,14},{7,15},{8,0},{9,1},... | collective-permute-start | bytes 196616 | tf_op jit(solution)/shard_map/ppermute | solution.py:528
  40.7 20.6 %collective-permute-start.6 = (f32[4,8,3072]{2,1,0:T(8,128)S(1)}, f32[4,8,3072]{2,1,0:T(8,128)S(1)}, u32[]{:S(2)}, u32[]{:S(2)}) collective-permute-start(f32[4,8,3072]{2,1,0:T(8,128)S(1)} %bitcast.18), channel_id=1, source_target_pairs={{16,0},{32,16},{48,32},{64,48},{80,64},{96,80},{112,96},{128,112},... | collective-permute-start | bytes 1179656 | tf_op jit(solution)/shard_map/ppermute | solution.py:521
  42.4 0.6 copy-start.18
  51.0 15.8 %copy-start = (f32[16,16,768]{2,1,0:T(8,128)}, f32[16,16,768]{2,1,0:T(8,128)S(1)}, u32[]{:S(2)}) copy-start(f32[16,16,768]{2,1,0:T(8,128)S(1)} %all-to-all-done.1.back_ref.back_hbm) | copy-start | bytes 2359300
  51.0 1.3 %copy-start.5 = (f32[32,3072]{1,0:T(8,128)S(1)}, f32[32,3072]{1,0:T(8,128)}, u32[]{:S(2)}) copy-start(f32[32,3072]{1,0:T(8,128)} %get-tuple-element.33.rows_ref) | copy-start | bytes 1179652
  52.6 9.8 %collective-permute-start.4 = (f32[24,3072]{1,0:T(8,128)S(1)}, f32[24,3072]{1,0:T(8,128)S(1)}, u32[]{:S(2)}, u32[]{:S(2)}) collective-permute-start(f32[24,3072]{1,0:T(8,128)S(1)} %get-tuple-element.34), channel_id=1, source_target_pairs={{0,1},{1,2},{2,3},{3,4},{4,5},{5,6},{6,7},{7,8},{8,9},{9,10},{10,1... | collective-permute-start | bytes 884744 | tf_op jit(solution)/shard_map/ppermute | solution.py:591
  58.8 8.0 %collective-permute-start.5 = (f32[24,3072]{1,0:T(8,128)S(1)}, f32[24,3072]{1,0:T(8,128)S(1)}, u32[]{:S(2)}, u32[]{:S(2)}) collective-permute-start(f32[24,3072]{1,0:T(8,128)S(1)} %get-tuple-element.35), channel_id=1, source_target_pairs={{1,0},{2,1},{3,2},{4,3},{5,4},{6,5},{7,6},{8,7},{9,8},{10,9},{11,1... | collective-permute-start | bytes 884744 | tf_op jit(solution)/shard_map/ppermute | solution.py:592
  61.3 5.5 %copy-start.15 = (f32[4,8,3072]{2,1,0:T(8,128)}, f32[4,8,3072]{2,1,0:T(8,128)S(1)}, u32[]{:S(2)}) copy-start(f32[4,8,3072]{2,1,0:T(8,128)S(1)} %collective-permute-done.6.rm_next_hbm) | copy-start | bytes 1179652
  62.4 4.4 %copy-start.16 = (f32[24,3072]{1,0:T(8,128)}, f32[24,3072]{1,0:T(8,128)S(1)}, u32[]{:S(2)}) copy-start(f32[24,3072]{1,0:T(8,128)S(1)} %collective-permute-done.4.below_hbm) | copy-start | bytes 884740
  66.8 0.7 copy-start.17
  67.6 42.2 %copy-start.2 = (f32[1,4,8,3072]{3,2,1,0:T(8,128)S(1)}, f32[1,4,8,3072]{3,2,1,0:T(8,128)}, u32[]{:S(2)}) copy-start(f32[1,4,8,3072]{3,2,1,0:T(8,128)} %param.25) | copy-start | bytes 1179652
  67.6 42.2 %copy-start.4 = (f32[1,4,8,3072]{3,2,1,0:T(8,128)S(1)}, f32[1,4,8,3072]{3,2,1,0:T(8,128)}, u32[]{:S(2)}) copy-start(f32[1,4,8,3072]{3,2,1,0:T(8,128)} %param.23) | copy-start | bytes 1179652
  67.6 42.2 %copy-start.6 = (f32[1,4,8,3072]{3,2,1,0:T(8,128)S(1)}, f32[1,4,8,3072]{3,2,1,0:T(8,128)}, u32[]{:S(2)}) copy-start(f32[1,4,8,3072]{3,2,1,0:T(8,128)} %param.20) | copy-start | bytes 1179652
  67.6 42.2 %copy-start.7 = (f32[1,4,8,3072]{3,2,1,0:T(8,128)S(1)}, f32[1,4,8,3072]{3,2,1,0:T(8,128)}, u32[]{:S(2)}) copy-start(f32[1,4,8,3072]{3,2,1,0:T(8,128)} %param.22) | copy-start | bytes 1179652
  67.6 42.2 %copy-start.13 = (s32[3]{0:T(128)S(1)}, s32[3]{0:T(128)}, u32[]{:S(2)}) copy-start(s32[3]{0:T(128)} %pad_add_fusion.where_ref) | copy-start | bytes 40
  67.6 42.2 %copy-start.14 = (f32[1,1024]{1,0:T(1,128)S(1)}, f32[1,1024]{1,0:T(1,128)}, u32[]{:S(2)}) copy-start(f32[1,1024]{1,0:T(1,128)} %do_ref.1) | copy-start | bytes 12292
  77.5 32.3 %collective-permute-start.7 = (f32[4,8,3072]{2,1,0:T(8,128)}, f32[4,8,3072]{2,1,0:T(8,128)S(1)}, u32[]{:S(2)}, u32[]{:S(2)}) collective-permute-start(f32[4,8,3072]{2,1,0:T(8,128)} %get-tuple-element.41), channel_id=1, source_target_pairs={{0,16},{16,32},{32,48},{48,64},{64,80},{80,96},{96,112},{112,128},... | collective-permute-start | bytes 1179656 | tf_op jit(solution)/shard_map/ppermute | solution.py:619
  109.8 1.1 copy-start.1
  110.9 1.0 copy-start.8

commit v3 on v2

v3 whole, which is shorter than its diff:
```python
import functools

import jax
import jax.numpy as jnp
from jax import lax
from jax.experimental import pallas as pl
from jax.experimental.pallas import tpu as pltpu
from jax.sharding import PartitionSpec as P

LANES = 128
SLOTS = 64
BLOCK = 512
CHUNK = 1024
MIB = 1024 * 1024


def params(mib):
    return pltpu.CompilerParams(vmem_limit_bytes=mib * MIB)


def cost(flops, touched):
    return pl.CostEstimate(flops=flops, bytes_accessed=touched, transcendentals=0)


VMEM = pl.BlockSpec(memory_space=pltpu.VMEM)
SMEM = pl.BlockSpec(memory_space=pltpu.SMEM)
ANY = pl.BlockSpec(memory_space=pl.ANY)
HBM = pl.BlockSpec(memory_space=pltpu.HBM)


def f32(*shape):
    return jax.ShapeDtypeStruct(shape, jnp.float32)


def i32(*shape):
    return jax.ShapeDtypeStruct(shape, jnp.int32)


def b16(*shape):
    return jax.ShapeDtypeStruct(shape, jnp.bfloat16)


def duals_kernel(ro_ref, ov_ref, out_ref):
    count = ro_ref.shape[1]
    out_ref[:, 0:count] = ro_ref[...]
    out_ref[:, count : 2 * count] = ro_ref[...] / ov_ref[...]


def join_kernel(*refs):
    out_ref = refs[-1]
    rows = refs[0].shape[0]
    for place, ref in enumerate(refs[:-1]):
        out_ref[place * rows : (place + 1) * rows, :] = ref[...]


def gather_fields_kernel(cx_ref, cy_ref, rs_ref, after_ref, out_ref):
    levels = cx_ref.shape[0]
    for place, ref in enumerate((cx_ref, cy_ref, rs_ref)):
        out_ref[place * levels : (place + 1) * levels] = ref[...]


def pack_kernel(parts, rs_ref, rm_ref, mv_ref, out_ref):
    levels, rows, columns = rs_ref.shape
    per_level = parts // levels
    width = columns // per_level
    for part in range(parts):
        level, piece = part // per_level, part % per_level
        cols = slice(piece * width, (piece + 1) * width)
        for place, ref in enumerate((rs_ref, rm_ref, mv_ref)):
            out_ref[part, rows * place : rows * (place + 1), :] = ref[level, :, cols]


def scan_kernel(in_ref, *rest):
    out_ref = rest[-1]
    steps = in_ref.shape[0]
    rows = in_ref.shape[1] // 3
    later = jnp.zeros((rows, in_ref.shape[2]), jnp.float32)
    for t in reversed(range(steps)):
        out_ref[t, rows : 2 * rows, :] = later
        later = later + in_ref[t, 0:rows, :]
        out_ref[t, 0:rows, :] = (
            in_ref[t, rows : 2 * rows, :] - in_ref[t, 2 * rows : 3 * rows, :] * later
        )
    total = jnp.zeros((rows, in_ref.shape[2]), jnp.float32)
    for t in range(steps):
        total = total + out_ref[t, 0:rows, :]
        out_ref[t, 0:rows, :] = total


def collect_kernel(at_ref, *refs):
    out_ref = refs[-1]
    here = at_ref[0]
    rows = refs[0].shape[0]
    for place, ref in enumerate(refs[:-1]):
        for i in range(rows):
            at = lax.bitwise_xor(jnp.int32(place * rows + i), here)
            out_ref[pl.ds(at, 1), :] = ref[i : i + 1, :]


def edge_kernel(levels, back_ref, bundle_ref, up_ref, down_ref, rows_s):
    parts, both, width = back_ref.shape
    rows = both // 2
    per_level = parts // levels
    for part in range(parts):
        level, piece = part // per_level, part % per_level
        cols = slice(piece * width, (piece + 1) * width)
        for place, row in enumerate((rows - 1, 0, rows - 2, 1)):
            for field in range(2):
                at = 16 * field + 4 * place + level
                row_at = rows * field + row
                rows_s[at : at + 1, cols] = back_ref[part, row_at : row_at + 1, :]
    incr, incr_in, dual, dual_in = (rows_s[8 * i : 8 * i + 8, :] for i in range(4))
    cx, cy, cy_in, middle = (bundle_ref[2 * levels + i] for i in range(4))
    own, west, east, south, north = weights_of(cx, cy)
    is_up = lax.broadcasted_iota(jnp.int32, cx.shape, 0) < 4
    inner, outer = jnp.where(is_up, south, north), jnp.where(is_up, north, south)
    one = own * incr + west * west_of(incr) + east * east_of(incr) + inner * incr_in
    from_in = jnp.maximum(jnp.where(is_up, -cy_in, cy_in), 0.0) * dual_in
    kept = middle - (own * dual + east_of(west * dual) + west_of(east * dual) + from_in)
    for place, value in enumerate((incr, one, outer, outer * kept, outer * dual)):
        up_ref[4 * place : 4 * place + 4, :] = value[0:4]
        down_ref[4 * place : 4 * place + 4, :] = value[4:8]


def slots_held(rank_ref, k, half, first):
    slot = lax.broadcasted_iota(jnp.int32, (SLOTS, BLOCK), 0) + first
    row = rank_ref[pl.ds(k, 1), half * BLOCK : (half + 1) * BLOCK]
    return jnp.broadcast_to(row, (SLOTS, BLOCK)) == slot


def build_slots(rank_ref, code_ref, first, codes_ref, groups_ref):
    eye = (lax.broadcasted_iota(jnp.int32, (LANES, LANES), 0)
           == lax.broadcasted_iota(jnp.int32, (LANES, LANES), 1))

    def one_chunk(k, carry):
        parts = []
        for half in range(CHUNK // BLOCK):
            held = slots_held(rank_ref, k, half, first)
            row = (code_ref[pl.ds(k, 1), half * BLOCK : (half + 1) * BLOCK] + 1).astype(jnp.float32)
            code = jnp.sum(
                jnp.where(held, jnp.broadcast_to(row, (SLOTS, BLOCK)), 0.0), axis=1, keepdims=True
            )
            parts.append(jnp.broadcast_to(code, (SLOTS, LANES)))
        codes = jnp.concatenate(parts, axis=0) - 1.0
        codes_ref[pl.ds(pl.multiple_of(k * LANES, LANES), LANES), :] = codes
        groups_ref[pl.ds(k, 1), :] = jnp.sum(
            jnp.where(eye, codes.astype(jnp.int32) >> 8, 0), axis=0, keepdims=True
        )
        return carry

    lax.fori_loop(0, rank_ref.shape[0], one_chunk, 0, unroll=4)


def sections(chunks):
    tall = CHUNK // LANES
    sizes = dict(
        codes=chunks * LANES, rank=chunks * tall, code=chunks * tall, groups=chunks,
        square=8,
    )
    places, at = {}, 0
    for name, size in sizes.items():
        places[name] = at
        at += size
    return places, at


def fold(table_ref, first, lines):
    tall = lines.shape[1] // LANES
    for i in range(lines.shape[0] // 8):
        for j in range(tall):
            at = first + (i * tall + j) * 8
            table_ref[at : at + 8, :] = lines[8 * i : 8 * i + 8, j * LANES : (j + 1) * LANES]


def unfold(table_ref, first, count):
    tall = CHUNK // LANES
    return jnp.concatenate([
        jnp.concatenate(
            [table_ref[first + (i * tall + j) * 8 : first + (i * tall + j) * 8 + 8, :] for j in range(tall)],
            axis=1,
        )
        for i in range(count // 8)
    ], axis=0)


def place_kernel(columns, at_ref, brick_ref, cell_ref, step_ref, rm_ref,
                 table_ref, passes_ref, brick_s, cell_s, step_s, groups_s):
    chunks = brick_s.shape[0]
    rank_ref, code_ref = brick_s, cell_s
    places, _ = sections(chunks)
    here = at_ref[0]
    lane_groups = columns // LANES
    for k in range(chunks):
        cols = slice(k * CHUNK, (k + 1) * CHUNK)
        brick_s[k : k + 1, :] = brick_ref[0:1, cols]
        cell_s[k : k + 1, :] = cell_ref[0:1, cols]
        step_s[k : k + 1, :] = step_ref[0:1, cols]
    brick, cell, step = brick_s[...], cell_s[...], step_s[...]
    line = ((cell >> 10) * 171) >> 9
    level, row = line >> 3, line & 7
    column = cell - line * columns
    group, lane = column >> 7, column & 127
    code_ref[...] = ((level * lane_groups + group) * 8 + row) * 256 + step * LANES + lane
    inside = brick == here
    count = inside.astype(jnp.int32)
    lanes = lax.broadcasted_iota(jnp.int32, count.shape, 1) & (BLOCK - 1)
    shift = 1
    while shift < BLOCK:
        count = count + jnp.where(lanes >= shift, pltpu.roll(count, shift, 1), 0)
        shift *= 2
    rank_ref[...] = jnp.where(inside, count - 1, -1)
    build_slots(rank_ref, code_ref, 0, table_ref, groups_s)
    fold(table_ref, places["rank"], rank_ref[...].astype(jnp.float32))
    fold(table_ref, places["code"], code_ref[...].astype(jnp.float32))
    table_ref[places["groups"] : places["groups"] + chunks, :] = groups_s[...].astype(jnp.float32)
    passes_ref[0] = (jnp.max(count.astype(jnp.float32)).astype(jnp.int32) + SLOTS - 1) // SLOTS
    square = jnp.zeros(rm_ref.shape[1:], jnp.float32)
    for level in range(rm_ref.shape[0]):
        square += rm_ref[level] * rm_ref[level]
    table_ref[places["square"] : places["square"] + 8, :] = jnp.broadcast_to(
        jnp.sum(square), (8, LANES)
    )


def in_column(codes, values, which):
    codes = codes.astype(jnp.int32)
    lane = lax.broadcasted_iota(jnp.int32, codes.shape, 1) + which * LANES
    return jnp.where((codes & 255) == lane, values, 0.0)


def split_two(x):
    high = x.astype(jnp.bfloat16)
    low = (x - high.astype(jnp.float32)).astype(jnp.bfloat16)
    return high, low


def spread_kernel(passes_ref, table_ref, lines_ref, cx_ref, cy_ref, bundle_ref,
                  rank_ref, code_ref, again_codes, groups_ref, hot_s, high_s, low_s, total):
    chunks = rank_ref.shape[0]
    places, _ = sections(chunks)
    rank_ref[...] = unfold(table_ref, places["rank"], chunks).astype(jnp.int32)
    groups_ref[...] = table_ref[places["groups"] : places["groups"] + chunks, :].astype(jnp.int32)
    levels, rows, columns = cx_ref.shape
    lane_groups = columns // LANES
    groups = total.shape[0]
    for k in range(chunks // 8):
        bundle_ref[3 * levels, :, k * CHUNK : (k + 1) * CHUNK] = lines_ref[8 * k : 8 * k + 8, 0:CHUNK]
    rows_ref = bundle_ref.at[2 * levels : 3 * levels]
    for level in range(levels):
        for place, row in enumerate((rows - 1, 0)):
            at = 4 * place + level
            rows_ref[0, at : at + 1, :] = cx_ref[level, row : row + 1, :]
            rows_ref[1, at : at + 1, :] = cy_ref[level, row : row + 1, :]
            inner = row - 1 if place == 0 else row + 1
            rows_ref[2, at : at + 1, :] = cy_ref[level, inner : inner + 1, :]
    group_id = lax.broadcasted_iota(jnp.int32, (groups, LANES), 0)

    def add_up(first, codes_ref):
        def one_chunk(k, carry):
            at = pl.ds(pl.multiple_of(k * LANES, LANES), LANES)
            parts = []
            for half in range(CHUNK // BLOCK):
                held = slots_held(rank_ref, k, half, first)
                row = lines_ref[pl.ds(k, 1), CHUNK + half * BLOCK : CHUNK + (half + 1) * BLOCK]
                dual = jnp.sum(
                    jnp.where(held, jnp.broadcast_to(row, (SLOTS, BLOCK)), 0.0),
                    axis=1, keepdims=True,
                )
                parts.append(jnp.broadcast_to(dual, (SLOTS, LANES)))
            dual = jnp.concatenate(parts, axis=0)
            codes = codes_ref[at, :]
            for which in range(2):
                high, low = split_two(in_column(codes, dual, which))
                high_s[at, which * LANES : (which + 1) * LANES] = high
                low_s[at, which * LANES : (which + 1) * LANES] = low
            row = jnp.broadcast_to(groups_ref[pl.ds(k, 1), :], (groups, LANES))
            hot_s[:, at] = (row == group_id).astype(jnp.float32).astype(jnp.bfloat16)
            return carry

        lax.fori_loop(0, chunks, one_chunk, 0, unroll=4)
        return jnp.dot(
            hot_s[...], high_s[...], preferred_element_type=jnp.float32
        ) + jnp.dot(hot_s[...], low_s[...], preferred_element_type=jnp.float32)

    total[...] = add_up(0, table_ref)

    def one_more(number, carry):
        code_ref[...] = unfold(table_ref, places["code"], chunks).astype(jnp.int32)
        build_slots(rank_ref, code_ref, number * SLOTS, again_codes, groups_ref)
        total[...] += add_up(number * SLOTS, again_codes)
        return carry

    lax.fori_loop(1, passes_ref[0], one_more, 0)

    for g in range(lane_groups):
        cols = slice(g * LANES, (g + 1) * LANES)
        for level in range(levels):
            at = (level * lane_groups + g) * 8
            bundle_ref[level, :, cols] = total[at : at + 8, 0:LANES]
            bundle_ref[levels + level, :, cols] = total[at : at + 8, LANES : 2 * LANES]
    for level in range(levels):
        for place, row in enumerate((rows - 1, 0)):
            at = 4 * place + level
            rows_ref[3, at : at + 1, :] = bundle_ref[levels + level, row : row + 1, :]


def west_of(v):
    return pltpu.roll(v, 1, 1)


def east_of(v):
    return pltpu.roll(v, v.shape[1] - 1, 1)


def weights_of(cx, cy):
    west, east = jnp.maximum(cx, 0.0), jnp.maximum(-cx, 0.0)
    south, north = jnp.maximum(cy, 0.0), jnp.maximum(-cy, 0.0)
    return 1.0 - jnp.abs(cx) - jnp.abs(cy), west, east, south, north


def forward(v, below, above, coeffs):
    own, west, east, south, north = coeffs
    return own * v + west * west_of(v) + east * east_of(v) + south * below + north * above


def adjoint(v, from_above, from_below, coeffs):
    own, west, east, _, _ = coeffs
    return own * v + east_of(west * v) + west_of(east * v) + from_above + from_below


def row_below(v, edge, first):
    return jnp.where(first, jnp.broadcast_to(edge, v.shape), pltpu.roll(v, 1, 0))


def row_above(v, edge, last):
    return jnp.where(last, jnp.broadcast_to(edge, v.shape), pltpu.roll(v, v.shape[0] - 1, 0))


def image_kernel(windows, window_ref, passes_ref, back_ref, below_ref, above_ref, args_ref,
                 bundle_ref, rm_next_ref, table_ref, next_ref, state_ref, sent_ref,
                 fields, rank_ref, code_ref, again_codes, again_groups, hot_s, found):
    levels, rows, columns = rm_next_ref.shape
    parts, _, width = back_ref.shape
    per_level = parts // levels
    chunks = found.shape[0]
    places, _ = sections(chunks)
    rank_ref[...] = unfold(table_ref, places["rank"], chunks).astype(jnp.int32)
    lane_groups = columns // LANES
    window = window_ref[0]

    row_id = lax.broadcasted_iota(jnp.int32, (rows, columns), 0)
    first, last = row_id == 0, row_id == rows - 1
    projected = jnp.zeros((rows, columns), jnp.float32)
    curvature = jnp.zeros((rows, columns), jnp.float32)
    has_next = jnp.where(window < windows - 1, 1.0, 0.0)
    for level in range(levels):
        pieces = range(level * per_level, (level + 1) * per_level)
        incr = jnp.concatenate([back_ref[p, 0:rows, :] for p in pieces], axis=1)
        next_dual = jnp.concatenate([back_ref[p, rows : 2 * rows, :] for p in pieces], axis=1)
        coeffs = weights_of(args_ref[level], args_ref[levels + level])
        south, north = coeffs[3], coeffs[4]
        low, high = (
            [ref[4 * i + level : 4 * i + level + 1, :] for i in range(5)] for ref in (below_ref, above_ref)
        )
        after_one = forward(
            incr,
            row_below(incr, low[0], first),
            row_above(incr, high[0], last),
            coeffs,
        )
        after_two = forward(
            after_one,
            row_below(after_one, low[1] + low[2] * incr[0:1], first),
            row_above(after_one, high[1] + high[2] * incr[rows - 1 :], last),
            coeffs,
        )
        rm_next = rm_next_ref[level]
        image_next = (rm_next + incr - after_two) * has_next
        next_ref[level] = image_next
        south_dual, north_dual = south * next_dual, north * next_dual
        back_one = adjoint(
            next_dual,
            row_above(south_dual, high[4], last),
            row_below(north_dual, low[4], first),
            coeffs,
        )
        kept = bundle_ref[levels + level] - back_one
        rs = args_ref[2 * levels + level]
        image_state = (next_dual + rs) + bundle_ref[level] + adjoint(
            kept,
            row_above(south * kept, high[3] - high[2] * north_dual[rows - 1 :], last),
            row_below(north * kept, low[3] - low[2] * south_dual[0:1], first),
            coeffs,
        )
        state_ref[level] = image_state
        projected += rm_next * image_next + rs * image_state
        curvature += image_next * image_next + image_state * image_state
        for g in range(lane_groups):
            at = (level * lane_groups + g) * 8
            cols = slice(g * LANES, (g + 1) * LANES)
            fields[at : at + 8, 0:LANES] = incr[:, cols]
            fields[at : at + 8, LANES : 2 * LANES] = after_one[:, cols]

    high_fields, low_fields = split_two(fields[...])
    groups = levels * lane_groups * 8
    together = hot_s.shape[0] // LANES
    group_id = lax.broadcasted_iota(jnp.int32, (LANES, groups), 1)

    def look_up(first, fresh, codes_ref):
        def some_chunks(q, carry):
            codes = []
            for j in range(together):
                k = q * together + j
                code = codes_ref[pl.ds(pl.multiple_of(k * LANES, LANES), LANES), :]
                wide = jnp.concatenate([code.astype(jnp.int32) >> 8] * (groups // LANES), axis=1)
                hot_s[j * LANES : (j + 1) * LANES, :] = (
                    (wide == group_id).astype(jnp.float32).astype(jnp.bfloat16)
                )
                codes.append(code)
            picks = hot_s[...]
            picked = jnp.dot(
                picks, high_fields, preferred_element_type=jnp.float32
            ) + jnp.dot(picks, low_fields, preferred_element_type=jnp.float32)
            for j in range(together):
                k = q * together + j
                at = slice(j * LANES, (j + 1) * LANES)
                value = jnp.sum(
                    in_column(codes[j], picked[at, 0:LANES], 0)
                    + in_column(codes[j], picked[at, LANES : 2 * LANES], 1),
                    axis=1, keepdims=True,
                )
                for half in range(CHUNK // BLOCK):
                    held = slots_held(rank_ref, k, half, first)
                    part = value[half * SLOTS : (half + 1) * SLOTS]
                    line = jnp.sum(
                        jnp.where(held, jnp.broadcast_to(part, (SLOTS, BLOCK)), 0.0),
                        axis=0, keepdims=True,
                    )
                    lanes = slice(half * BLOCK, (half + 1) * BLOCK)
                    if fresh:
                        found[pl.ds(k, 1), lanes] = line
                    else:
                        found[pl.ds(k, 1), lanes] += line
            return carry

        lax.fori_loop(0, chunks // together, some_chunks, 0, unroll=fresh)

    look_up(0, True, table_ref)

    def one_more(number, carry):
        code_ref[...] = unfold(table_ref, places["code"], chunks).astype(jnp.int32)
        build_slots(rank_ref, code_ref, number * SLOTS, again_codes, again_groups)
        look_up(number * SLOTS, False, again_codes)
        return carry

    lax.fori_loop(1, passes_ref[0], one_more, 0)

    observed = found[...]
    resid = jnp.concatenate(
        [bundle_ref[3 * levels, :, k * CHUNK : (k + 1) * CHUNK] for k in range(chunks // 8)], axis=0
    )
    image_obs = jnp.where(rank_ref[...] >= 0, resid + observed, 0.0)
    square = jnp.where(window == 0, table_ref[places["square"] : places["square"] + 1, :], 0.0)
    all_projected = jnp.sum(projected) + jnp.sum(resid * image_obs) + square
    all_curvature = jnp.sum(curvature) + jnp.sum(image_obs * image_obs) + square
    lane = lax.broadcasted_iota(jnp.int32, (1, LANES), 1)
    sums = jnp.where(lane == 0, all_projected, jnp.where(lane == 1, all_curvature, 0.0))
    for k in range(chunks):
        sent_ref[k, :, 0:CHUNK] = found[k : k + 1, :]
        sent_ref[k, :, CHUNK : CHUNK + LANES] = sums


def gather_kernel(got_ref, observed_ref, sums_ref):
    total = got_ref[0]
    for k in range(1, got_ref.shape[0]):
        total = total + got_ref[k]
    observed_ref[...] = total[:, 0:CHUNK]
    for k in range(sums_ref.shape[0]):
        sums_ref[k] = total[:, CHUNK : CHUNK + LANES]


def update_kernel(window_ref, sums_ref, ds_ref, inc_ref, rm_ref, rs_ref, back_ref, image_ref, state_ref,
                  do_ref, ro_ref, ov_ref, observed_ref,
                  ds_out, do_out, inc_out, rm_out, ro_out, rs_out, ds_s, inc_s, rm_s, rs_s, sems):
    sums = sums_ref[0]
    for k in range(1, sums_ref.shape[0]):
        sums = sums + sums_ref[k]
    lane = lax.broadcasted_iota(jnp.int32, sums.shape, 1)
    projected = jnp.sum(jnp.where(lane == 0, sums, 0.0), axis=1, keepdims=True)
    curvature = jnp.sum(jnp.where(lane == 1, sums, 0.0), axis=1, keepdims=True)
    step = projected / curvature
    levels, rows, columns = rs_ref.shape
    parts, _, width = back_ref.shape
    per_level = parts // levels
    wide = jnp.broadcast_to(step, (rows, width))
    starts = window_ref[0] == 0
    copies = []
    for level in range(levels):
        for piece in range(per_level):
            part = level * per_level + piece
            cols = slice(piece * width, (piece + 1) * width)
            rs, rm = rs_ref[level, :, cols], rm_ref[level, :, cols]
            dual = back_ref[part, rows : 2 * rows, :] + rs
            ds_s[level, :, cols] = ds_ref[level, :, cols] + wide * dual
            inc_s[level, :, cols] = inc_ref[level, :, cols] + wide * back_ref[part, 0:rows, :]
            image = jnp.where(starts, rm, image_ref[level, :, cols])
            rm_s[level, :, cols] = rm - wide * image
            rs_s[level, :, cols] = rs - wide * state_ref[level, :, cols]
        pairs = ((ds_s, ds_out), (inc_s, inc_out), (rm_s, rm_out), (rs_s, rs_out))
        for place, (held, out) in enumerate(pairs):
            copies.append(pltpu.make_async_copy(held.at[level], out.at[level], sems.at[level, place]))
            copies[-1].start()
    narrow = jnp.broadcast_to(step, ro_ref.shape)
    ro, ov = ro_ref[...], ov_ref[...]
    dual = ro / ov
    do_out[...] = do_ref[...] + narrow * dual
    ro_out[...] = ro - narrow * (ov * dual + observed_ref[...])
    for copy in copies:
        copy.wait()


def body(windows, bricks, courant_x, courant_y, model_var, obs_var, obs_brick, obs_cell, obs_step,
         dual_state, dual_obs, increment, resid_model, resid_obs, resid_state):
    cx, cy, mv = courant_x[0], courant_y[0], model_var[0]
    ds, inc, rm, rs = dual_state[0], increment[0], resid_model[0], resid_state[0]
    levels, rows, columns = rs.shape
    per_level = windows // levels
    width = columns // per_level
    blocks = bricks
    groups = levels * (columns // LANES) * 8
    field_bytes = 4 * levels * rows * columns
    here = lax.axis_index("space").astype(jnp.int32)
    window = lax.axis_index("tm").astype(jnp.int32)
    at, window_at = here[None], window[None]

    upward = [(i, i + 1) for i in range(bricks - 1)]
    downward = [(i + 1, i) for i in range(bricks - 1)]

    packed = pl.pallas_call(
        functools.partial(pack_kernel, windows),
        out_shape=f32(windows, 3 * rows, width),
        in_specs=[VMEM] * 3,
        out_specs=VMEM,
        compiler_params=params(60),
        cost_estimate=cost(1, 1),
        name="pack",
    )(rs, rm, mv)
    windows_of = lax.all_to_all(packed, "tm", 0, 0)

    rm_next = lax.ppermute(rm, "tm", [(i + 1, i) for i in range(windows - 1)])
    near = pl.pallas_call(
        duals_kernel,
        out_shape=f32(1, 2 * CHUNK),
        in_specs=[VMEM] * 2,
        out_specs=VMEM,
        compiler_params=params(2),
        cost_estimate=cost(1, 1),
        name="duals",
    )(resid_obs, obs_var)
    distance = 1
    while 4 * distance < bricks:
        others = [
            lax.ppermute(near, "space", [(i, i ^ (distance * k)) for i in range(bricks)]) for k in (1, 2, 3)
        ]
        near = pl.pallas_call(
            join_kernel,
            out_shape=f32(4 * distance, 2 * CHUNK),
            in_specs=[VMEM] * 4,
            out_specs=VMEM,
            compiler_params=params(2),
            cost_estimate=cost(1, 1),
            name="join",
        )(near, *others)
        distance *= 4
    far = [
        lax.ppermute(near, "space", [(i, i ^ (distance * k)) for i in range(bricks)])
        for k in range(1, bricks // distance)
    ]
    slots = blocks * LANES
    field_s = pltpu.VMEM((levels, rows, columns), jnp.float32)
    table_s = pltpu.VMEM((blocks, CHUNK), jnp.int32)
    line_s = pltpu.VMEM((blocks, CHUNK), jnp.float32)
    codes_s = pltpu.VMEM((slots, LANES), jnp.float32)
    groups_s = pltpu.VMEM((blocks, LANES), jnp.int32)
    table, passes = pl.pallas_call(
        functools.partial(place_kernel, columns),
        out_shape=(f32(sections(blocks)[1], LANES), i32(1)),
        in_specs=[SMEM] + [VMEM] * 4,
        out_specs=(VMEM, SMEM),
        scratch_shapes=[table_s, table_s, table_s, groups_s],
        compiler_params=params(8),
        cost_estimate=cost(1, 1),
        name="places",
    )(at, obs_brick, obs_cell, obs_step, rm)
    lines = pl.pallas_call(
        collect_kernel,
        out_shape=f32(blocks, 2 * CHUNK),
        in_specs=[SMEM] + [VMEM] * (1 + len(far)),
        out_specs=VMEM,
        compiler_params=params(2),
        cost_estimate=cost(1, 1),
        name="collect",
    )(at, near, *far)
    bundle = pl.pallas_call(
        spread_kernel,
        out_shape=f32(3 * levels + 1, rows, columns),
        in_specs=[SMEM] + [VMEM] * 4,
        out_specs=VMEM,
        scratch_shapes=[
            table_s, table_s, codes_s, groups_s,
            pltpu.VMEM((groups, slots), jnp.bfloat16),
            pltpu.VMEM((slots, 2 * LANES), jnp.bfloat16),
            pltpu.VMEM((slots, 2 * LANES), jnp.bfloat16),
            pltpu.VMEM((groups, 2 * LANES), jnp.float32),
        ],
        compiler_params=params(24),
        cost_estimate=cost(1, 1),
        name="spread",
    )(passes, table, lines, cx, cy)

    summed = pl.pallas_call(
        scan_kernel,
        out_shape=f32(windows, 2 * rows, width),
        in_specs=[VMEM, ANY, ANY],
        out_specs=VMEM,
        compiler_params=params(4),
        cost_estimate=cost(1, 1),
        name="scan",
    )(windows_of, table, lines)
    back = lax.all_to_all(summed, "tm", 0, 0)
    up, down = pl.pallas_call(
        functools.partial(edge_kernel, levels),
        out_shape=(f32(24, columns), f32(24, columns)),
        in_specs=[VMEM, VMEM],
        out_specs=(VMEM, VMEM),
        scratch_shapes=[pltpu.VMEM((32, columns), jnp.float32)],
        compiler_params=params(6),
        cost_estimate=cost(1, 1),
        name="edges",
    )(back, bundle)
    below = lax.ppermute(up, "space", upward)
    above = lax.ppermute(down, "space", downward)

    fields = pl.pallas_call(
        gather_fields_kernel,
        out_shape=f32(3 * levels, rows, columns),
        in_specs=[VMEM] * 3 + [ANY],
        out_specs=VMEM,
        compiler_params=params(6),
        cost_estimate=cost(1, 1),
        name="fields",
    )(cx, cy, rs, up)

    image_next, image_state, sent = pl.pallas_call(
        functools.partial(image_kernel, windows),
        out_shape=(
            f32(levels, rows, columns), f32(levels, rows, columns), f32(blocks, 1, CHUNK + LANES),
        ),
        in_specs=[SMEM, SMEM] + [VMEM] * 7,
        out_specs=(VMEM, VMEM, VMEM),
        scratch_shapes=[
            pltpu.VMEM((groups, 2 * LANES), jnp.float32),
            table_s, table_s, codes_s, groups_s,
            pltpu.VMEM((min(4, blocks) * LANES, groups), jnp.bfloat16),
            line_s,
        ],
        compiler_params=params(24),
        cost_estimate=cost(1, 1),
        name="images",
    )(window_at, passes, back, below, above, fields, bundle, rm_next, table)

    image_model = lax.ppermute(image_next, "tm", [(i, i + 1) for i in range(windows - 1)])
    got = lax.all_to_all(sent, "space", 0, 0)
    observed, sums = pl.pallas_call(
        gather_kernel,
        out_shape=(f32(1, CHUNK), f32(windows, 1, LANES)),
        in_specs=[VMEM],
        out_specs=(VMEM, VMEM),
        compiler_params=params(4),
        cost_estimate=cost(1, 1),
        name="first_sums",
    )(got)
    all_sums = lax.all_to_all(sums, "tm", 0, 0)

    count = resid_obs.shape[1]
    new_ds, new_do, new_inc, new_rm, new_ro, new_rs = pl.pallas_call(
        update_kernel,
        out_shape=(
            f32(levels, rows, columns), f32(1, count), f32(levels, rows, columns),
            f32(levels, rows, columns), f32(1, count), f32(levels, rows, columns),
        ),
        in_specs=[SMEM] + [VMEM] * 12,
        out_specs=(HBM, VMEM, HBM, HBM, VMEM, HBM),
        scratch_shapes=[field_s] * 4 + [pltpu.SemaphoreType.DMA((levels, 4))],
        compiler_params=params(8),
        cost_estimate=cost(1, 1),
        name="updates",
    )(window_at, all_sums, ds, inc, rm, rs, back, image_model, image_state,
      dual_obs, resid_obs, obs_var, observed)
    return new_ds[None], new_do, new_inc[None], new_rm[None], new_ro, new_rs[None]


def solution(mesh):
    field = P("tm", None, "space", None)
    obs = P("tm", "space")
    shared = P("tm", None)
    return jax.shard_map(
        functools.partial(body, mesh.shape["tm"], mesh.shape["space"]),
        mesh=mesh,
        in_specs=(
            field, field, field, obs, shared, shared, shared,
            field, obs, field, field, obs, field,
        ),
        out_specs=(field, obs, field, field, obs, field),
        check_vma=False,
    )
```

time: 115 us -> 103 us (0.90)
  Pallas kernels: 30.7 us -> 22.4 us
  starting transfers between devices: 37.7 us -> 35.5 us
  waiting for transfers between devices: 10 us -> 8.69 us
    pallas_call x3 -> x7, Pallas kernels: 24.5 us -> 14.9 us  [the longest x1 6.23 us: body(): pl.pallas_call(functools.partial(image_kernel, windows), out_shape=(f32(l...]
    ppermute x1, waiting for transfers between devices: 4.39 us -> 0.01 us  [body(): above = lax.ppermute(down, 'space', downward)]
    ppermute x1, starting transfers between devices: 6.17 us -> 2.2 us  [body(): below = lax.ppermute(up, 'space', upward)]
    all_to_all x1, waiting for transfers between devices: 0.01 us -> 3.75 us  [body(): back = lax.all_to_all(summed, 'tm', 0, 0)]
    ppermute x1, starting transfers between devices: 1.92 us -> 4.66 us  [body(): above = lax.ppermute(down, 'space', downward)]
    all_to_all x1, waiting for transfers between devices: 1.85 us -> 0.01 us  [body(): windows_of = lax.all_to_all(packed, 'tm', 0, 0)]
    all_to_all x1, starting transfers between devices: 5.25 us -> 6.86 us  [body(): back = lax.all_to_all(summed, 'tm', 0, 0)]
    ppermute x4 -> x6, starting transfers between devices: 11.9 us -> 10.4 us  [body(): lax.ppermute(near, 'space', [(i, i ^ distance * k) for i in range(bricks)])]
  transfers between devices with their start and end apart: 10 -> 12, of which waited for: 6 -> 5; matrix products, arithmetic and copies ran while one was open for 1% -> 0% of each run, Pallas kernels for 13% -> 10%
where the time goes in v3:
time: 103 us; the launch traced here: 102 us
  starting transfers between devices  35.5 us (34%)
  blocking collectives  29.5 us (29%)
  Pallas kernels  22.4 us (22%)
  waiting for transfers between devices  8.69 us (8%)
  local copies, waits for them, and re-layouts  5.01 us (5%)
    all_to_all x1, blocking collectives, body(): got = lax.all_to_all(sent, 'space', 0, 0)  16.4 us
    all_to_all x1, blocking collectives, body(): all_sums = lax.all_to_all(sums, 'tm', 0, 0)  13.1 us
    ppermute x6, starting transfers between devices, body(): lax.ppermute(near, 'space', [(i, i ^ distance * k) for i in range(bricks)])  10.4 us
    all_to_all x1, starting transfers between devices, body(): windows_of = lax.all_to_all(packed, 'tm', 0, 0)  7.73 us
    all_to_all x1, starting transfers between devices, body(): back = lax.all_to_all(summed, 'tm', 0, 0)  6.86 us
    pallas_call x1, Pallas kernels, body(): pl.pallas_call(functools.partial(image_kernel, windows), out_shape=(f32(l...  6.23 us
    pallas_call x1, Pallas kernels, body(): pl.pallas_call(spread_kernel, out_shape=f32(3 * levels + 1, rows, columns...  5.44 us
    unnamed x30, local copies, waits for them, and re-layouts  5.01 us
  transfers between devices with their start and end apart: 12, of which 5 were waited for; matrix products, arithmetic and copies ran while one was open for 0% of the time, Pallas kernels for 10%

profile of v3, /device:TPU:1, one launch (start us, length us, event | category | flops | bytes accessed | tf_op | source)
XLA Modules:
  0.0 102.2 jit_solution(10475404788503162248)
XLA Ops:
  0.6 2.3 %pack.1 = f32[16,24,768]{2,1,0:T(8,128)} custom-call(f32[4,8,3072]{2,1,0:T(8,128)} %bitcast.13, f32[4,8,3072]{2,1,0:T(8,128)} %bitcast.2.rm_ref, f32[4,8,3072]{2,1,0:T(8,128)} %bitcast.22), custom_call_target="tpu_custom_call" | custom-call | flops 1 | bytes 1 | tf_op jit(solution)/shard_map/pack/pallas_call | solution.py:539
  3.0 0.0 copy-start.11
  3.0 0.0 copy-start.12
  3.0 0.0 copy-start.8
  3.0 0.0 copy-start.9
  3.0 0.0 copy-start.10
  3.0 7.7 %all-to-all-start = ((f32[16,24,768]{2,1,0:T(8,128)}), f32[16,24,768]{2,1,0:T(8,128)S(1)}, u32[]{:S(2)}, u32[]{:S(2)}) async-start(f32[16,24,768]{2,1,0:T(8,128)} %pack.1), calls=%async_computation | async-start | bytes 2359296 | tf_op jit(solution)/shard_map/all_to_all | solution.py:548
  10.7 0.0 copy-done.11
  10.7 0.0 copy-done.12
  10.8 2.6 %collective-permute-start.2 = (f32[1,2048]{1,0:T(1,128)S(1)}, f32[1,2048]{1,0:T(1,128)S(1)}, u32[]{:S(2)}, u32[]{:S(2)}) collective-permute-start(f32[1,2048]{1,0:T(1,128)S(1)} %duals.1.refs_0_), channel_id=1, source_target_pairs={{0,3},{1,2},{2,1},{3,0},{4,7},{5,6},{6,5},{7,4},{8,11},{9,10},{10,... | collective-permute-start | bytes 24584 | tf_op jit(solution)/shard_map/ppermute | solution.py:563
  13.3 0.0 collective-permute-start.1
  13.3 0.5 collective-permute-start
  13.8 0.8 collective-permute-done.2.refs_3_
  14.7 1.5 %collective-permute-done.1.refs_2_ = f32[1,2048]{1,0:T(1,128)S(1)} collective-permute-done((f32[1,2048]{1,0:T(1,128)S(1)}, f32[1,2048]{1,0:T(1,128)S(1)}, u32[]{:S(2)}, u32[]{:S(2)}) %collective-permute-start.1) | collective-permute-done | bytes 8224 | tf_op jit(solution)/shard_map/ppermute | solution.py:563
  16.2 0.0 collective-permute-done.refs_1_
  16.2 5.1 %collective-permute-start.5 = (f32[4,2048]{1,0:T(4,128)S(1)}, f32[4,2048]{1,0:T(4,128)S(1)}, u32[]{:S(2)}, u32[]{:S(2)}) collective-permute-start(f32[4,2048]{1,0:T(4,128)S(1)} %join.1.refs_0_), channel_id=1, source_target_pairs={{0,12},{1,13},{2,14},{3,15},{4,8},{5,9},{6,10},{7,11},{8,4},{9,5},... | collective-permute-start | bytes 98312 | tf_op jit(solution)/shard_map/ppermute | solution.py:576
  21.3 1.2 %collective-permute-start.4 = (f32[4,2048]{1,0:T(4,128)S(1)}, f32[4,2048]{1,0:T(4,128)S(1)}, u32[]{:S(2)}, u32[]{:S(2)}) collective-permute-start(f32[4,2048]{1,0:T(4,128)S(1)} %join.1.refs_0_), channel_id=1, source_target_pairs={{0,8},{1,9},{2,10},{3,11},{4,12},{5,13},{6,14},{7,15},{8,0},{9,1},... | collective-permute-start | bytes 98312 | tf_op jit(solution)/shard_map/ppermute | solution.py:576
  22.5 1.0 collective-permute-start.3
  23.5 0.0 copy-done.8
  23.5 0.0 copy-done.9
  23.5 0.0 copy-done.10
  23.5 3.2 %places.1 = (f32[2328,128]{1,0:T(8,128)S(1)}, s32[1]{0:T(128)}) custom-call(s32[1]{0:T(128)} %bitcast.1.at_ref, s32[1,16384]{1,0:T(1,128)S(1)} %copy-done.8, s32[1,16384]{1,0:T(1,128)S(1)} %copy-done.9, s32[1,16384]{1,0:T(1,128)S(1)} %copy-done.10, f32[4,8,3072]{2,1,0:T(8,128)} %bitcast.2.rm_ref), custom_call_target="tpu_custom_call" | custom-call | flops 1 | bytes 1 | tf_op jit(solution)/shard_map/places/pallas_call | solution.py:585
  26.7 0.0 collective-permute-done.5.refs_3_
  26.7 1.9 %collective-permute-done.4.refs_2_ = f32[4,2048]{1,0:T(4,128)S(1)} collective-permute-done((f32[4,2048]{1,0:T(4,128)S(1)}, f32[4,2048]{1,0:T(4,128)S(1)}, u32[]{:S(2)}, u32[]{:S(2)}) %collective-permute-start.4) | collective-permute-done | bytes 32800 | tf_op jit(solution)/shard_map/ppermute | solution.py:576
  28.6 0.0 collective-permute-done.3.refs_1_
  28.6 0.0 all-to-all-done.in_ref
  28.6 1.0 scan.1
  29.6 6.9 %all-to-all-start.1 = ((f32[16,16,768]{2,1,0:T(8,128)}), f32[16,16,768]{2,1,0:T(8,128)S(1)}, u32[]{:S(2)}, u32[]{:S(2)}) async-start(f32[16,16,768]{2,1,0:T(8,128)} %scan.1), calls=%async_computation.1 | async-start | bytes 1572864 | tf_op jit(solution)/shard_map/all_to_all | solution.py:630
  36.5 1.3 %collective-permute-start.8 = (f32[4,8,3072]{2,1,0:T(8,128)}, f32[4,8,3072]{2,1,0:T(8,128)}, u32[]{:S(2)}, u32[]{:S(2)}) collective-permute-start(f32[4,8,3072]{2,1,0:T(8,128)} %bitcast.2.rm_ref), channel_id=1, source_target_pairs={{16,0},{32,16},{48,32},{64,48},{80,64},{96,80},{112,96},{128,112},... | collective-permute-start | bytes 1179656 | tf_op jit(solution)/shard_map/ppermute | solution.py:550
  37.8 0.0 copy-start.2
  37.8 1.0 copy-done.2
  38.8 0.0 copy-start.4
  38.8 1.0 copy-done.4
  39.8 5.4 %spread.1.bundle_ref = f32[13,8,3072]{2,1,0:T(8,128)S(1)} custom-call(s32[1]{0:T(128)} %get-tuple-element.21.passes_ref, f32[2328,128]{1,0:T(8,128)S(1)} %get-tuple-element.22.rest_0_.table_ref, f32[16,2048]{1,0:T(8,128)S(1)} %collect.1.rest_1_.lines_ref, f32[4,8,3072]{2,1,0:T(8,128)S(1)} %bitcast.16, f32[4,8,3072]{2,1,0:T(8,128)S(1)} %bitcast.18), custom_call_target="tpu_custom_call" | custom-call | flops 1 | bytes 1 | tf_op jit(solution)/shard_map/spread/pallas_call | solution.py:604
  45.2 3.8 %all-to-all-done.1.back_ref = f32[16,16,768]{2,1,0:T(8,128)S(1)} async-done(((f32[16,16,768]{2,1,0:T(8,128)}), f32[16,16,768]{2,1,0:T(8,128)S(1)}, u32[]{:S(2)}, u32[]{:S(2)}) %all-to-all-start.1) | async-done | bytes 786464 | tf_op jit(solution)/shard_map/all_to_all | solution.py:630
  49.0 1.1 %edges.1 = (f32[24,3072]{1,0:T(8,128)}, f32[24,3072]{1,0:T(8,128)}) custom-call(f32[16,16,768]{2,1,0:T(8,128)S(1)} %all-to-all-done.1.back_ref, f32[13,8,3072]{2,1,0:T(8,128)S(1)} %spread.1.bundle_ref), custom_call_target="tpu_custom_call" | custom-call | flops 1 | bytes 1 | tf_op jit(solution)/shard_map/edges/pallas_call | solution.py:631
  50.1 4.7 %collective-permute-start.7 = (f32[24,3072]{1,0:T(8,128)}, f32[24,3072]{1,0:T(8,128)S(1)}, u32[]{:S(2)}, u32[]{:S(2)}) collective-permute-start(f32[24,3072]{1,0:T(8,128)} %get-tuple-element.24), channel_id=1, source_target_pairs={{1,0},{2,1},{3,2},{4,3},{5,4},{6,5},{7,6},{8,7},{9,8},{10,9},{11,1... | collective-permute-start | bytes 884744 | tf_op jit(solution)/shard_map/ppermute | solution.py:642
  54.8 2.2 %collective-permute-start.6 = (f32[24,3072]{1,0:T(8,128)}, f32[24,3072]{1,0:T(8,128)}, u32[]{:S(2)}, u32[]{:S(2)}) collective-permute-start(f32[24,3072]{1,0:T(8,128)} %get-tuple-element.23.after_ref), channel_id=1, source_target_pairs={{0,1},{1,2},{2,3},{3,4},{4,5},{5,6},{6,7},{7,8},{8,9},{9,10},{10,1... | collective-permute-start | bytes 884744 | tf_op jit(solution)/shard_map/ppermute | solution.py:641
  57.0 0.0 copy-start
  57.0 1.0 copy-done
  58.0 0.0 copy-start.3
  58.0 1.0 copy-done.3
  59.0 0.0 copy-start.5
  59.0 1.0 copy-done.5
  60.0 0.1 fields.1.args_ref
  60.0 0.0 collective-permute-done.8.rm_next_ref
  60.1 0.0 collective-permute-done.7.above_ref
  60.1 0.7 collective-permute-done.6.below_ref
  60.7 0.0 copy-start.1
  60.8 0.0 copy-start.6
  60.8 0.0 copy-start.7
  60.8 0.0 copy-start.13
  60.8 0.0 copy-start.14
  60.8 6.2 %images.1 = (f32[4,8,3072]{2,1,0:T(8,128)S(1)}, f32[4,8,3072]{2,1,0:T(8,128)S(1)}, f32[16,1,1152]{2,1,0:T(1,128)S(1)}) custom-call(s32[1]{0:T(128)} %bitcast.window_ref, s32[1]{0:T(128)} %get-tuple-element.21.passes_ref, f32[16,16,768]{2,1,0:T(8,128)S(1)} %all-to-all-done.1.back_ref, f32[24,3072]{1,0:T(8,128)} %collective-permute-done.6.below_ref, ...), custom_call_target="tpu_custom_call" | custom-call | flops 1 | bytes 1 | tf_op jit(solution)/shard_map/images/pallas_call | solution.py:654
  67.0 2.4 %collective-permute-start.9 = (f32[4,8,3072]{2,1,0:T(8,128)S(1)}, f32[4,8,3072]{2,1,0:T(8,128)S(1)}, u32[]{:S(2)}, u32[]{:S(2)}) collective-permute-start(f32[4,8,3072]{2,1,0:T(8,128)S(1)} %get-tuple-element.27), channel_id=1, source_target_pairs={{0,16},{16,32},{32,48},{48,64},{64,80},{80,96},{96,112},{112,128},... | collective-permute-start | bytes 1179656 | tf_op jit(solution)/shard_map/ppermute | solution.py:672
  69.4 16.4 %all_to_all.20.got_ref = f32[16,1,1152]{2,1,0:T(1,128)S(1)} all-to-all(f32[16,1,1152]{2,1,0:T(1,128)S(1)} %get-tuple-element.25), channel_id=1, replica_groups=mesh['tm'=16,'space'=16] {'space'}, dimensions={0} | all-to-all | bytes 147456 | tf_op jit(solution)/shard_map/all_to_all | solution.py:673
  85.9 13.1 %all_to_all.21.sums_ref = f32[16,1,128]{2,1,0:T(1,128)S(1)} all-to-all(f32[16,1,128]{2,1,0:T(1,128)S(1)} %get-tuple-element.26), channel_id=1, replica_groups=mesh['tm'=16,'space'=16] {'tm'}, dimensions={0} | all-to-all | bytes 16384 | tf_op jit(solution)/shard_map/all_to_all | solution.py:683
  99.0 0.0 collective-permute-done.9.image_ref
  99.0 0.0 copy-done.1
  99.0 0.0 copy-done.6
  99.0 0.0 copy-done.7
  99.0 0.0 copy-done.13
  99.0 0.0 copy-done.14
  99.0 3.0 %updates.1 = (f32[4,8,3072]{2,1,0:T(8,128)}, f32[1,1024]{1,0:T(1,128)}, f32[4,8,3072]{2,1,0:T(8,128)}, f32[4,8,3072]{2,1,0:T(8,128)}, f32[1,1024]{1,0:T(1,128)}, /*index=5*/f32[4,8,3072]{2,1,0:T(8,128)}) custom-call(s32[1]{0:T(128)} %bitcast.window_ref, f32[16,1,128]{2,1,0:T(1,128)S(1)} %all_to_all.21.sums_ref, f32[4,8,3072]{2,1,0:T(8,128)S(1)} %bitcast.20, ...), custom_call_target="tpu_custom_call" | custom-call | flops 1 | bytes 1 | tf_op jit(solution)/shard_map/updates/pallas_call | solution.py:686
  (4 shorter events, 0.1 us)
Async XLA Ops:
  3.0 7.8 %copy-start.11 = (f32[1,1024]{1,0:T(1,128)S(1)}, f32[1,1024]{1,0:T(1,128)}, u32[]{:S(2)}) copy-start(f32[1,1024]{1,0:T(1,128)} %ro_ref.3) | copy-start | bytes 12292
  3.0 7.8 %copy-start.12 = (f32[1,1024]{1,0:T(1,128)S(1)}, f32[1,1024]{1,0:T(1,128)}, u32[]{:S(2)}) copy-start(f32[1,1024]{1,0:T(1,128)} %ov_ref.3) | copy-start | bytes 12292
  3.0 20.5 %copy-start.8 = (s32[1,16384]{1,0:T(1,128)S(1)}, s32[1,16384]{1,0:T(1,128)}, u32[]{:S(2)}) copy-start(s32[1,16384]{1,0:T(1,128)} %brick_ref.1) | copy-start | bytes 196612
  3.0 20.5 %copy-start.9 = (s32[1,16384]{1,0:T(1,128)S(1)}, s32[1,16384]{1,0:T(1,128)}, u32[]{:S(2)}) copy-start(s32[1,16384]{1,0:T(1,128)} %cell_ref.1) | copy-start | bytes 196612
  3.0 20.5 %copy-start.10 = (s32[1,16384]{1,0:T(1,128)S(1)}, s32[1,16384]{1,0:T(1,128)}, u32[]{:S(2)}) copy-start(s32[1,16384]{1,0:T(1,128)} %step_ref.1) | copy-start | bytes 196612
  3.0 25.6 %all-to-all-start = ((f32[16,24,768]{2,1,0:T(8,128)}), f32[16,24,768]{2,1,0:T(8,128)S(1)}, u32[]{:S(2)}, u32[]{:S(2)}) async-start(f32[16,24,768]{2,1,0:T(8,128)} %pack.1), calls=%async_computation | async-start | bytes 2359296 | tf_op jit(solution)/shard_map/all_to_all | solution.py:548
  10.8 3.9 %collective-permute-start.2 = (f32[1,2048]{1,0:T(1,128)S(1)}, f32[1,2048]{1,0:T(1,128)S(1)}, u32[]{:S(2)}, u32[]{:S(2)}) collective-permute-start(f32[1,2048]{1,0:T(1,128)S(1)} %duals.1.refs_0_), channel_id=1, source_target_pairs={{0,3},{1,2},{2,1},{3,0},{4,7},{5,6},{6,5},{7,4},{8,11},{9,10},{10,... | collective-permute-start | bytes 24584 | tf_op jit(solution)/shard_map/ppermute | solution.py:563
  13.3 2.9 %collective-permute-start.1 = (f32[1,2048]{1,0:T(1,128)S(1)}, f32[1,2048]{1,0:T(1,128)S(1)}, u32[]{:S(2)}, u32[]{:S(2)}) collective-permute-start(f32[1,2048]{1,0:T(1,128)S(1)} %duals.1.refs_0_), channel_id=1, source_target_pairs={{0,2},{1,3},{2,0},{3,1},{4,6},{5,7},{6,4},{7,5},{8,10},{9,11},{10,... | collective-permute-start | bytes 24584 | tf_op jit(solution)/shard_map/ppermute | solution.py:563
  13.3 2.9 %collective-permute-start = (f32[1,2048]{1,0:T(1,128)S(1)}, f32[1,2048]{1,0:T(1,128)S(1)}, u32[]{:S(2)}, u32[]{:S(2)}) collective-permute-start(f32[1,2048]{1,0:T(1,128)S(1)} %duals.1.refs_0_), channel_id=1, source_target_pairs={{0,1},{1,0},{2,3},{3,2},{4,5},{5,4},{6,7},{7,6},{8,9},{9,8},{10,11... | collective-permute-start | bytes 24584 | tf_op jit(solution)/shard_map/ppermute | solution.py:563
  16.2 10.5 %collective-permute-start.5 = (f32[4,2048]{1,0:T(4,128)S(1)}, f32[4,2048]{1,0:T(4,128)S(1)}, u32[]{:S(2)}, u32[]{:S(2)}) collective-permute-start(f32[4,2048]{1,0:T(4,128)S(1)} %join.1.refs_0_), channel_id=1, source_target_pairs={{0,12},{1,13},{2,14},{3,15},{4,8},{5,9},{6,10},{7,11},{8,4},{9,5},... | collective-permute-start | bytes 98312 | tf_op jit(solution)/shard_map/ppermute | solution.py:576
  21.3 7.2 %collective-permute-start.4 = (f32[4,2048]{1,0:T(4,128)S(1)}, f32[4,2048]{1,0:T(4,128)S(1)}, u32[]{:S(2)}, u32[]{:S(2)}) collective-permute-start(f32[4,2048]{1,0:T(4,128)S(1)} %join.1.refs_0_), channel_id=1, source_target_pairs={{0,8},{1,9},{2,10},{3,11},{4,12},{5,13},{6,14},{7,15},{8,0},{9,1},... | collective-permute-start | bytes 98312 | tf_op jit(solution)/shard_map/ppermute | solution.py:576
  22.5 6.1 %collective-permute-start.3 = (f32[4,2048]{1,0:T(4,128)S(1)}, f32[4,2048]{1,0:T(4,128)S(1)}, u32[]{:S(2)}, u32[]{:S(2)}) collective-permute-start(f32[4,2048]{1,0:T(4,128)S(1)} %join.1.refs_0_), channel_id=1, source_target_pairs={{0,4},{1,5},{2,6},{3,7},{4,0},{5,1},{6,2},{7,3},{8,12},{9,13},{10,... | collective-permute-start | bytes 98312 | tf_op jit(solution)/shard_map/ppermute | solution.py:576
  29.6 19.4 %all-to-all-start.1 = ((f32[16,16,768]{2,1,0:T(8,128)}), f32[16,16,768]{2,1,0:T(8,128)S(1)}, u32[]{:S(2)}, u32[]{:S(2)}) async-start(f32[16,16,768]{2,1,0:T(8,128)} %scan.1), calls=%async_computation.1 | async-start | bytes 1572864 | tf_op jit(solution)/shard_map/all_to_all | solution.py:630
  36.5 23.6 %collective-permute-start.8 = (f32[4,8,3072]{2,1,0:T(8,128)}, f32[4,8,3072]{2,1,0:T(8,128)}, u32[]{:S(2)}, u32[]{:S(2)}) collective-permute-start(f32[4,8,3072]{2,1,0:T(8,128)} %bitcast.2.rm_ref), channel_id=1, source_target_pairs={{16,0},{32,16},{48,32},{64,48},{80,64},{96,80},{112,96},{128,112},... | collective-permute-start | bytes 1179656 | tf_op jit(solution)/shard_map/ppermute | solution.py:550
  37.8 1.0 copy-start.2
  38.8 1.0 copy-start.4
  50.1 10.0 %collective-permute-start.7 = (f32[24,3072]{1,0:T(8,128)}, f32[24,3072]{1,0:T(8,128)S(1)}, u32[]{:S(2)}, u32[]{:S(2)}) collective-permute-start(f32[24,3072]{1,0:T(8,128)} %get-tuple-element.24), channel_id=1, source_target_pairs={{1,0},{2,1},{3,2},{4,3},{5,4},{6,5},{7,6},{8,7},{9,8},{10,9},{11,1... | collective-permute-start | bytes 884744 | tf_op jit(solution)/shard_map/ppermute | solution.py:642
  54.8 6.0 %collective-permute-start.6 = (f32[24,3072]{1,0:T(8,128)}, f32[24,3072]{1,0:T(8,128)}, u32[]{:S(2)}, u32[]{:S(2)}) collective-permute-start(f32[24,3072]{1,0:T(8,128)} %get-tuple-element.23.after_ref), channel_id=1, source_target_pairs={{0,1},{1,2},{2,3},{3,4},{4,5},{5,6},{6,7},{7,8},{8,9},{9,10},{10,1... | collective-permute-start | bytes 884744 | tf_op jit(solution)/shard_map/ppermute | solution.py:641
  57.0 1.0 copy-start
  58.0 1.0 copy-start.3
  59.0 1.0 copy-start.5
  60.7 38.3 %copy-start.1 = (f32[1,4,8,3072]{3,2,1,0:T(8,128)S(1)}, f32[1,4,8,3072]{3,2,1,0:T(8,128)}, u32[]{:S(2)}) copy-start(f32[1,4,8,3072]{3,2,1,0:T(8,128)} %param.25) | copy-start | bytes 1179652
  60.8 38.3 %copy-start.6 = (f32[1,4,8,3072]{3,2,1,0:T(8,128)S(1)}, f32[1,4,8,3072]{3,2,1,0:T(8,128)}, u32[]{:S(2)}) copy-start(f32[1,4,8,3072]{3,2,1,0:T(8,128)} %param.20) | copy-start | bytes 1179652
  60.8 38.3 %copy-start.7 = (f32[1,4,8,3072]{3,2,1,0:T(8,128)S(1)}, f32[1,4,8,3072]{3,2,1,0:T(8,128)}, u32[]{:S(2)}) copy-start(f32[1,4,8,3072]{3,2,1,0:T(8,128)} %param.22) | copy-start | bytes 1179652
  60.8 38.3 %copy-start.13 = (f32[1,1024]{1,0:T(1,128)S(1)}, f32[1,1024]{1,0:T(1,128)}, u32[]{:S(2)}) copy-start(f32[1,1024]{1,0:T(1,128)} %ov_ref.3) | copy-start | bytes 12292
  60.8 38.3 %copy-start.14 = (f32[1,1024]{1,0:T(1,128)S(1)}, f32[1,1024]{1,0:T(1,128)}, u32[]{:S(2)}) copy-start(f32[1,1024]{1,0:T(1,128)} %do_ref.1) | copy-start | bytes 12292
  67.0 32.0 %collective-permute-start.9 = (f32[4,8,3072]{2,1,0:T(8,128)S(1)}, f32[4,8,3072]{2,1,0:T(8,128)S(1)}, u32[]{:S(2)}, u32[]{:S(2)}) collective-permute-start(f32[4,8,3072]{2,1,0:T(8,128)S(1)} %get-tuple-element.27), channel_id=1, source_target_pairs={{0,16},{16,32},{32,48},{48,64},{64,80},{80,96},{96,112},{112,128},... | collective-permute-start | bytes 1179656 | tf_op jit(solution)/shard_map/ppermute | solution.py:672

commit v4 on v3

--- a/solution.py
+++ b/solution.py
@@ -59,7 +59,7 @@
         out_ref[place * levels : (place + 1) * levels] = ref[...]
 
 
-def pack_kernel(parts, rs_ref, rm_ref, mv_ref, out_ref):
+def pack_kernel(parts, rs_ref, rm_ref, mv_ref, out_ref, square_ref):
     levels, rows, columns = rs_ref.shape
     per_level = parts // levels
     width = columns // per_level
@@ -68,6 +68,10 @@
         cols = slice(piece * width, (piece + 1) * width)
         for place, ref in enumerate((rs_ref, rm_ref, mv_ref)):
             out_ref[part, rows * place : rows * (place + 1), :] = ref[level, :, cols]
+    square = jnp.zeros((rows, columns), jnp.float32)
+    for level in range(levels):
+        square += rm_ref[level] * rm_ref[level]
+    square_ref[...] = jnp.broadcast_to(jnp.sum(square), square_ref.shape)
 
 
 def scan_kernel(in_ref, *rest):
@@ -97,7 +101,7 @@
             out_ref[pl.ds(at, 1), :] = ref[i : i + 1, :]
 
 
-def edge_kernel(levels, back_ref, bundle_ref, up_ref, down_ref, rows_s):
+def edge_kernel(levels, first_row, back_ref, bundle_ref, table_ref, up_ref, down_ref, rows_s):
     parts, both, width = back_ref.shape
     rows = both // 2
     per_level = parts // levels
@@ -110,7 +114,18 @@
                 row_at = rows * field + row
                 rows_s[at : at + 1, cols] = back_ref[part, row_at : row_at + 1, :]
     incr, incr_in, dual, dual_in = (rows_s[8 * i : 8 * i + 8, :] for i in range(4))
-    cx, cy, cy_in, middle = (bundle_ref[2 * levels + i] for i in range(4))
+    lane_groups = rows_s.shape[1] // LANES
+    cx, cy, cy_in = (
+        jnp.concatenate(
+            [
+                table_ref[at : at + 8, :]
+                for at in range(first_row + i * lane_groups * 8, first_row + (i + 1) * lane_groups * 8, 8)
+            ],
+            axis=1,
+        )
+        for i in range(3)
+    )
+    middle = bundle_ref[2 * levels]
     own, west, east, south, north = weights_of(cx, cy)
     is_up = lax.broadcasted_iota(jnp.int32, cx.shape, 0) < 4
     inner, outer = jnp.where(is_up, south, north), jnp.where(is_up, north, south)
@@ -151,11 +166,11 @@
     lax.fori_loop(0, rank_ref.shape[0], one_chunk, 0, unroll=4)
 
 
-def sections(chunks):
+def sections(chunks, lane_groups):
     tall = CHUNK // LANES
     sizes = dict(
         codes=chunks * LANES, rank=chunks * tall, code=chunks * tall, groups=chunks,
-        square=8,
+        edges=3 * lane_groups * 8,
     )
     places, at = {}, 0
     for name, size in sizes.items():
@@ -183,13 +198,13 @@
     ], axis=0)
 
 
-def place_kernel(columns, at_ref, brick_ref, cell_ref, step_ref, rm_ref,
+def place_kernel(columns, at_ref, brick_ref, cell_ref, step_ref, cx_ref, cy_ref,
                  table_ref, passes_ref, brick_s, cell_s, step_s, groups_s):
     chunks = brick_s.shape[0]
     rank_ref, code_ref = brick_s, cell_s
-    places, _ = sections(chunks)
     here = at_ref[0]
     lane_groups = columns // LANES
+    places, _ = sections(chunks, lane_groups)
     for k in range(chunks):
         cols = slice(k * CHUNK, (k + 1) * CHUNK)
         brick_s[k : k + 1, :] = brick_ref[0:1, cols]
@@ -214,18 +229,21 @@
     fold(table_ref, places["code"], code_ref[...].astype(jnp.float32))
     table_ref[places["groups"] : places["groups"] + chunks, :] = groups_s[...].astype(jnp.float32)
     passes_ref[0] = (jnp.max(count.astype(jnp.float32)).astype(jnp.int32) + SLOTS - 1) // SLOTS
-    square = jnp.zeros(rm_ref.shape[1:], jnp.float32)
-    for level in range(rm_ref.shape[0]):
-        square += rm_ref[level] * rm_ref[level]
-    table_ref[places["square"] : places["square"] + 8, :] = jnp.broadcast_to(
-        jnp.sum(square), (8, LANES)
-    )
-
-
-def in_column(codes, values, which):
-    codes = codes.astype(jnp.int32)
-    lane = lax.broadcasted_iota(jnp.int32, codes.shape, 1) + which * LANES
-    return jnp.where((codes & 255) == lane, values, 0.0)
+    rows = cx_ref.shape[1]
+    for place, (ref, pair) in enumerate((
+        (cx_ref, (rows - 1, 0)), (cy_ref, (rows - 1, 0)), (cy_ref, (rows - 2, 1)),
+    )):
+        edge = jnp.concatenate(
+            [ref[level, row : row + 1, :] for row in pair for level in range(cx_ref.shape[0])], axis=0
+        )
+        for g in range(lane_groups):
+            at = places["edges"] + (place * lane_groups + g) * 8
+            table_ref[at : at + 8, :] = edge[:, g * LANES : (g + 1) * LANES]
+
+
+def in_column(columns, values, which):
+    lane = lax.broadcasted_iota(jnp.int32, columns.shape, 1) + which * LANES
+    return jnp.where(columns == lane, values, 0.0)
 
 
 def split_two(x):
@@ -234,26 +252,21 @@
     return high, low
 
 
-def spread_kernel(passes_ref, table_ref, lines_ref, cx_ref, cy_ref, bundle_ref,
+def spread_kernel(passes_ref, table_ref, lines_ref, bundle_ref,
                   rank_ref, code_ref, again_codes, groups_ref, hot_s, high_s, low_s, total):
     chunks = rank_ref.shape[0]
-    places, _ = sections(chunks)
+    _, rows, columns = bundle_ref.shape
+    lane_groups = columns // LANES
+    groups = total.shape[0]
+    levels = groups // (lane_groups * rows)
+    places, _ = sections(chunks, lane_groups)
     rank_ref[...] = unfold(table_ref, places["rank"], chunks).astype(jnp.int32)
     groups_ref[...] = table_ref[places["groups"] : places["groups"] + chunks, :].astype(jnp.int32)
-    levels, rows, columns = cx_ref.shape
-    lane_groups = columns // LANES
-    groups = total.shape[0]
     for k in range(chunks // 8):
-        bundle_ref[3 * levels, :, k * CHUNK : (k + 1) * CHUNK] = lines_ref[8 * k : 8 * k + 8, 0:CHUNK]
-    rows_ref = bundle_ref.at[2 * levels : 3 * levels]
-    for level in range(levels):
-        for place, row in enumerate((rows - 1, 0)):
-            at = 4 * place + level
-            rows_ref[0, at : at + 1, :] = cx_ref[level, row : row + 1, :]
-            rows_ref[1, at : at + 1, :] = cy_ref[level, row : row + 1, :]
-            inner = row - 1 if place == 0 else row + 1
-            rows_ref[2, at : at + 1, :] = cy_ref[level, inner : inner + 1, :]
-    group_id = lax.broadcasted_iota(jnp.int32, (groups, LANES), 0)
+        bundle_ref[2 * levels + 1, :, k * CHUNK : (k + 1) * CHUNK] = lines_ref[8 * k : 8 * k + 8, 0:CHUNK]
+    rows_ref = bundle_ref.at[2 * levels]
+    group_id = lax.broadcasted_iota(jnp.int32, (groups, LANES), 0).astype(jnp.int16)
+    one, zero = jnp.ones((), jnp.bfloat16), jnp.zeros((), jnp.bfloat16)
 
     def add_up(first, codes_ref):
         def one_chunk(k, carry):
@@ -268,13 +281,15 @@
                 )
                 parts.append(jnp.broadcast_to(dual, (SLOTS, LANES)))
             dual = jnp.concatenate(parts, axis=0)
-            codes = codes_ref[at, :]
+            columns = codes_ref[at, :].astype(jnp.int32) & 255
+            high = dual.astype(jnp.bfloat16).astype(jnp.float32)
             for which in range(2):
-                high, low = split_two(in_column(codes, dual, which))
-                high_s[at, which * LANES : (which + 1) * LANES] = high
-                low_s[at, which * LANES : (which + 1) * LANES] = low
-            row = jnp.broadcast_to(groups_ref[pl.ds(k, 1), :], (groups, LANES))
-            hot_s[:, at] = (row == group_id).astype(jnp.float32).astype(jnp.bfloat16)
+                cols = slice(which * LANES, (which + 1) * LANES)
+                high_s[at, cols] = in_column(columns, high, which).astype(jnp.bfloat16)
+                low_s[at, cols] = in_column(columns, dual - high, which).astype(jnp.bfloat16)
+            row = jnp.broadcast_to(groups_ref[pl.ds(k, 1), :], (16, LANES)).astype(jnp.int16)
+            row = jnp.concatenate([row] * (groups // 16), axis=0)
+            hot_s[:, at] = jnp.where(row == group_id, one, zero)
             return carry
 
         lax.fori_loop(0, chunks, one_chunk, 0, unroll=4)
@@ -301,7 +316,7 @@
     for level in range(levels):
         for place, row in enumerate((rows - 1, 0)):
             at = 4 * place + level
-            rows_ref[3, at : at + 1, :] = bundle_ref[levels + level, row : row + 1, :]
+            rows_ref[at : at + 1, :] = bundle_ref[levels + level, row : row + 1, :]
 
 
 def west_of(v):
@@ -336,17 +351,19 @@
     return jnp.where(last, jnp.broadcast_to(edge, v.shape), pltpu.roll(v, v.shape[0] - 1, 0))
 
 
-def image_kernel(windows, window_ref, passes_ref, back_ref, below_ref, above_ref, args_ref,
-                 bundle_ref, rm_next_ref, table_ref, next_ref, state_ref, sent_ref,
+def image_kernel(windows, bricks, window_ref, at_ref, passes_ref, back_ref, below_ref, above_ref, args_ref,
+                 bundle_ref, rm_next_ref, square_ref, table_ref, next_ref, state_ref, sent_ref,
                  fields, rank_ref, code_ref, again_codes, again_groups, hot_s, found):
     levels, rows, columns = rm_next_ref.shape
     parts, _, width = back_ref.shape
     per_level = parts // levels
     chunks = found.shape[0]
-    places, _ = sections(chunks)
+    lane_groups = columns // LANES
+    places, _ = sections(chunks, lane_groups)
     rank_ref[...] = unfold(table_ref, places["rank"], chunks).astype(jnp.int32)
-    lane_groups = columns // LANES
-    window = window_ref[0]
+    window, here = window_ref[0], at_ref[0]
+    has_below = jnp.where(here > 0, 1.0, 0.0)
+    has_above = jnp.where(here < bricks - 1, 1.0, 0.0)
 
     row_id = lax.broadcasted_iota(jnp.int32, (rows, columns), 0)
     first, last = row_id == 0, row_id == rows - 1
@@ -360,7 +377,8 @@
         coeffs = weights_of(args_ref[level], args_ref[levels + level])
         south, north = coeffs[3], coeffs[4]
         low, high = (
-            [ref[4 * i + level : 4 * i + level + 1, :] for i in range(5)] for ref in (below_ref, above_ref)
+            [held * ref[4 * i + level : 4 * i + level + 1, :] for i in range(5)]
+            for ref, held in ((below_ref, has_below), (above_ref, has_above))
         )
         after_one = forward(
             incr,
@@ -404,19 +422,18 @@
     high_fields, low_fields = split_two(fields[...])
     groups = levels * lane_groups * 8
     together = hot_s.shape[0] // LANES
-    group_id = lax.broadcasted_iota(jnp.int32, (LANES, groups), 1)
+    group_id = lax.broadcasted_iota(jnp.int32, (LANES, groups), 1).astype(jnp.int16)
+    one, zero = jnp.ones((), jnp.bfloat16), jnp.zeros((), jnp.bfloat16)
 
     def look_up(first, fresh, codes_ref):
         def some_chunks(q, carry):
             codes = []
             for j in range(together):
                 k = q * together + j
-                code = codes_ref[pl.ds(pl.multiple_of(k * LANES, LANES), LANES), :]
-                wide = jnp.concatenate([code.astype(jnp.int32) >> 8] * (groups // LANES), axis=1)
-                hot_s[j * LANES : (j + 1) * LANES, :] = (
-                    (wide == group_id).astype(jnp.float32).astype(jnp.bfloat16)
-                )
-                codes.append(code)
+                code = codes_ref[pl.ds(pl.multiple_of(k * LANES, LANES), LANES), :].astype(jnp.int32)
+                wide = jnp.concatenate([(code >> 8).astype(jnp.int16)] * (groups // LANES), axis=1)
+                hot_s[j * LANES : (j + 1) * LANES, :] = jnp.where(wide == group_id, one, zero)
+                codes.append(code & 255)
             picks = hot_s[...]
             picked = jnp.dot(
                 picks, high_fields, preferred_element_type=jnp.float32
@@ -457,10 +474,10 @@
 
     observed = found[...]
     resid = jnp.concatenate(
-        [bundle_ref[3 * levels, :, k * CHUNK : (k + 1) * CHUNK] for k in range(chunks // 8)], axis=0
+        [bundle_ref[2 * levels + 1, :, k * CHUNK : (k + 1) * CHUNK] for k in range(chunks // 8)], axis=0
     )
     image_obs = jnp.where(rank_ref[...] >= 0, resid + observed, 0.0)
-    square = jnp.where(window == 0, table_ref[places["square"] : places["square"] + 1, :], 0.0)
+    square = jnp.where(window == 0, square_ref[...], 0.0)
     all_projected = jnp.sum(projected) + jnp.sum(resid * image_obs) + square
     all_curvature = jnp.sum(curvature) + jnp.sum(image_obs * image_obs) + square
     lane = lax.broadcasted_iota(jnp.int32, (1, LANES), 1)
@@ -479,9 +496,12 @@
         sums_ref[k] = total[:, CHUNK : CHUNK + LANES]
 
 
-def update_kernel(window_ref, sums_ref, ds_ref, inc_ref, rm_ref, rs_ref, back_ref, image_ref, state_ref,
+def update_kernel(window_ref, sums_ref, ds_ref, inc_ref, rm_hbm, rs_ref, back_ref, image_ref, state_ref,
                   do_ref, ro_ref, ov_ref, observed_ref,
-                  ds_out, do_out, inc_out, rm_out, ro_out, rs_out, ds_s, inc_s, rm_s, rs_s, sems):
+                  ds_out, do_out, inc_out, rm_out, ro_out, rs_out, ds_s, inc_s, rm_s, rs_s,
+                  rm_ref, sems, rm_sem):
+    rm_copy = pltpu.make_async_copy(rm_hbm, rm_ref, rm_sem)
+    rm_copy.start()
     sums = sums_ref[0]
     for k in range(1, sums_ref.shape[0]):
         sums = sums + sums_ref[k]
@@ -495,21 +515,29 @@
     wide = jnp.broadcast_to(step, (rows, width))
     starts = window_ref[0] == 0
     copies = []
+
+    def store(place, level, held, out):
+        copies.append(pltpu.make_async_copy(held.at[level], out.at[level], sems.at[level, place]))
+        copies[-1].start()
+
     for level in range(levels):
         for piece in range(per_level):
             part = level * per_level + piece
             cols = slice(piece * width, (piece + 1) * width)
-            rs, rm = rs_ref[level, :, cols], rm_ref[level, :, cols]
+            rs = rs_ref[level, :, cols]
             dual = back_ref[part, rows : 2 * rows, :] + rs
             ds_s[level, :, cols] = ds_ref[level, :, cols] + wide * dual
             inc_s[level, :, cols] = inc_ref[level, :, cols] + wide * back_ref[part, 0:rows, :]
-            image = jnp.where(starts, rm, image_ref[level, :, cols])
-            rm_s[level, :, cols] = rm - wide * image
             rs_s[level, :, cols] = rs - wide * state_ref[level, :, cols]
-        pairs = ((ds_s, ds_out), (inc_s, inc_out), (rm_s, rm_out), (rs_s, rs_out))
-        for place, (held, out) in enumerate(pairs):
-            copies.append(pltpu.make_async_copy(held.at[level], out.at[level], sems.at[level, place]))
-            copies[-1].start()
+        store(0, level, ds_s, ds_out)
+        store(1, level, inc_s, inc_out)
+        store(2, level, rs_s, rs_out)
+    rm_copy.wait()
+    whole_step = jnp.broadcast_to(step, (rows, columns))
+    for level in range(levels):
+        rm = rm_ref[level]
+        rm_s[level] = rm - whole_step * jnp.where(starts, rm, image_ref[level])
+        store(3, level, rm_s, rm_out)
     narrow = jnp.broadcast_to(step, ro_ref.shape)
     ro, ov = ro_ref[...], ov_ref[...]
     dual = ro / ov
@@ -533,14 +561,15 @@
     window = lax.axis_index("tm").astype(jnp.int32)
     at, window_at = here[None], window[None]
 
-    upward = [(i, i + 1) for i in range(bricks - 1)]
-    downward = [(i + 1, i) for i in range(bricks - 1)]
-
-    packed = pl.pallas_call(
+    upward = [(i, (i + 1) % bricks) for i in range(bricks)]
+    downward = [((i + 1) % bricks, i) for i in range(bricks)]
+    later = [(i, (i + 1) % windows) for i in range(windows)]
+
+    packed, square = pl.pallas_call(
         functools.partial(pack_kernel, windows),
-        out_shape=f32(windows, 3 * rows, width),
+        out_shape=(f32(windows, 3 * rows, width), f32(1, LANES)),
         in_specs=[VMEM] * 3,
-        out_specs=VMEM,
+        out_specs=(VMEM, VMEM),
         compiler_params=params(60),
         cost_estimate=cost(1, 1),
         name="pack",
@@ -577,6 +606,7 @@
         for k in range(1, bricks // distance)
     ]
     slots = blocks * LANES
+    places, table_rows = sections(blocks, columns // LANES)
     field_s = pltpu.VMEM((levels, rows, columns), jnp.float32)
     table_s = pltpu.VMEM((blocks, CHUNK), jnp.int32)
     line_s = pltpu.VMEM((blocks, CHUNK), jnp.float32)
@@ -584,14 +614,14 @@
     groups_s = pltpu.VMEM((blocks, LANES), jnp.int32)
     table, passes = pl.pallas_call(
         functools.partial(place_kernel, columns),
-        out_shape=(f32(sections(blocks)[1], LANES), i32(1)),
-        in_specs=[SMEM] + [VMEM] * 4,
+        out_shape=(f32(table_rows, LANES), i32(1)),
+        in_specs=[SMEM] + [VMEM] * 5,
         out_specs=(VMEM, SMEM),
         scratch_shapes=[table_s, table_s, table_s, groups_s],
         compiler_params=params(8),
         cost_estimate=cost(1, 1),
         name="places",
-    )(at, obs_brick, obs_cell, obs_step, rm)
+    )(at, obs_brick, obs_cell, obs_step, cx, cy)
     lines = pl.pallas_call(
         collect_kernel,
         out_shape=f32(blocks, 2 * CHUNK),
@@ -603,8 +633,8 @@
     )(at, near, *far)
     bundle = pl.pallas_call(
         spread_kernel,
-        out_shape=f32(3 * levels + 1, rows, columns),
-        in_specs=[SMEM] + [VMEM] * 4,
+        out_shape=f32(2 * levels + 2, rows, columns),
+        in_specs=[SMEM] + [VMEM] * 2,
         out_specs=VMEM,
         scratch_shapes=[
             table_s, table_s, codes_s, groups_s,
@@ -616,7 +646,7 @@
         compiler_params=params(24),
         cost_estimate=cost(1, 1),
         name="spread",
-    )(passes, table, lines, cx, cy)
+    )(passes, table, lines)
 
     summed = pl.pallas_call(
         scan_kernel,
@@ -629,15 +659,15 @@
     )(windows_of, table, lines)
     back = lax.all_to_all(summed, "tm", 0, 0)
     up, down = pl.pallas_call(
-        functools.partial(edge_kernel, levels),
+        functools.partial(edge_kernel, levels, places["edges"]),
         out_shape=(f32(24, columns), f32(24, columns)),
-        in_specs=[VMEM, VMEM],
+        in_specs=[VMEM, VMEM, VMEM],
         out_specs=(VMEM, VMEM),
         scratch_shapes=[pltpu.VMEM((32, columns), jnp.float32)],
         compiler_params=params(6),
         cost_estimate=cost(1, 1),
         name="edges",
-    )(back, bundle)
+    )(back, bundle, table)
     below = lax.ppermute(up, "space", upward)
     above = lax.ppermute(down, "space", downward)
 
@@ -652,11 +682,11 @@
     )(cx, cy, rs, up)
 
     image_next, image_state, sent = pl.pallas_call(
-        functools.partial(image_kernel, windows),
+        functools.partial(image_kernel, windows, bricks),
         out_shape=(
             f32(levels, rows, columns), f32(levels, rows, columns), f32(blocks, 1, CHUNK + LANES),
         ),
-        in_specs=[SMEM, SMEM] + [VMEM] * 7,
+        in_specs=[SMEM, SMEM, SMEM] + [VMEM] * 8,
         out_specs=(VMEM, VMEM, VMEM),
         scratch_shapes=[
             pltpu.VMEM((groups, 2 * LANES), jnp.float32),
@@ -667,9 +697,9 @@
         compiler_params=params(24),
         cost_estimate=cost(1, 1),
         name="images",
-    )(window_at, passes, back, below, above, fields, bundle, rm_next, table)
-
-    image_model = lax.ppermute(image_next, "tm", [(i, i + 1) for i in range(windows - 1)])
+    )(window_at, at, passes, back, below, above, fields, bundle, rm_next, square, table)
+
+    image_model = lax.ppermute(image_next, "tm", later)
     got = lax.all_to_all(sent, "space", 0, 0)
     observed, sums = pl.pallas_call(
         gather_kernel,
@@ -689,9 +719,10 @@
             f32(levels, rows, columns), f32(1, count), f32(levels, rows, columns),
             f32(levels, rows, columns), f32(1, count), f32(levels, rows, columns),
         ),
-        in_specs=[SMEM] + [VMEM] * 12,
+        in_specs=[SMEM] + [VMEM] * 3 + [HBM] + [VMEM] * 8,
         out_specs=(HBM, VMEM, HBM, HBM, VMEM, HBM),
-        scratch_shapes=[field_s] * 4 + [pltpu.SemaphoreType.DMA((levels, 4))],
+        scratch_shapes=[field_s] * 5
+        + [pltpu.SemaphoreType.DMA((levels, 4)), pltpu.SemaphoreType.DMA(())],
         compiler_params=params(8),
         cost_estimate=cost(1, 1),
         name="updates",

time: 103 us -> 96.4 us (0.936)
  starting transfers between devices: 35.5 us -> 29.8 us
  waiting for transfers between devices: 8.69 us -> 12 us
  Pallas kernels: 22.4 us -> 20.4 us
  blocking collectives: 29.5 us -> 27.7 us
    all_to_all x1, waiting for transfers between devices: 3.75 us -> 6.51 us  [body(): back = lax.all_to_all(summed, 'tm', 0, 0)]
    pallas_call x5, Pallas kernels: 18.3 us -> 16 us  [the longest x1 5.71 us: body(): pl.pallas_call(functools.partial(image_kernel, windows, bricks), out_shap...]
    ppermute x1, starting transfers between devices: 2.2 us -> 0.1 us  [body(): below = lax.ppermute(up, 'space', upward)]
    ppermute x1, waiting for transfers between devices: 0.01 us -> 1.93 us  [body(): above = lax.ppermute(down, 'space', downward)]
    ppermute x1, starting transfers between devices: 4.66 us -> 2.77 us  [body(): above = lax.ppermute(down, 'space', downward)]
    ppermute x1, starting transfers between devices: 2.43 us -> 0.57 us  [body(): image_model = lax.ppermute(image_next, 'tm', later)]
    all_to_all x1, blocking collectives: 16.4 us -> 15.3 us  [body(): got = lax.all_to_all(sent, 'space', 0, 0)]
  transfers between devices with their start and end apart: 12 -> 12, of which waited for: 5 -> 5; matrix products, arithmetic and copies ran while one was open for 0% -> 0% of each run, Pallas kernels for 10% -> 9%
where the time goes in v4:
time: 96.4 us; the launch traced here: 95.6 us
  starting transfers between devices  29.8 us (31%)
  blocking collectives  27.7 us (29%)
  Pallas kernels  20.4 us (21%)
  waiting for transfers between devices  12 us (12%)
  local copies, waits for them, and re-layouts  4.71 us (5%)
  between operations  0.99 us (1%)
    all_to_all x1, blocking collectives, body(): got = lax.all_to_all(sent, 'space', 0, 0)  15.3 us
    all_to_all x1, blocking collectives, body(): all_sums = lax.all_to_all(sums, 'tm', 0, 0)  12.4 us
    ppermute x6, starting transfers between devices, body(): lax.ppermute(near, 'space', [(i, i ^ distance * k) for i in range(bricks)])  10.4 us
    all_to_all x1, starting transfers between devices, body(): windows_of = lax.all_to_all(packed, 'tm', 0, 0)  7.73 us
    all_to_all x1, starting transfers between devices, body(): back = lax.all_to_all(summed, 'tm', 0, 0)  6.96 us
    all_to_all x1, waiting for transfers between devices, body(): back = lax.all_to_all(summed, 'tm', 0, 0)  6.51 us
    pallas_call x1, Pallas kernels, body(): pl.pallas_call(functools.partial(image_kernel, windows, bricks), out_shap...  5.71 us
    unnamed x30, local copies, waits for them, and re-layouts  4.71 us
  transfers between devices with their start and end apart: 12, of which 5 were waited for; matrix products, arithmetic and copies ran while one was open for 0% of the time, Pallas kernels for 9%

profile of v4, /device:TPU:1, one launch (start us, length us, event | category | flops | bytes accessed | tf_op | source)
XLA Modules:
  0.0 95.6 jit_solution(4741864450428714322)
XLA Ops:
  0.6 2.4 %pack.1 = (f32[16,24,768]{2,1,0:T(8,128)}, f32[1,128]{1,0:T(1,128)}) custom-call(f32[4,8,3072]{2,1,0:T(8,128)} %bitcast.13, f32[4,8,3072]{2,1,0:T(8,128)} %bitcast.5.rm_ref.rm_hbm, f32[4,8,3072]{2,1,0:T(8,128)} %bitcast.22), custom_call_target="tpu_custom_call" | custom-call | flops 1 | bytes 1 | tf_op jit(solution)/shard_map/pack/pallas_call | solution.py:568
  3.0 0.0 copy-start.11
  3.0 0.0 copy-start.12
  3.0 0.0 copy-start.2
  3.0 0.0 copy-start.4
  3.0 0.0 copy-start.8
  3.0 7.7 %all-to-all-start = ((f32[16,24,768]{2,1,0:T(8,128)}), f32[16,24,768]{2,1,0:T(8,128)S(1)}, u32[]{:S(2)}, u32[]{:S(2)}) async-start(f32[16,24,768]{2,1,0:T(8,128)} %get-tuple-element.24), calls=%async_computation | async-start | bytes 2359296 | tf_op jit(solution)/shard_map/all_to_all | solution.py:577
  10.8 0.0 copy-done.11
  10.8 0.0 copy-done.12
  10.8 2.6 %collective-permute-start.2 = (f32[1,2048]{1,0:T(1,128)S(1)}, f32[1,2048]{1,0:T(1,128)S(1)}, u32[]{:S(2)}, u32[]{:S(2)}) collective-permute-start(f32[1,2048]{1,0:T(1,128)S(1)} %duals.1.refs_0_), channel_id=1, source_target_pairs={{0,3},{1,2},{2,1},{3,0},{4,7},{5,6},{6,5},{7,4},{8,11},{9,10},{10,... | collective-permute-start | bytes 24584 | tf_op jit(solution)/shard_map/ppermute | solution.py:592
  13.4 0.0 collective-permute-start.1
  13.4 0.5 collective-permute-start
  13.8 0.8 collective-permute-done.2.refs_3_
  14.7 1.5 %collective-permute-done.1.refs_2_ = f32[1,2048]{1,0:T(1,128)S(1)} collective-permute-done((f32[1,2048]{1,0:T(1,128)S(1)}, f32[1,2048]{1,0:T(1,128)S(1)}, u32[]{:S(2)}, u32[]{:S(2)}) %collective-permute-start.1) | collective-permute-done | bytes 8224 | tf_op jit(solution)/shard_map/ppermute | solution.py:592
  16.2 0.0 collective-permute-done.refs_1_
  16.2 5.1 %collective-permute-start.5 = (f32[4,2048]{1,0:T(4,128)S(1)}, f32[4,2048]{1,0:T(4,128)}, u32[]{:S(2)}, u32[]{:S(2)}) collective-permute-start(f32[4,2048]{1,0:T(4,128)S(1)} %join.1.refs_0_), channel_id=1, source_target_pairs={{0,12},{1,13},{2,14},{3,15},{4,8},{5,9},{6,10},{7,11},{8,4},{9,5},... | collective-permute-start | bytes 98312 | tf_op jit(solution)/shard_map/ppermute | solution.py:605
  21.3 1.2 %collective-permute-start.4 = (f32[4,2048]{1,0:T(4,128)S(1)}, f32[4,2048]{1,0:T(4,128)}, u32[]{:S(2)}, u32[]{:S(2)}) collective-permute-start(f32[4,2048]{1,0:T(4,128)S(1)} %join.1.refs_0_), channel_id=1, source_target_pairs={{0,8},{1,9},{2,10},{3,11},{4,12},{5,13},{6,14},{7,15},{8,0},{9,1},... | collective-permute-start | bytes 98312 | tf_op jit(solution)/shard_map/ppermute | solution.py:605
  22.5 1.0 %collective-permute-start.3 = (f32[4,2048]{1,0:T(4,128)S(1)}, f32[4,2048]{1,0:T(4,128)}, u32[]{:S(2)}, u32[]{:S(2)}) collective-permute-start(f32[4,2048]{1,0:T(4,128)S(1)} %join.1.refs_0_), channel_id=1, source_target_pairs={{0,4},{1,5},{2,6},{3,7},{4,0},{5,1},{6,2},{7,3},{8,12},{9,13},{10,... | collective-permute-start | bytes 98312 | tf_op jit(solution)/shard_map/ppermute | solution.py:605
  23.5 0.0 copy-done.2
  23.5 0.0 copy-done.4
  23.5 0.0 copy-done.8
  23.5 0.0 copy-start.9
  23.5 0.8 copy-done.9
  24.4 0.0 copy-start.10
  24.4 0.8 copy-done.10
  25.2 2.1 %places.1 = (f32[2896,128]{1,0:T(8,128)S(1)}, s32[1]{0:T(128)}) custom-call(s32[1]{0:T(128)} %bitcast.1.at_ref, s32[1,16384]{1,0:T(1,128)S(1)} %copy-done.8, s32[1,16384]{1,0:T(1,128)S(1)} %copy-done.9, s32[1,16384]{1,0:T(1,128)S(1)} %copy-done.10, f32[4,8,3072]{2,1,0:T(8,128)S(1)} %bitcast.16, f32[4,8,3072]{2,1,0:T(8,128)S(1)} %bitcast.18), custom_call_target="tpu_custom_call" | custom-call | flops 1 | bytes 1 | tf_op jit(solution)/shard_map/places/pallas_call | solution.py:615
  27.4 0.0 collective-permute-done.5.refs_3_
  27.4 1.2 %collective-permute-done.4.refs_2_ = f32[4,2048]{1,0:T(4,128)} collective-permute-done((f32[4,2048]{1,0:T(4,128)S(1)}, f32[4,2048]{1,0:T(4,128)}, u32[]{:S(2)}, u32[]{:S(2)}) %collective-permute-start.4) | collective-permute-done | bytes 32800 | tf_op jit(solution)/shard_map/ppermute | solution.py:605
  28.6 0.0 collective-permute-done.3.refs_1_
  28.6 0.8 collect.1.rest_1_.lines_ref
  29.4 0.0 all-to-all-done.in_ref
  29.4 1.0 %scan.1 = f32[16,16,768]{2,1,0:T(8,128)} custom-call(f32[16,24,768]{2,1,0:T(8,128)S(1)} %all-to-all-done.in_ref, f32[2896,128]{1,0:T(8,128)S(1)} %get-tuple-element.25.rest_0_.table_ref, f32[16,2048]{1,0:T(8,128)S(1)} %collect.1.rest_1_.lines_ref), custom_call_target="tpu_custom_call" | custom-call | flops 1 | bytes 1 | tf_op jit(solution)/shard_map/scan/pallas_call | solution.py:651
  30.4 7.0 %all-to-all-start.1 = ((f32[16,16,768]{2,1,0:T(8,128)}), f32[16,16,768]{2,1,0:T(8,128)S(1)}, u32[]{:S(2)}, u32[]{:S(2)}) async-start(f32[16,16,768]{2,1,0:T(8,128)} %scan.1), calls=%async_computation.1 | async-start | bytes 1572864 | tf_op jit(solution)/shard_map/all_to_all | solution.py:660
  37.4 1.3 %collective-permute-start.8 = (f32[4,8,3072]{2,1,0:T(8,128)}, f32[4,8,3072]{2,1,0:T(8,128)}, u32[]{:S(2)}, u32[]{:S(2)}) collective-permute-start(f32[4,8,3072]{2,1,0:T(8,128)} %bitcast.5.rm_ref.rm_hbm), channel_id=1, source_target_pairs={{16,0},{32,16},{48,32},{64,48},{80,64},{96,80},{112,96},{128,112},... | collective-permute-start | bytes 1179656 | tf_op jit(solution)/shard_map/ppermute | solution.py:579
  38.7 4.7 %spread.1.bundle_ref = f32[10,8,3072]{2,1,0:T(8,128)S(1)} custom-call(s32[1]{0:T(128)} %get-tuple-element.23.passes_ref, f32[2896,128]{1,0:T(8,128)S(1)} %get-tuple-element.25.rest_0_.table_ref, f32[16,2048]{1,0:T(8,128)S(1)} %collect.1.rest_1_.lines_ref), custom_call_target="tpu_custom_call" | custom-call | flops 1 | bytes 1 | tf_op jit(solution)/shard_map/spread/pallas_call | solution.py:634
  43.4 6.5 %all-to-all-done.1.back_ref = f32[16,16,768]{2,1,0:T(8,128)S(1)} async-done(((f32[16,16,768]{2,1,0:T(8,128)}), f32[16,16,768]{2,1,0:T(8,128)S(1)}, u32[]{:S(2)}, u32[]{:S(2)}) %all-to-all-start.1) | async-done | bytes 786464 | tf_op jit(solution)/shard_map/all_to_all | solution.py:660
  49.9 1.1 %edges.1 = (f32[24,3072]{1,0:T(8,128)}, f32[24,3072]{1,0:T(8,128)}) custom-call(f32[16,16,768]{2,1,0:T(8,128)S(1)} %all-to-all-done.1.back_ref, f32[10,8,3072]{2,1,0:T(8,128)S(1)} %spread.1.bundle_ref, f32[2896,128]{1,0:T(8,128)S(1)} %get-tuple-element.25.rest_0_.table_ref), custom_call_target="tpu_custom_call" | custom-call | flops 1 | bytes 1 | tf_op jit(solution)/shard_map/edges/pallas_call | solution.py:661
  51.0 2.8 %collective-permute-start.7 = (f32[24,3072]{1,0:T(8,128)}, f32[24,3072]{1,0:T(8,128)S(1)}, u32[]{:S(2)}, u32[]{:S(2)}) collective-permute-start(f32[24,3072]{1,0:T(8,128)} %get-tuple-element.27), channel_id=1, source_target_pairs={{1,0},{2,1},{3,2},{4,3},{5,4},{6,5},{7,6},{8,7},{9,8},{10,9},{11,1... | collective-permute-start | bytes 884744 | tf_op jit(solution)/shard_map/ppermute | solution.py:672
  53.8 0.1 collective-permute-start.6
  53.9 0.0 copy-start
  53.9 1.0 %copy-done = f32[1,4,8,3072]{3,2,1,0:T(8,128)S(1)} copy-done((f32[1,4,8,3072]{3,2,1,0:T(8,128)S(1)}, f32[1,4,8,3072]{3,2,1,0:T(8,128)}, u32[]{:S(2)}) %copy-start) | copy-done | bytes 393240
  54.9 0.0 copy-start.3
  54.9 1.0 %copy-done.3 = f32[1,4,8,3072]{3,2,1,0:T(8,128)S(1)} copy-done((f32[1,4,8,3072]{3,2,1,0:T(8,128)S(1)}, f32[1,4,8,3072]{3,2,1,0:T(8,128)}, u32[]{:S(2)}) %copy-start.3) | copy-done | bytes 393240
  55.9 0.0 copy-start.5
  55.9 1.0 %copy-done.5 = f32[1,4,8,3072]{3,2,1,0:T(8,128)S(1)} copy-done((f32[1,4,8,3072]{3,2,1,0:T(8,128)S(1)}, f32[1,4,8,3072]{3,2,1,0:T(8,128)}, u32[]{:S(2)}) %copy-start.5) | copy-done | bytes 393240
  56.9 0.0 copy-start.14
  56.9 0.1 fields.1.args_ref
  56.9 0.0 collective-permute-done.8.rm_next_ref
  57.0 1.9 %collective-permute-done.7.above_ref = f32[24,3072]{1,0:T(8,128)S(1)} collective-permute-done((f32[24,3072]{1,0:T(8,128)}, f32[24,3072]{1,0:T(8,128)S(1)}, u32[]{:S(2)}, u32[]{:S(2)}) %collective-permute-start.7) | collective-permute-done | bytes 294944 | tf_op jit(solution)/shard_map/ppermute | solution.py:672
  58.9 0.0 collective-permute-done.6.below_ref
  58.9 0.0 copy-done.14
  58.9 0.0 copy-start.6
  58.9 0.0 copy-start.7
  58.9 0.0 copy-start.13
  58.9 5.7 %images.1 = (f32[4,8,3072]{2,1,0:T(8,128)S(1)}, f32[4,8,3072]{2,1,0:T(8,128)S(1)}, f32[16,1,1152]{2,1,0:T(1,128)S(1)}) custom-call(s32[1]{0:T(128)} %bitcast.window_ref, s32[1]{0:T(128)} %bitcast.1.at_ref, s32[1]{0:T(128)} %get-tuple-element.23.passes_ref, f32[16,16,768]{2,1,0:T(8,128)S(1)} %all-to-all-done.1.back_ref, ...), custom_call_target="tpu_custom_call" | custom-call | flops 1 | bytes 1 | tf_op jit(solution)/shard_map/images/pallas_call | solution.py:684
  64.6 0.6 collective-permute-start.9
  65.2 15.3 %all_to_all.20.got_ref = f32[16,1,1152]{2,1,0:T(1,128)S(1)} all-to-all(f32[16,1,1152]{2,1,0:T(1,128)S(1)} %get-tuple-element.29), channel_id=1, replica_groups=mesh['tm'=16,'space'=16] {'space'}, dimensions={0} | all-to-all | bytes 147456 | tf_op jit(solution)/shard_map/all_to_all | solution.py:703
  80.5 12.4 %all_to_all.21.sums_ref = f32[16,1,128]{2,1,0:T(1,128)S(1)} all-to-all(f32[16,1,128]{2,1,0:T(1,128)S(1)} %get-tuple-element.30), channel_id=1, replica_groups=mesh['tm'=16,'space'=16] {'tm'}, dimensions={0} | all-to-all | bytes 16384 | tf_op jit(solution)/shard_map/all_to_all | solution.py:713
  92.9 0.0 collective-permute-done.9.image_ref
  92.9 0.0 copy-done.1
  92.9 0.0 copy-done.6
  92.9 0.0 copy-done.7
  93.0 0.0 copy-done.13
  93.0 2.5 %updates.1 = (f32[4,8,3072]{2,1,0:T(8,128)}, f32[1,1024]{1,0:T(1,128)}, f32[4,8,3072]{2,1,0:T(8,128)}, f32[4,8,3072]{2,1,0:T(8,128)}, f32[1,1024]{1,0:T(1,128)}, /*index=5*/f32[4,8,3072]{2,1,0:T(8,128)}) custom-call(s32[1]{0:T(128)} %bitcast.window_ref, f32[16,1,128]{2,1,0:T(1,128)S(1)} %all_to_all.21.sums_ref, f32[4,8,3072]{2,1,0:T(8,128)S(1)} %bitcast.20, ...), custom_call_target="tpu_custom_call" | custom-call | flops 1 | bytes 1 | tf_op jit(solution)/shard_map/updates/pallas_call | solution.py:716
  (4 shorter events, 0.0 us)
Async XLA Ops:
  3.0 7.8 %copy-start.11 = (f32[1,1024]{1,0:T(1,128)S(1)}, f32[1,1024]{1,0:T(1,128)}, u32[]{:S(2)}) copy-start(f32[1,1024]{1,0:T(1,128)} %ro_ref.3) | copy-start | bytes 12292
  3.0 7.8 %copy-start.12 = (f32[1,1024]{1,0:T(1,128)S(1)}, f32[1,1024]{1,0:T(1,128)}, u32[]{:S(2)}) copy-start(f32[1,1024]{1,0:T(1,128)} %ov_ref.3) | copy-start | bytes 12292
  3.0 20.5 %copy-start.2 = (f32[1,4,8,3072]{3,2,1,0:T(8,128)S(1)}, f32[1,4,8,3072]{3,2,1,0:T(8,128)}, u32[]{:S(2)}) copy-start(f32[1,4,8,3072]{3,2,1,0:T(8,128)} %param.13) | copy-start | bytes 1179652
  3.0 20.5 %copy-start.4 = (f32[1,4,8,3072]{3,2,1,0:T(8,128)S(1)}, f32[1,4,8,3072]{3,2,1,0:T(8,128)}, u32[]{:S(2)}) copy-start(f32[1,4,8,3072]{3,2,1,0:T(8,128)} %param.14) | copy-start | bytes 1179652
  3.0 20.5 %copy-start.8 = (s32[1,16384]{1,0:T(1,128)S(1)}, s32[1,16384]{1,0:T(1,128)}, u32[]{:S(2)}) copy-start(s32[1,16384]{1,0:T(1,128)} %brick_ref.1) | copy-start | bytes 196612
  3.0 26.4 %all-to-all-start = ((f32[16,24,768]{2,1,0:T(8,128)}), f32[16,24,768]{2,1,0:T(8,128)S(1)}, u32[]{:S(2)}, u32[]{:S(2)}) async-start(f32[16,24,768]{2,1,0:T(8,128)} %get-tuple-element.24), calls=%async_computation | async-start | bytes 2359296 | tf_op jit(solution)/shard_map/all_to_all | solution.py:577
  10.8 3.9 %collective-permute-start.2 = (f32[1,2048]{1,0:T(1,128)S(1)}, f32[1,2048]{1,0:T(1,128)S(1)}, u32[]{:S(2)}, u32[]{:S(2)}) collective-permute-start(f32[1,2048]{1,0:T(1,128)S(1)} %duals.1.refs_0_), channel_id=1, source_target_pairs={{0,3},{1,2},{2,1},{3,0},{4,7},{5,6},{6,5},{7,4},{8,11},{9,10},{10,... | collective-permute-start | bytes 24584 | tf_op jit(solution)/shard_map/ppermute | solution.py:592
  13.4 2.9 %collective-permute-start.1 = (f32[1,2048]{1,0:T(1,128)S(1)}, f32[1,2048]{1,0:T(1,128)S(1)}, u32[]{:S(2)}, u32[]{:S(2)}) collective-permute-start(f32[1,2048]{1,0:T(1,128)S(1)} %duals.1.refs_0_), channel_id=1, source_target_pairs={{0,2},{1,3},{2,0},{3,1},{4,6},{5,7},{6,4},{7,5},{8,10},{9,11},{10,... | collective-permute-start | bytes 24584 | tf_op jit(solution)/shard_map/ppermute | solution.py:592
  13.4 2.9 %collective-permute-start = (f32[1,2048]{1,0:T(1,128)S(1)}, f32[1,2048]{1,0:T(1,128)S(1)}, u32[]{:S(2)}, u32[]{:S(2)}) collective-permute-start(f32[1,2048]{1,0:T(1,128)S(1)} %duals.1.refs_0_), channel_id=1, source_target_pairs={{0,1},{1,0},{2,3},{3,2},{4,5},{5,4},{6,7},{7,6},{8,9},{9,8},{10,11... | collective-permute-start | bytes 24584 | tf_op jit(solution)/shard_map/ppermute | solution.py:592
  16.2 11.1 %collective-permute-start.5 = (f32[4,2048]{1,0:T(4,128)S(1)}, f32[4,2048]{1,0:T(4,128)}, u32[]{:S(2)}, u32[]{:S(2)}) collective-permute-start(f32[4,2048]{1,0:T(4,128)S(1)} %join.1.refs_0_), channel_id=1, source_target_pairs={{0,12},{1,13},{2,14},{3,15},{4,8},{5,9},{6,10},{7,11},{8,4},{9,5},... | collective-permute-start | bytes 98312 | tf_op jit(solution)/shard_map/ppermute | solution.py:605
  21.3 7.2 %collective-permute-start.4 = (f32[4,2048]{1,0:T(4,128)S(1)}, f32[4,2048]{1,0:T(4,128)}, u32[]{:S(2)}, u32[]{:S(2)}) collective-permute-start(f32[4,2048]{1,0:T(4,128)S(1)} %join.1.refs_0_), channel_id=1, source_target_pairs={{0,8},{1,9},{2,10},{3,11},{4,12},{5,13},{6,14},{7,15},{8,0},{9,1},... | collective-permute-start | bytes 98312 | tf_op jit(solution)/shard_map/ppermute | solution.py:605
  22.5 6.1 %collective-permute-start.3 = (f32[4,2048]{1,0:T(4,128)S(1)}, f32[4,2048]{1,0:T(4,128)}, u32[]{:S(2)}, u32[]{:S(2)}) collective-permute-start(f32[4,2048]{1,0:T(4,128)S(1)} %join.1.refs_0_), channel_id=1, source_target_pairs={{0,4},{1,5},{2,6},{3,7},{4,0},{5,1},{6,2},{7,3},{8,12},{9,13},{10,... | collective-permute-start | bytes 98312 | tf_op jit(solution)/shard_map/ppermute | solution.py:605
  23.5 0.8 copy-start.9
  24.4 0.8 copy-start.10
  30.4 19.5 %all-to-all-start.1 = ((f32[16,16,768]{2,1,0:T(8,128)}), f32[16,16,768]{2,1,0:T(8,128)S(1)}, u32[]{:S(2)}, u32[]{:S(2)}) async-start(f32[16,16,768]{2,1,0:T(8,128)} %scan.1), calls=%async_computation.1 | async-start | bytes 1572864 | tf_op jit(solution)/shard_map/all_to_all | solution.py:660
  37.4 19.6 %collective-permute-start.8 = (f32[4,8,3072]{2,1,0:T(8,128)}, f32[4,8,3072]{2,1,0:T(8,128)}, u32[]{:S(2)}, u32[]{:S(2)}) collective-permute-start(f32[4,8,3072]{2,1,0:T(8,128)} %bitcast.5.rm_ref.rm_hbm), channel_id=1, source_target_pairs={{16,0},{32,16},{48,32},{64,48},{80,64},{96,80},{112,96},{128,112},... | collective-permute-start | bytes 1179656 | tf_op jit(solution)/shard_map/ppermute | solution.py:579
  51.0 7.9 %collective-permute-start.7 = (f32[24,3072]{1,0:T(8,128)}, f32[24,3072]{1,0:T(8,128)S(1)}, u32[]{:S(2)}, u32[]{:S(2)}) collective-permute-start(f32[24,3072]{1,0:T(8,128)} %get-tuple-element.27), channel_id=1, source_target_pairs={{1,0},{2,1},{3,2},{4,3},{5,4},{6,5},{7,6},{8,7},{9,8},{10,9},{11,1... | collective-permute-start | bytes 884744 | tf_op jit(solution)/shard_map/ppermute | solution.py:672
  53.8 5.1 %collective-permute-start.6 = (f32[24,3072]{1,0:T(8,128)}, f32[24,3072]{1,0:T(8,128)}, u32[]{:S(2)}, u32[]{:S(2)}) collective-permute-start(f32[24,3072]{1,0:T(8,128)} %get-tuple-element.26.after_ref), channel_id=1, source_target_pairs={{0,1},{1,2},{2,3},{3,4},{4,5},{5,6},{6,7},{7,8},{8,9},{9,10},{10,1... | collective-permute-start | bytes 884744 | tf_op jit(solution)/shard_map/ppermute | solution.py:671
  53.9 1.0 %copy-start = (f32[1,4,8,3072]{3,2,1,0:T(8,128)S(1)}, f32[1,4,8,3072]{3,2,1,0:T(8,128)}, u32[]{:S(2)}) copy-start(f32[1,4,8,3072]{3,2,1,0:T(8,128)} %param.25) | copy-start | bytes 1179652
  54.9 1.0 %copy-start.3 = (f32[1,4,8,3072]{3,2,1,0:T(8,128)S(1)}, f32[1,4,8,3072]{3,2,1,0:T(8,128)}, u32[]{:S(2)}) copy-start(f32[1,4,8,3072]{3,2,1,0:T(8,128)} %param.13) | copy-start | bytes 1179652
  55.9 1.0 %copy-start.5 = (f32[1,4,8,3072]{3,2,1,0:T(8,128)S(1)}, f32[1,4,8,3072]{3,2,1,0:T(8,128)}, u32[]{:S(2)}) copy-start(f32[1,4,8,3072]{3,2,1,0:T(8,128)} %param.14) | copy-start | bytes 1179652
  56.9 2.0 %copy-start.14 = (f32[1,128]{1,0:T(1,128)S(1)}, f32[1,128]{1,0:T(1,128)}, u32[]{:S(2)}) copy-start(f32[1,128]{1,0:T(1,128)} %get-tuple-element.28.square_ref) | copy-start | bytes 1540
  58.9 34.0 %copy-start.1 = (f32[1,4,8,3072]{3,2,1,0:T(8,128)S(1)}, f32[1,4,8,3072]{3,2,1,0:T(8,128)}, u32[]{:S(2)}) copy-start(f32[1,4,8,3072]{3,2,1,0:T(8,128)} %param.25) | copy-start | bytes 1179652
  58.9 34.0 %copy-start.6 = (f32[1,4,8,3072]{3,2,1,0:T(8,128)S(1)}, f32[1,4,8,3072]{3,2,1,0:T(8,128)}, u32[]{:S(2)}) copy-start(f32[1,4,8,3072]{3,2,1,0:T(8,128)} %param.20) | copy-start | bytes 1179652
  58.9 34.0 %copy-start.7 = (f32[1,4,8,3072]{3,2,1,0:T(8,128)S(1)}, f32[1,4,8,3072]{3,2,1,0:T(8,128)}, u32[]{:S(2)}) copy-start(f32[1,4,8,3072]{3,2,1,0:T(8,128)} %param.22) | copy-start | bytes 1179652
  58.9 34.0 %copy-start.13 = (f32[1,1024]{1,0:T(1,128)S(1)}, f32[1,1024]{1,0:T(1,128)}, u32[]{:S(2)}) copy-start(f32[1,1024]{1,0:T(1,128)} %do_ref.1) | copy-start | bytes 12292
  64.6 28.3 %collective-permute-start.9 = (f32[4,8,3072]{2,1,0:T(8,128)S(1)}, f32[4,8,3072]{2,1,0:T(8,128)S(1)}, u32[]{:S(2)}, u32[]{:S(2)}) collective-permute-start(f32[4,8,3072]{2,1,0:T(8,128)S(1)} %get-tuple-element.31), channel_id=1, source_target_pairs={{0,16},{16,32},{32,48},{48,64},{64,80},{80,96},{96,112},{112,128},... | collective-permute-start | bytes 1179656 | tf_op jit(solution)/shard_map/ppermute | solution.py:702

commit v5 on v4

--- a/solution.py
+++ b/solution.py
@@ -59,19 +59,56 @@
         out_ref[place * levels : (place + 1) * levels] = ref[...]
 
 
-def pack_kernel(parts, rs_ref, rm_ref, mv_ref, out_ref, square_ref):
+def pack_kernel(parts, rs_hbm, rm_hbm, mv_hbm, cx_hbm, cy_hbm, out_hbm, square_hbm, rows_hbm,
+                rs_ref, rm_ref, mv_ref, cx_ref, cy_ref, out_ref, square_ref, rows_ref, in_sems, out_sems):
     levels, rows, columns = rs_ref.shape
     per_level = parts // levels
     width = columns // per_level
-    for part in range(parts):
-        level, piece = part // per_level, part % per_level
-        cols = slice(piece * width, (piece + 1) * width)
-        for place, ref in enumerate((rs_ref, rm_ref, mv_ref)):
-            out_ref[part, rows * place : rows * (place + 1), :] = ref[level, :, cols]
+    fields = ((rs_hbm, rs_ref), (rm_hbm, rm_ref), (mv_hbm, mv_ref))
+    loads = [
+        [
+            pltpu.make_async_copy(a.at[level], b.at[level], in_sems.at[level, place])
+            for place, (a, b) in enumerate(fields)
+        ]
+        for level in range(levels)
+    ]
+    winds = [
+        pltpu.make_async_copy(cx_hbm, cx_ref, in_sems.at[0, 3]),
+        pltpu.make_async_copy(cy_hbm, cy_ref, in_sems.at[1, 3]),
+    ]
+    for copies in loads + [winds]:
+        for copy in copies:
+            copy.start()
+    stores = []
     square = jnp.zeros((rows, columns), jnp.float32)
     for level in range(levels):
+        for copy in loads[level]:
+            copy.wait()
+        for piece in range(per_level):
+            part = level * per_level + piece
+            cols = slice(piece * width, (piece + 1) * width)
+            for place, (_, ref) in enumerate(fields):
+                out_ref[part, rows * place : rows * (place + 1), :] = ref[level, :, cols]
+        mine = pl.ds(level * per_level, per_level)
+        stores.append(pltpu.make_async_copy(out_ref.at[mine], out_hbm.at[mine], out_sems.at[level]))
+        stores[-1].start()
         square += rm_ref[level] * rm_ref[level]
     square_ref[...] = jnp.broadcast_to(jnp.sum(square), square_ref.shape)
+    stores.append(pltpu.make_async_copy(square_ref, square_hbm, out_sems.at[levels]))
+    stores[-1].start()
+    for copy in winds:
+        copy.wait()
+    for place, (ref, pair) in enumerate((
+        (cx_ref, (rows - 1, 0)), (cy_ref, (rows - 1, 0)), (cy_ref, (rows - 2, 1)),
+    )):
+        for half, row in enumerate(pair):
+            for level in range(levels):
+                at = 8 * place + 4 * half + level
+                rows_ref[at : at + 1, :] = ref[level, row : row + 1, :]
+    stores.append(pltpu.make_async_copy(rows_ref, rows_hbm, out_sems.at[levels + 1]))
+    stores[-1].start()
+    for copy in stores:
+        copy.wait()
 
 
 def scan_kernel(in_ref, *rest):
@@ -133,8 +170,11 @@
     from_in = jnp.maximum(jnp.where(is_up, -cy_in, cy_in), 0.0) * dual_in
     kept = middle - (own * dual + east_of(west * dual) + west_of(east * dual) + from_in)
     for place, value in enumerate((incr, one, outer, outer * kept, outer * dual)):
-        up_ref[4 * place : 4 * place + 4, :] = value[0:4]
-        down_ref[4 * place : 4 * place + 4, :] = value[4:8]
+        for half in range(2):
+            at = slice(20 * half + 4 * place, 20 * half + 4 * place + 4)
+            cols = slice(half * up_ref.shape[1], (half + 1) * up_ref.shape[1])
+            up_ref[at, :] = value[0:4, cols]
+            down_ref[at, :] = value[4:8, cols]
 
 
 def slots_held(rank_ref, k, half, first):
@@ -198,7 +238,7 @@
     ], axis=0)
 
 
-def place_kernel(columns, at_ref, brick_ref, cell_ref, step_ref, cx_ref, cy_ref,
+def place_kernel(columns, at_ref, brick_ref, cell_ref, step_ref, rows_ref,
                  table_ref, passes_ref, brick_s, cell_s, step_s, groups_s):
     chunks = brick_s.shape[0]
     rank_ref, code_ref = brick_s, cell_s
@@ -229,16 +269,10 @@
     fold(table_ref, places["code"], code_ref[...].astype(jnp.float32))
     table_ref[places["groups"] : places["groups"] + chunks, :] = groups_s[...].astype(jnp.float32)
     passes_ref[0] = (jnp.max(count.astype(jnp.float32)).astype(jnp.int32) + SLOTS - 1) // SLOTS
-    rows = cx_ref.shape[1]
-    for place, (ref, pair) in enumerate((
-        (cx_ref, (rows - 1, 0)), (cy_ref, (rows - 1, 0)), (cy_ref, (rows - 2, 1)),
-    )):
-        edge = jnp.concatenate(
-            [ref[level, row : row + 1, :] for row in pair for level in range(cx_ref.shape[0])], axis=0
-        )
+    for place in range(3):
         for g in range(lane_groups):
             at = places["edges"] + (place * lane_groups + g) * 8
-            table_ref[at : at + 8, :] = edge[:, g * LANES : (g + 1) * LANES]
+            table_ref[at : at + 8, :] = rows_ref[8 * place : 8 * place + 8, g * LANES : (g + 1) * LANES]
 
 
 def in_column(columns, values, which):
@@ -252,8 +286,10 @@
     return high, low
 
 
-def spread_kernel(passes_ref, table_ref, lines_ref, bundle_ref,
-                  rank_ref, code_ref, again_codes, groups_ref, hot_s, high_s, low_s, total):
+def spread_kernel(passes_ref, table_ref, lines_ref, rm_hbm, bundle_ref, rm_out,
+                  rank_ref, code_ref, again_codes, groups_ref, hot_s, high_s, low_s, total, rm_s, sems):
+    rm_in = pltpu.make_async_copy(rm_hbm, rm_s, sems.at[0])
+    rm_in.start()
     chunks = rank_ref.shape[0]
     _, rows, columns = bundle_ref.shape
     lane_groups = columns // LANES
@@ -297,6 +333,9 @@
             hot_s[...], high_s[...], preferred_element_type=jnp.float32
         ) + jnp.dot(hot_s[...], low_s[...], preferred_element_type=jnp.float32)
 
+    rm_in.wait()
+    rm_back = pltpu.make_async_copy(rm_s, rm_out, sems.at[1])
+    rm_back.start()
     total[...] = add_up(0, table_ref)
 
     def one_more(number, carry):
@@ -317,6 +356,7 @@
         for place, row in enumerate((rows - 1, 0)):
             at = 4 * place + level
             rows_ref[at : at + 1, :] = bundle_ref[levels + level, row : row + 1, :]
+    rm_back.wait()
 
 
 def west_of(v):
@@ -377,7 +417,12 @@
         coeffs = weights_of(args_ref[level], args_ref[levels + level])
         south, north = coeffs[3], coeffs[4]
         low, high = (
-            [held * ref[4 * i + level : 4 * i + level + 1, :] for i in range(5)]
+            [
+                held * jnp.concatenate(
+                    [ref[at : at + 1, :] for at in (4 * i + level, 20 + 4 * i + level)], axis=1
+                )
+                for i in range(5)
+            ]
             for ref, held in ((below_ref, has_below), (above_ref, has_above))
         )
         after_one = forward(
@@ -477,7 +522,7 @@
         [bundle_ref[2 * levels + 1, :, k * CHUNK : (k + 1) * CHUNK] for k in range(chunks // 8)], axis=0
     )
     image_obs = jnp.where(rank_ref[...] >= 0, resid + observed, 0.0)
-    square = jnp.where(window == 0, square_ref[...], 0.0)
+    square = jnp.where(window == 0, square_ref[0:1, :], 0.0)
     all_projected = jnp.sum(projected) + jnp.sum(resid * image_obs) + square
     all_curvature = jnp.sum(curvature) + jnp.sum(image_obs * image_obs) + square
     lane = lax.broadcasted_iota(jnp.int32, (1, LANES), 1)
@@ -565,18 +610,25 @@
     downward = [((i + 1) % bricks, i) for i in range(bricks)]
     later = [(i, (i + 1) % windows) for i in range(windows)]
 
-    packed, square = pl.pallas_call(
+    packed, square, edge_rows = pl.pallas_call(
         functools.partial(pack_kernel, windows),
-        out_shape=(f32(windows, 3 * rows, width), f32(1, LANES)),
-        in_specs=[VMEM] * 3,
-        out_specs=(VMEM, VMEM),
+        out_shape=(f32(windows, 3 * rows, width), f32(8, LANES), f32(24, columns)),
+        in_specs=[HBM] * 5,
+        out_specs=(HBM, HBM, HBM),
+        scratch_shapes=[
+            *[pltpu.VMEM((levels, rows, columns), jnp.float32)] * 5,
+            pltpu.VMEM((windows, 3 * rows, width), jnp.float32),
+            pltpu.VMEM((8, LANES), jnp.float32),
+            pltpu.VMEM((24, columns), jnp.float32),
+            pltpu.SemaphoreType.DMA((levels, 4)),
+            pltpu.SemaphoreType.DMA((levels + 2,)),
+        ],
         compiler_params=params(60),
         cost_estimate=cost(1, 1),
         name="pack",
-    )(rs, rm, mv)
+    )(rs, rm, mv, cx, cy)
     windows_of = lax.all_to_all(packed, "tm", 0, 0)
 
-    rm_next = lax.ppermute(rm, "tm", [(i + 1, i) for i in range(windows - 1)])
     near = pl.pallas_call(
         duals_kernel,
         out_shape=f32(1, 2 * CHUNK),
@@ -615,13 +667,13 @@
     table, passes = pl.pallas_call(
         functools.partial(place_kernel, columns),
         out_shape=(f32(table_rows, LANES), i32(1)),
-        in_specs=[SMEM] + [VMEM] * 5,
+        in_specs=[SMEM] + [VMEM] * 4,
         out_specs=(VMEM, SMEM),
         scratch_shapes=[table_s, table_s, table_s, groups_s],
         compiler_params=params(8),
         cost_estimate=cost(1, 1),
         name="places",
-    )(at, obs_brick, obs_cell, obs_step, cx, cy)
+    )(at, obs_brick, obs_cell, obs_step, edge_rows)
     lines = pl.pallas_call(
         collect_kernel,
         out_shape=f32(blocks, 2 * CHUNK),
@@ -631,22 +683,25 @@
         cost_estimate=cost(1, 1),
         name="collect",
     )(at, near, *far)
-    bundle = pl.pallas_call(
+    bundle, relayed = pl.pallas_call(
         spread_kernel,
-        out_shape=f32(2 * levels + 2, rows, columns),
-        in_specs=[SMEM] + [VMEM] * 2,
-        out_specs=VMEM,
+        out_shape=(f32(2 * levels + 2, rows, columns), f32(levels, rows, columns)),
+        in_specs=[SMEM] + [VMEM] * 2 + [HBM],
+        out_specs=(VMEM, HBM),
         scratch_shapes=[
             table_s, table_s, codes_s, groups_s,
             pltpu.VMEM((groups, slots), jnp.bfloat16),
             pltpu.VMEM((slots, 2 * LANES), jnp.bfloat16),
             pltpu.VMEM((slots, 2 * LANES), jnp.bfloat16),
             pltpu.VMEM((groups, 2 * LANES), jnp.float32),
+            pltpu.VMEM((levels, rows, columns), jnp.float32),
+            pltpu.SemaphoreType.DMA((2,)),
         ],
         compiler_params=params(24),
         cost_estimate=cost(1, 1),
         name="spread",
-    )(passes, table, lines)
+    )(passes, table, lines, rm)
+    rm_next = lax.ppermute(relayed, "tm", [(i + 1, i) for i in range(windows - 1)])
 
     summed = pl.pallas_call(
         scan_kernel,
@@ -660,7 +715,7 @@
     back = lax.all_to_all(summed, "tm", 0, 0)
     up, down = pl.pallas_call(
         functools.partial(edge_kernel, levels, places["edges"]),
-        out_shape=(f32(24, columns), f32(24, columns)),
+        out_shape=(f32(40, columns // 2), f32(40, columns // 2)),
         in_specs=[VMEM, VMEM, VMEM],
         out_specs=(VMEM, VMEM),
         scratch_shapes=[pltpu.VMEM((32, columns), jnp.float32)],

time: 96.4 us -> 94.4 us (0.979)
  blocking collectives: 27.7 us -> 26.4 us
    ppermute x6, waiting for transfers between devices: 3.58 us -> 5.28 us  [body(): lax.ppermute(near, 'space', [(i, i ^ distance * k) for i in range(bricks)])]
    all_to_all x1, waiting for transfers between devices: 6.51 us -> 5.31 us  [body(): back = lax.all_to_all(summed, 'tm', 0, 0)]
    ppermute x1, waiting for transfers between devices: 1.93 us -> 0.82 us  [body(): above = lax.ppermute(down, 'space', downward)]
    unnamed x30 -> x32, local copies, waits for them, and re-layouts: 4.71 us -> 4.05 us
  transfers between devices with their start and end apart: 12 -> 12, of which waited for: 5 -> 6; matrix products, arithmetic and copies ran while one was open for 0% -> 0% of each run, Pallas kernels for 9% -> 8%
where the time goes in v5:
time: 94.4 us; the launch traced here: 93.8 us
  starting transfers between devices  30.5 us (32%)
  blocking collectives  26.4 us (28%)
  Pallas kernels  19.8 us (21%)
  waiting for transfers between devices  12 us (13%)
  local copies, waits for them, and re-layouts  4.05 us (4%)
  between operations  1.04 us (1%)
    all_to_all x1, blocking collectives, body(): got = lax.all_to_all(sent, 'space', 0, 0)  14.5 us
    all_to_all x1, blocking collectives, body(): all_sums = lax.all_to_all(sums, 'tm', 0, 0)  11.9 us
    ppermute x6, starting transfers between devices, body(): lax.ppermute(near, 'space', [(i, i ^ distance * k) for i in range(bricks)])  10.4 us
    all_to_all x1, starting transfers between devices, body(): windows_of = lax.all_to_all(packed, 'tm', 0, 0)  7.73 us
    all_to_all x1, starting transfers between devices, body(): back = lax.all_to_all(summed, 'tm', 0, 0)  6.86 us
    pallas_call x1, Pallas kernels, body(): pl.pallas_call(functools.partial(image_kernel, windows, bricks), out_shap...  6.09 us
    all_to_all x1, waiting for transfers between devices, body(): back = lax.all_to_all(summed, 'tm', 0, 0)  5.31 us
    ppermute x6, waiting for transfers between devices, body(): lax.ppermute(near, 'space', [(i, i ^ distance * k) for i in range(bricks)])  5.28 us
  transfers between devices with their start and end apart: 12, of which 6 were waited for; matrix products, arithmetic and copies ran while one was open for 0% of the time, Pallas kernels for 8%

profile of v5, /device:TPU:1, one launch (start us, length us, event | category | flops | bytes accessed | tf_op | source)
XLA Modules:
  0.0 93.8 jit_solution(13508562972245588318)
XLA Ops:
  0.6 2.6 %pack.1 = (f32[16,24,768]{2,1,0:T(8,128)}, f32[8,128]{1,0:T(8,128)}, f32[24,3072]{1,0:T(8,128)}) custom-call(f32[4,8,3072]{2,1,0:T(8,128)} %bitcast.13, f32[4,8,3072]{2,1,0:T(8,128)} %bitcast.16, f32[4,8,3072]{2,1,0:T(8,128)} %bitcast.25, f32[4,8,3072]{2,1,0:T(8,128)} %bitcast.19, f32[4,8,3072]{2,1,0:T(8,128)} %bitcast.21), custom_call_target="tpu_custom_call" | custom-call | flops 1 | bytes 1 | tf_op jit(solution)/shard_map/pack/pallas_call | solution.py:613
  3.2 0.0 copy-start.12
  3.2 0.0 copy-start.13
  3.2 0.0 copy-start.8
  3.2 0.0 copy-start.9
  3.3 0.0 copy-start.10
  3.3 0.0 copy-start.11
  3.3 7.7 %all-to-all-start = ((f32[16,24,768]{2,1,0:T(8,128)}), f32[16,24,768]{2,1,0:T(8,128)S(1)}, u32[]{:S(2)}, u32[]{:S(2)}) async-start(f32[16,24,768]{2,1,0:T(8,128)} %get-tuple-element.28), calls=%async_computation | async-start | bytes 2359296 | tf_op jit(solution)/shard_map/all_to_all | solution.py:630
  11.0 0.0 copy-done.12
  11.0 0.0 copy-done.13
  11.1 2.6 %collective-permute-start.2 = (f32[1,2048]{1,0:T(1,128)S(1)}, f32[1,2048]{1,0:T(1,128)S(1)}, u32[]{:S(2)}, u32[]{:S(2)}) collective-permute-start(f32[1,2048]{1,0:T(1,128)S(1)} %duals.1.refs_0_), channel_id=1, source_target_pairs={{0,3},{1,2},{2,1},{3,0},{4,7},{5,6},{6,5},{7,4},{8,11},{9,10},{10,... | collective-permute-start | bytes 24584 | tf_op jit(solution)/shard_map/ppermute | solution.py:644
  13.6 0.0 collective-permute-start.1
  13.6 0.5 collective-permute-start
  14.1 0.8 collective-permute-done.2.refs_3_
  15.0 1.5 %collective-permute-done.1.refs_2_ = f32[1,2048]{1,0:T(1,128)S(1)} collective-permute-done((f32[1,2048]{1,0:T(1,128)S(1)}, f32[1,2048]{1,0:T(1,128)S(1)}, u32[]{:S(2)}, u32[]{:S(2)}) %collective-permute-start.1) | collective-permute-done | bytes 8224 | tf_op jit(solution)/shard_map/ppermute | solution.py:644
  16.5 0.0 collective-permute-done.refs_1_
  16.5 5.1 %collective-permute-start.5 = (f32[4,2048]{1,0:T(4,128)S(1)}, f32[4,2048]{1,0:T(4,128)S(1)}, u32[]{:S(2)}, u32[]{:S(2)}) collective-permute-start(f32[4,2048]{1,0:T(4,128)S(1)} %join.1.refs_0_), channel_id=1, source_target_pairs={{0,12},{1,13},{2,14},{3,15},{4,8},{5,9},{6,10},{7,11},{8,4},{9,5},... | collective-permute-start | bytes 98312 | tf_op jit(solution)/shard_map/ppermute | solution.py:657
  21.6 1.2 %collective-permute-start.4 = (f32[4,2048]{1,0:T(4,128)S(1)}, f32[4,2048]{1,0:T(4,128)S(1)}, u32[]{:S(2)}, u32[]{:S(2)}) collective-permute-start(f32[4,2048]{1,0:T(4,128)S(1)} %join.1.refs_0_), channel_id=1, source_target_pairs={{0,8},{1,9},{2,10},{3,11},{4,12},{5,13},{6,14},{7,15},{8,0},{9,1},... | collective-permute-start | bytes 98312 | tf_op jit(solution)/shard_map/ppermute | solution.py:657
  22.8 1.0 %collective-permute-start.3 = (f32[4,2048]{1,0:T(4,128)S(1)}, f32[4,2048]{1,0:T(4,128)S(1)}, u32[]{:S(2)}, u32[]{:S(2)}) collective-permute-start(f32[4,2048]{1,0:T(4,128)S(1)} %join.1.refs_0_), channel_id=1, source_target_pairs={{0,4},{1,5},{2,6},{3,7},{4,0},{5,1},{6,2},{7,3},{8,12},{9,13},{10,... | collective-permute-start | bytes 98312 | tf_op jit(solution)/shard_map/ppermute | solution.py:657
  23.8 0.0 copy-done.8
  23.8 0.0 copy-done.9
  23.8 0.0 copy-done.10
  23.8 0.0 copy-done.11
  23.8 2.1 %places.1 = (f32[2896,128]{1,0:T(8,128)S(1)}, s32[1]{0:T(128)}) custom-call(s32[1]{0:T(128)} %bitcast.1.at_ref, s32[1,16384]{1,0:T(1,128)S(1)} %copy-done.9, s32[1,16384]{1,0:T(1,128)S(1)} %copy-done.10, s32[1,16384]{1,0:T(1,128)S(1)} %copy-done.11, f32[24,3072]{1,0:T(8,128)S(1)} %copy-done.8), custom_call_target="tpu_custom_call" | custom-call | flops 1 | bytes 1 | tf_op jit(solution)/shard_map/places/pallas_call | solution.py:667
  25.9 0.0 collective-permute-done.5.refs_3_
  25.9 2.9 %collective-permute-done.4.refs_2_ = f32[4,2048]{1,0:T(4,128)S(1)} collective-permute-done((f32[4,2048]{1,0:T(4,128)S(1)}, f32[4,2048]{1,0:T(4,128)S(1)}, u32[]{:S(2)}, u32[]{:S(2)}) %collective-permute-start.4) | collective-permute-done | bytes 32800 | tf_op jit(solution)/shard_map/ppermute | solution.py:657
  28.8 0.0 collective-permute-done.3.refs_1_
  28.9 0.0 all-to-all-done.in_ref
  28.9 1.0 %scan.1 = f32[16,16,768]{2,1,0:T(8,128)} custom-call(f32[16,24,768]{2,1,0:T(8,128)S(1)} %all-to-all-done.in_ref, f32[2896,128]{1,0:T(8,128)S(1)} %get-tuple-element.29.rest_0_.table_ref, f32[16,2048]{1,0:T(8,128)S(1)} %collect.1.rest_1_.lines_ref), custom_call_target="tpu_custom_call" | custom-call | flops 1 | bytes 1 | tf_op jit(solution)/shard_map/scan/pallas_call | solution.py:706
  29.9 6.9 %all-to-all-start.1 = ((f32[16,16,768]{2,1,0:T(8,128)}), f32[16,16,768]{2,1,0:T(8,128)S(1)}, u32[]{:S(2)}, u32[]{:S(2)}) async-start(f32[16,16,768]{2,1,0:T(8,128)} %scan.1), calls=%async_computation.1 | async-start | bytes 1572864 | tf_op jit(solution)/shard_map/all_to_all | solution.py:715
  36.7 0.0 copy-start.2
  36.8 1.0 %copy-done.2 = f32[1,4,8,3072]{3,2,1,0:T(8,128)S(1)} copy-done((f32[1,4,8,3072]{3,2,1,0:T(8,128)S(1)}, f32[1,4,8,3072]{3,2,1,0:T(8,128)}, u32[]{:S(2)}) %copy-start.2) | copy-done | bytes 393240
  37.7 4.7 %spread.1 = (f32[10,8,3072]{2,1,0:T(8,128)S(1)}, f32[4,8,3072]{2,1,0:T(8,128)}) custom-call(s32[1]{0:T(128)} %get-tuple-element.27.passes_ref, f32[2896,128]{1,0:T(8,128)S(1)} %get-tuple-element.29.rest_0_.table_ref, f32[16,2048]{1,0:T(8,128)S(1)} %collect.1.rest_1_.lines_ref, f32[4,8,3072]{2,1,0:T(8,128)S(1)} %bitcast.17), custom_call_target="tpu_custom_call" | custom-call | flops 1 | bytes 1 | tf_op jit(solution)/shard_map/spread/pallas_call | solution.py:686
  42.5 1.5 %collective-permute-start.8 = (f32[4,8,3072]{2,1,0:T(8,128)}, f32[4,8,3072]{2,1,0:T(8,128)}, u32[]{:S(2)}, u32[]{:S(2)}) collective-permute-start(f32[4,8,3072]{2,1,0:T(8,128)} %get-tuple-element.33), channel_id=1, source_target_pairs={{16,0},{32,16},{48,32},{64,48},{80,64},{96,80},{112,96},{128,112},... | collective-permute-start | bytes 1179656 | tf_op jit(solution)/shard_map/ppermute | solution.py:704
  43.9 5.3 %all-to-all-done.1.back_ref = f32[16,16,768]{2,1,0:T(8,128)S(1)} async-done(((f32[16,16,768]{2,1,0:T(8,128)}), f32[16,16,768]{2,1,0:T(8,128)S(1)}, u32[]{:S(2)}, u32[]{:S(2)}) %all-to-all-start.1) | async-done | bytes 786464 | tf_op jit(solution)/shard_map/all_to_all | solution.py:715
  49.2 1.0 %edges.1 = (f32[40,1536]{1,0:T(8,128)S(1)}, f32[40,1536]{1,0:T(8,128)}) custom-call(f32[16,16,768]{2,1,0:T(8,128)S(1)} %all-to-all-done.1.back_ref, f32[10,8,3072]{2,1,0:T(8,128)S(1)} %get-tuple-element.30.bundle_ref, f32[2896,128]{1,0:T(8,128)S(1)} %get-tuple-element.29.rest_0_.table_ref), custom_call_target="tpu_custom_call" | custom-call | flops 1 | bytes 1 | tf_op jit(solution)/shard_map/edges/pallas_call | solution.py:716
  50.3 2.8 %collective-permute-start.7 = (f32[40,1536]{1,0:T(8,128)}, f32[40,1536]{1,0:T(8,128)}, u32[]{:S(2)}, u32[]{:S(2)}) collective-permute-start(f32[40,1536]{1,0:T(8,128)} %get-tuple-element.32), channel_id=1, source_target_pairs={{1,0},{2,1},{3,2},{4,3},{5,4},{6,5},{7,6},{8,7},{9,8},{10,9},{11,1... | collective-permute-start | bytes 737288 | tf_op jit(solution)/shard_map/ppermute | solution.py:727
  53.0 0.1 collective-permute-start.6
  53.1 0.0 copy-start
  53.1 1.0 %copy-done = f32[1,4,8,3072]{3,2,1,0:T(8,128)S(1)} copy-done((f32[1,4,8,3072]{3,2,1,0:T(8,128)S(1)}, f32[1,4,8,3072]{3,2,1,0:T(8,128)}, u32[]{:S(2)}) %copy-start) | copy-done | bytes 393240
  54.1 0.0 copy-start.4
  54.1 1.0 %copy-done.4 = f32[1,4,8,3072]{3,2,1,0:T(8,128)S(1)} copy-done((f32[1,4,8,3072]{3,2,1,0:T(8,128)S(1)}, f32[1,4,8,3072]{3,2,1,0:T(8,128)}, u32[]{:S(2)}) %copy-start.4) | copy-done | bytes 393240
  55.1 0.0 copy-start.5
  55.1 1.0 %copy-done.5 = f32[1,4,8,3072]{3,2,1,0:T(8,128)S(1)} copy-done((f32[1,4,8,3072]{3,2,1,0:T(8,128)S(1)}, f32[1,4,8,3072]{3,2,1,0:T(8,128)}, u32[]{:S(2)}) %copy-start.5) | copy-done | bytes 393240
  56.1 0.1 fields.1.args_ref
  56.2 0.6 collective-permute-done.8.rm_next_ref
  56.8 0.8 collective-permute-done.7.above_ref
  57.6 0.0 collective-permute-done.6.below_ref
  57.6 0.0 copy-done.15
  57.6 0.0 copy-start.3
  57.6 0.0 copy-start.6
  57.6 0.0 copy-start.7
  57.7 0.0 copy-start.14
  57.7 6.1 %images.1 = (f32[4,8,3072]{2,1,0:T(8,128)S(1)}, f32[4,8,3072]{2,1,0:T(8,128)S(1)}, f32[16,1,1152]{2,1,0:T(1,128)S(1)}) custom-call(s32[1]{0:T(128)} %bitcast.window_ref, s32[1]{0:T(128)} %bitcast.1.at_ref, s32[1]{0:T(128)} %get-tuple-element.27.passes_ref, f32[16,16,768]{2,1,0:T(8,128)S(1)} %all-to-all-done.1.back_ref, ...), custom_call_target="tpu_custom_call" | custom-call | flops 1 | bytes 1 | tf_op jit(solution)/shard_map/images/pallas_call | solution.py:739
  63.8 1.2 %collective-permute-start.9 = (f32[4,8,3072]{2,1,0:T(8,128)S(1)}, f32[4,8,3072]{2,1,0:T(8,128)S(1)}, u32[]{:S(2)}, u32[]{:S(2)}) collective-permute-start(f32[4,8,3072]{2,1,0:T(8,128)S(1)} %get-tuple-element.37), channel_id=1, source_target_pairs={{0,16},{16,32},{32,48},{48,64},{64,80},{80,96},{96,112},{112,128},... | collective-permute-start | bytes 1179656 | tf_op jit(solution)/shard_map/ppermute | solution.py:757
  65.0 14.5 %all_to_all.20.got_ref = f32[16,1,1152]{2,1,0:T(1,128)S(1)} all-to-all(f32[16,1,1152]{2,1,0:T(1,128)S(1)} %get-tuple-element.35), channel_id=1, replica_groups=mesh['tm'=16,'space'=16] {'space'}, dimensions={0} | all-to-all | bytes 147456 | tf_op jit(solution)/shard_map/all_to_all | solution.py:758
  79.5 11.9 %all_to_all.21.sums_ref = f32[16,1,128]{2,1,0:T(1,128)S(1)} all-to-all(f32[16,1,128]{2,1,0:T(1,128)S(1)} %get-tuple-element.36), channel_id=1, replica_groups=mesh['tm'=16,'space'=16] {'tm'}, dimensions={0} | all-to-all | bytes 16384 | tf_op jit(solution)/shard_map/all_to_all | solution.py:768
  91.4 0.0 collective-permute-done.9.image_ref
  91.4 0.0 copy-done.1
  91.4 0.0 copy-done.3
  91.4 0.0 copy-done.6
  91.4 0.0 copy-done.7
  91.4 0.0 copy-done.14
  91.4 2.2 %updates.1 = (f32[4,8,3072]{2,1,0:T(8,128)}, f32[1,1024]{1,0:T(1,128)}, f32[4,8,3072]{2,1,0:T(8,128)}, f32[4,8,3072]{2,1,0:T(8,128)}, f32[1,1024]{1,0:T(1,128)}, /*index=5*/f32[4,8,3072]{2,1,0:T(8,128)}) custom-call(s32[1]{0:T(128)} %bitcast.window_ref, f32[16,1,128]{2,1,0:T(1,128)S(1)} %all_to_all.21.sums_ref, f32[4,8,3072]{2,1,0:T(8,128)S(1)} %bitcast.23, ...), custom_call_target="tpu_custom_call" | custom-call | flops 1 | bytes 1 | tf_op jit(solution)/shard_map/updates/pallas_call | solution.py:771
  (6 shorter events, 0.1 us)
Async XLA Ops:
  3.2 7.8 %copy-start.12 = (f32[1,1024]{1,0:T(1,128)S(1)}, f32[1,1024]{1,0:T(1,128)}, u32[]{:S(2)}) copy-start(f32[1,1024]{1,0:T(1,128)} %ro_ref.3) | copy-start | bytes 12292
  3.2 7.8 %copy-start.13 = (f32[1,1024]{1,0:T(1,128)S(1)}, f32[1,1024]{1,0:T(1,128)}, u32[]{:S(2)}) copy-start(f32[1,1024]{1,0:T(1,128)} %ov_ref.3) | copy-start | bytes 12292
  3.2 20.6 %copy-start.8 = (f32[24,3072]{1,0:T(8,128)S(1)}, f32[24,3072]{1,0:T(8,128)}, u32[]{:S(2)}) copy-start(f32[24,3072]{1,0:T(8,128)} %get-tuple-element.26.rows_ref) | copy-start | bytes 884740
  3.2 20.6 %copy-start.9 = (s32[1,16384]{1,0:T(1,128)S(1)}, s32[1,16384]{1,0:T(1,128)}, u32[]{:S(2)}) copy-start(s32[1,16384]{1,0:T(1,128)} %brick_ref.1) | copy-start | bytes 196612
  3.3 20.5 %copy-start.10 = (s32[1,16384]{1,0:T(1,128)S(1)}, s32[1,16384]{1,0:T(1,128)}, u32[]{:S(2)}) copy-start(s32[1,16384]{1,0:T(1,128)} %cell_ref.1) | copy-start | bytes 196612
  3.3 20.5 %copy-start.11 = (s32[1,16384]{1,0:T(1,128)S(1)}, s32[1,16384]{1,0:T(1,128)}, u32[]{:S(2)}) copy-start(s32[1,16384]{1,0:T(1,128)} %step_ref.1) | copy-start | bytes 196612
  3.3 25.6 %all-to-all-start = ((f32[16,24,768]{2,1,0:T(8,128)}), f32[16,24,768]{2,1,0:T(8,128)S(1)}, u32[]{:S(2)}, u32[]{:S(2)}) async-start(f32[16,24,768]{2,1,0:T(8,128)} %get-tuple-element.28), calls=%async_computation | async-start | bytes 2359296 | tf_op jit(solution)/shard_map/all_to_all | solution.py:630
  11.1 3.9 %collective-permute-start.2 = (f32[1,2048]{1,0:T(1,128)S(1)}, f32[1,2048]{1,0:T(1,128)S(1)}, u32[]{:S(2)}, u32[]{:S(2)}) collective-permute-start(f32[1,2048]{1,0:T(1,128)S(1)} %duals.1.refs_0_), channel_id=1, source_target_pairs={{0,3},{1,2},{2,1},{3,0},{4,7},{5,6},{6,5},{7,4},{8,11},{9,10},{10,... | collective-permute-start | bytes 24584 | tf_op jit(solution)/shard_map/ppermute | solution.py:644
  13.6 2.9 %collective-permute-start.1 = (f32[1,2048]{1,0:T(1,128)S(1)}, f32[1,2048]{1,0:T(1,128)S(1)}, u32[]{:S(2)}, u32[]{:S(2)}) collective-permute-start(f32[1,2048]{1,0:T(1,128)S(1)} %duals.1.refs_0_), channel_id=1, source_target_pairs={{0,2},{1,3},{2,0},{3,1},{4,6},{5,7},{6,4},{7,5},{8,10},{9,11},{10,... | collective-permute-start | bytes 24584 | tf_op jit(solution)/shard_map/ppermute | solution.py:644
  13.6 2.9 %collective-permute-start = (f32[1,2048]{1,0:T(1,128)S(1)}, f32[1,2048]{1,0:T(1,128)S(1)}, u32[]{:S(2)}, u32[]{:S(2)}) collective-permute-start(f32[1,2048]{1,0:T(1,128)S(1)} %duals.1.refs_0_), channel_id=1, source_target_pairs={{0,1},{1,0},{2,3},{3,2},{4,5},{5,4},{6,7},{7,6},{8,9},{9,8},{10,11... | collective-permute-start | bytes 24584 | tf_op jit(solution)/shard_map/ppermute | solution.py:644
  16.5 9.4 %collective-permute-start.5 = (f32[4,2048]{1,0:T(4,128)S(1)}, f32[4,2048]{1,0:T(4,128)S(1)}, u32[]{:S(2)}, u32[]{:S(2)}) collective-permute-start(f32[4,2048]{1,0:T(4,128)S(1)} %join.1.refs_0_), channel_id=1, source_target_pairs={{0,12},{1,13},{2,14},{3,15},{4,8},{5,9},{6,10},{7,11},{8,4},{9,5},... | collective-permute-start | bytes 98312 | tf_op jit(solution)/shard_map/ppermute | solution.py:657
  21.6 7.2 %collective-permute-start.4 = (f32[4,2048]{1,0:T(4,128)S(1)}, f32[4,2048]{1,0:T(4,128)S(1)}, u32[]{:S(2)}, u32[]{:S(2)}) collective-permute-start(f32[4,2048]{1,0:T(4,128)S(1)} %join.1.refs_0_), channel_id=1, source_target_pairs={{0,8},{1,9},{2,10},{3,11},{4,12},{5,13},{6,14},{7,15},{8,0},{9,1},... | collective-permute-start | bytes 98312 | tf_op jit(solution)/shard_map/ppermute | solution.py:657
  22.8 6.1 %collective-permute-start.3 = (f32[4,2048]{1,0:T(4,128)S(1)}, f32[4,2048]{1,0:T(4,128)S(1)}, u32[]{:S(2)}, u32[]{:S(2)}) collective-permute-start(f32[4,2048]{1,0:T(4,128)S(1)} %join.1.refs_0_), channel_id=1, source_target_pairs={{0,4},{1,5},{2,6},{3,7},{4,0},{5,1},{6,2},{7,3},{8,12},{9,13},{10,... | collective-permute-start | bytes 98312 | tf_op jit(solution)/shard_map/ppermute | solution.py:657
  29.9 19.4 %all-to-all-start.1 = ((f32[16,16,768]{2,1,0:T(8,128)}), f32[16,16,768]{2,1,0:T(8,128)S(1)}, u32[]{:S(2)}, u32[]{:S(2)}) async-start(f32[16,16,768]{2,1,0:T(8,128)} %scan.1), calls=%async_computation.1 | async-start | bytes 1572864 | tf_op jit(solution)/shard_map/all_to_all | solution.py:715
  36.7 1.0 %copy-start.2 = (f32[1,4,8,3072]{3,2,1,0:T(8,128)S(1)}, f32[1,4,8,3072]{3,2,1,0:T(8,128)}, u32[]{:S(2)}) copy-start(f32[1,4,8,3072]{3,2,1,0:T(8,128)} %param.23) | copy-start | bytes 1179652
  42.5 14.3 %collective-permute-start.8 = (f32[4,8,3072]{2,1,0:T(8,128)}, f32[4,8,3072]{2,1,0:T(8,128)}, u32[]{:S(2)}, u32[]{:S(2)}) collective-permute-start(f32[4,8,3072]{2,1,0:T(8,128)} %get-tuple-element.33), channel_id=1, source_target_pairs={{16,0},{32,16},{48,32},{64,48},{80,64},{96,80},{112,96},{128,112},... | collective-permute-start | bytes 1179656 | tf_op jit(solution)/shard_map/ppermute | solution.py:704
  50.3 7.3 %collective-permute-start.7 = (f32[40,1536]{1,0:T(8,128)}, f32[40,1536]{1,0:T(8,128)}, u32[]{:S(2)}, u32[]{:S(2)}) collective-permute-start(f32[40,1536]{1,0:T(8,128)} %get-tuple-element.32), channel_id=1, source_target_pairs={{1,0},{2,1},{3,2},{4,3},{5,4},{6,5},{7,6},{8,7},{9,8},{10,9},{11,1... | collective-permute-start | bytes 737288 | tf_op jit(solution)/shard_map/ppermute | solution.py:727
  53.0 4.6 %collective-permute-start.6 = (f32[40,1536]{1,0:T(8,128)S(1)}, f32[40,1536]{1,0:T(8,128)}, u32[]{:S(2)}, u32[]{:S(2)}) collective-permute-start(f32[40,1536]{1,0:T(8,128)S(1)} %get-tuple-element.31.after_ref), channel_id=1, source_target_pairs={{0,1},{1,2},{2,3},{3,4},{4,5},{5,6},{6,7},{7,8},{8,9},{9,10},{10,1... | collective-permute-start | bytes 737288 | tf_op jit(solution)/shard_map/ppermute | solution.py:726
  53.1 1.0 %copy-start = (f32[1,4,8,3072]{3,2,1,0:T(8,128)S(1)}, f32[1,4,8,3072]{3,2,1,0:T(8,128)}, u32[]{:S(2)}) copy-start(f32[1,4,8,3072]{3,2,1,0:T(8,128)} %param.25) | copy-start | bytes 1179652
  54.1 1.0 %copy-start.4 = (f32[1,4,8,3072]{3,2,1,0:T(8,128)S(1)}, f32[1,4,8,3072]{3,2,1,0:T(8,128)}, u32[]{:S(2)}) copy-start(f32[1,4,8,3072]{3,2,1,0:T(8,128)} %param.13) | copy-start | bytes 1179652
  55.1 1.0 %copy-start.5 = (f32[1,4,8,3072]{3,2,1,0:T(8,128)S(1)}, f32[1,4,8,3072]{3,2,1,0:T(8,128)}, u32[]{:S(2)}) copy-start(f32[1,4,8,3072]{3,2,1,0:T(8,128)} %param.14) | copy-start | bytes 1179652
  56.1 1.5 %copy-start.15 = (f32[8,128]{1,0:T(8,128)S(1)}, f32[8,128]{1,0:T(8,128)}, u32[]{:S(2)}) copy-start(f32[8,128]{1,0:T(8,128)} %get-tuple-element.34.square_ref) | copy-start | bytes 12292
  57.6 33.8 %copy-start.1 = (f32[1,4,8,3072]{3,2,1,0:T(8,128)S(1)}, f32[1,4,8,3072]{3,2,1,0:T(8,128)}, u32[]{:S(2)}) copy-start(f32[1,4,8,3072]{3,2,1,0:T(8,128)} %param.25) | copy-start | bytes 1179652
  57.6 33.8 %copy-start.3 = (f32[1,4,8,3072]{3,2,1,0:T(8,128)S(1)}, f32[1,4,8,3072]{3,2,1,0:T(8,128)}, u32[]{:S(2)}) copy-start(f32[1,4,8,3072]{3,2,1,0:T(8,128)} %param.23) | copy-start | bytes 1179652
  57.6 33.8 %copy-start.6 = (f32[1,4,8,3072]{3,2,1,0:T(8,128)S(1)}, f32[1,4,8,3072]{3,2,1,0:T(8,128)}, u32[]{:S(2)}) copy-start(f32[1,4,8,3072]{3,2,1,0:T(8,128)} %param.20) | copy-start | bytes 1179652
  57.6 33.8 %copy-start.7 = (f32[1,4,8,3072]{3,2,1,0:T(8,128)S(1)}, f32[1,4,8,3072]{3,2,1,0:T(8,128)}, u32[]{:S(2)}) copy-start(f32[1,4,8,3072]{3,2,1,0:T(8,128)} %param.22) | copy-start | bytes 1179652
  57.7 33.8 %copy-start.14 = (f32[1,1024]{1,0:T(1,128)S(1)}, f32[1,1024]{1,0:T(1,128)}, u32[]{:S(2)}) copy-start(f32[1,1024]{1,0:T(1,128)} %do_ref.1) | copy-start | bytes 12292
  63.8 27.6 %collective-permute-start.9 = (f32[4,8,3072]{2,1,0:T(8,128)S(1)}, f32[4,8,3072]{2,1,0:T(8,128)S(1)}, u32[]{:S(2)}, u32[]{:S(2)}) collective-permute-start(f32[4,8,3072]{2,1,0:T(8,128)S(1)} %get-tuple-element.37), channel_id=1, source_target_pairs={{0,16},{16,32},{32,48},{48,64},{64,80},{80,96},{96,112},{112,128},... | collective-permute-start | bytes 1179656 | tf_op jit(solution)/shard_map/ppermute | solution.py:757

commit v6 on v5

--- a/solution.py
+++ b/solution.py
@@ -203,7 +203,7 @@
         )
         return carry
 
-    lax.fori_loop(0, rank_ref.shape[0], one_chunk, 0, unroll=4)
+    lax.fori_loop(0, rank_ref.shape[0], one_chunk, 0, unroll=8)
 
 
 def sections(chunks, lane_groups):
@@ -328,7 +328,7 @@
             hot_s[:, at] = jnp.where(row == group_id, one, zero)
             return carry
 
-        lax.fori_loop(0, chunks, one_chunk, 0, unroll=4)
+        lax.fori_loop(0, chunks, one_chunk, 0, unroll=8)
         return jnp.dot(
             hot_s[...], high_s[...], preferred_element_type=jnp.float32
         ) + jnp.dot(hot_s[...], low_s[...], preferred_element_type=jnp.float32)
@@ -391,9 +391,18 @@
     return jnp.where(last, jnp.broadcast_to(edge, v.shape), pltpu.roll(v, v.shape[0] - 1, 0))
 
 
-def image_kernel(windows, bricks, window_ref, at_ref, passes_ref, back_ref, below_ref, above_ref, args_ref,
-                 bundle_ref, rm_next_ref, square_ref, table_ref, next_ref, state_ref, sent_ref,
-                 fields, rank_ref, code_ref, again_codes, again_groups, hot_s, found):
+def image_kernel(windows, bricks, window_ref, at_ref, passes_ref, back_ref, below_hbm, above_hbm, args_ref,
+                 bundle_ref, rm_next_hbm, square_ref, table_ref, next_ref, state_ref, sent_ref,
+                 fields, rank_ref, code_ref, again_codes, again_groups, hot_s, found,
+                 below_ref, above_ref, rm_next_ref, sems):
+    arrivals = [
+        pltpu.make_async_copy(a, b, sems.at[i])
+        for i, (a, b) in enumerate(
+            ((below_hbm, below_ref), (above_hbm, above_ref), (rm_next_hbm, rm_next_ref))
+        )
+    ]
+    for copy in arrivals:
+        copy.start()
     levels, rows, columns = rm_next_ref.shape
     parts, _, width = back_ref.shape
     per_level = parts // levels
@@ -404,6 +413,24 @@
     window, here = window_ref[0], at_ref[0]
     has_below = jnp.where(here > 0, 1.0, 0.0)
     has_above = jnp.where(here < bricks - 1, 1.0, 0.0)
+
+    groups = levels * lane_groups * 8
+    group_id = lax.broadcasted_iota(jnp.int32, (LANES, groups), 1).astype(jnp.int16)
+    one, zero = jnp.ones((), jnp.bfloat16), jnp.zeros((), jnp.bfloat16)
+
+    def make_hot(codes_ref):
+        def one_chunk(k, carry):
+            at = pl.ds(pl.multiple_of(k * LANES, LANES), LANES)
+            group = (codes_ref[at, :].astype(jnp.int32) >> 8).astype(jnp.int16)
+            wide = jnp.concatenate([group] * (groups // LANES), axis=1)
+            hot_s[at, :] = jnp.where(wide == group_id, one, zero)
+            return carry
+
+        lax.fori_loop(0, chunks, one_chunk, 0, unroll=8)
+
+    make_hot(table_ref)
+    for copy in arrivals:
+        copy.wait()
 
     row_id = lax.broadcasted_iota(jnp.int32, (rows, columns), 0)
     first, last = row_id == 0, row_id == rows - 1
@@ -465,21 +492,15 @@
             fields[at : at + 8, LANES : 2 * LANES] = after_one[:, cols]
 
     high_fields, low_fields = split_two(fields[...])
-    groups = levels * lane_groups * 8
-    together = hot_s.shape[0] // LANES
-    group_id = lax.broadcasted_iota(jnp.int32, (LANES, groups), 1).astype(jnp.int16)
-    one, zero = jnp.ones((), jnp.bfloat16), jnp.zeros((), jnp.bfloat16)
+    together = min(4, chunks)
 
     def look_up(first, fresh, codes_ref):
         def some_chunks(q, carry):
-            codes = []
-            for j in range(together):
-                k = q * together + j
-                code = codes_ref[pl.ds(pl.multiple_of(k * LANES, LANES), LANES), :].astype(jnp.int32)
-                wide = jnp.concatenate([(code >> 8).astype(jnp.int16)] * (groups // LANES), axis=1)
-                hot_s[j * LANES : (j + 1) * LANES, :] = jnp.where(wide == group_id, one, zero)
-                codes.append(code & 255)
-            picks = hot_s[...]
+            codes = [
+                codes_ref[pl.ds(pl.multiple_of((q * together + j) * LANES, LANES), LANES), :].astype(jnp.int32) & 255
+                for j in range(together)
+            ]
+            picks = hot_s[pl.ds(pl.multiple_of(q * together * LANES, together * LANES), together * LANES), :]
             picked = jnp.dot(
                 picks, high_fields, preferred_element_type=jnp.float32
             ) + jnp.dot(picks, low_fields, preferred_element_type=jnp.float32)
@@ -512,6 +533,7 @@
     def one_more(number, carry):
         code_ref[...] = unfold(table_ref, places["code"], chunks).astype(jnp.int32)
         build_slots(rank_ref, code_ref, number * SLOTS, again_codes, again_groups)
+        make_hot(again_codes)
         look_up(number * SLOTS, False, again_codes)
         return carry
 
@@ -741,13 +763,16 @@
         out_shape=(
             f32(levels, rows, columns), f32(levels, rows, columns), f32(blocks, 1, CHUNK + LANES),
         ),
-        in_specs=[SMEM, SMEM, SMEM] + [VMEM] * 8,
+        in_specs=[SMEM] * 3 + [VMEM, HBM, HBM, VMEM, VMEM, HBM, VMEM, VMEM],
         out_specs=(VMEM, VMEM, VMEM),
         scratch_shapes=[
             pltpu.VMEM((groups, 2 * LANES), jnp.float32),
             table_s, table_s, codes_s, groups_s,
-            pltpu.VMEM((min(4, blocks) * LANES, groups), jnp.bfloat16),
+            pltpu.VMEM((slots, groups), jnp.bfloat16),
             line_s,
+            pltpu.VMEM((40, columns // 2), jnp.float32), pltpu.VMEM((40, columns // 2), jnp.float32),
+            pltpu.VMEM((levels, rows, columns), jnp.float32),
+            pltpu.SemaphoreType.DMA((3,)),
         ],
         compiler_params=params(24),
         cost_estimate=cost(1, 1),

time: 94.4 us -> 94.2 us (level)
  no operation moved by 1% of the time
where the time goes in v6:
time: 94.2 us; the launch traced here: 93.7 us
  starting transfers between devices  30.5 us (32%)
  blocking collectives  26.4 us (28%)
  Pallas kernels  19.5 us (21%)
  waiting for transfers between devices  12.1 us (13%)
  local copies, waits for them, and re-layouts  4.05 us (4%)
  between operations  1.04 us (1%)
    all_to_all x1, blocking collectives, body(): got = lax.all_to_all(sent, 'space', 0, 0)  14.5 us
    all_to_all x1, blocking collectives, body(): all_sums = lax.all_to_all(sums, 'tm', 0, 0)  11.9 us
    ppermute x6, starting transfers between devices, body(): lax.ppermute(near, 'space', [(i, i ^ distance * k) for i in range(bricks)])  10.4 us
    all_to_all x1, starting transfers between devices, body(): windows_of = lax.all_to_all(packed, 'tm', 0, 0)  7.73 us
    all_to_all x1, starting transfers between devices, body(): back = lax.all_to_all(summed, 'tm', 0, 0)  6.86 us
    pallas_call x1, Pallas kernels, body(): pl.pallas_call(functools.partial(image_kernel, windows, bricks), out_shap...  5.92 us
    ppermute x6, waiting for transfers between devices, body(): lax.ppermute(near, 'space', [(i, i ^ distance * k) for i in range(bricks)])  5.36 us
    all_to_all x1, waiting for transfers between devices, body(): back = lax.all_to_all(summed, 'tm', 0, 0)  5.35 us
  transfers between devices with their start and end apart: 12, of which 6 were waited for; matrix products, arithmetic and copies ran while one was open for 0% of the time, Pallas kernels for 8%

profile of v6, /device:TPU:1, one launch (start us, length us, event | category | flops | bytes accessed | tf_op | source)
XLA Modules:
  0.0 93.7 jit_solution(15106556315663902681)
XLA Ops:
  0.6 2.6 %pack.1 = (f32[16,24,768]{2,1,0:T(8,128)}, f32[8,128]{1,0:T(8,128)}, f32[24,3072]{1,0:T(8,128)}) custom-call(f32[4,8,3072]{2,1,0:T(8,128)} %bitcast.13, f32[4,8,3072]{2,1,0:T(8,128)} %bitcast.16, f32[4,8,3072]{2,1,0:T(8,128)} %bitcast.25, f32[4,8,3072]{2,1,0:T(8,128)} %bitcast.19, f32[4,8,3072]{2,1,0:T(8,128)} %bitcast.21), custom_call_target="tpu_custom_call" | custom-call | flops 1 | bytes 1 | tf_op jit(solution)/shard_map/pack/pallas_call | solution.py:635
  3.2 0.0 copy-start.12
  3.2 0.0 copy-start.13
  3.2 0.0 copy-start.8
  3.2 0.0 copy-start.9
  3.3 0.0 copy-start.10
  3.3 0.0 copy-start.11
  3.3 7.7 %all-to-all-start = ((f32[16,24,768]{2,1,0:T(8,128)}), f32[16,24,768]{2,1,0:T(8,128)S(1)}, u32[]{:S(2)}, u32[]{:S(2)}) async-start(f32[16,24,768]{2,1,0:T(8,128)} %get-tuple-element.28), calls=%async_computation | async-start | bytes 2359296 | tf_op jit(solution)/shard_map/all_to_all | solution.py:652
  11.0 0.0 copy-done.12
  11.0 0.0 copy-done.13
  11.1 2.6 %collective-permute-start.2 = (f32[1,2048]{1,0:T(1,128)S(1)}, f32[1,2048]{1,0:T(1,128)S(1)}, u32[]{:S(2)}, u32[]{:S(2)}) collective-permute-start(f32[1,2048]{1,0:T(1,128)S(1)} %duals.1.refs_0_), channel_id=1, source_target_pairs={{0,3},{1,2},{2,1},{3,0},{4,7},{5,6},{6,5},{7,4},{8,11},{9,10},{10,... | collective-permute-start | bytes 24584 | tf_op jit(solution)/shard_map/ppermute | solution.py:666
  13.6 0.0 collective-permute-start.1
  13.6 0.5 collective-permute-start
  14.1 0.8 collective-permute-done.2.refs_3_
  15.0 1.5 %collective-permute-done.1.refs_2_ = f32[1,2048]{1,0:T(1,128)S(1)} collective-permute-done((f32[1,2048]{1,0:T(1,128)S(1)}, f32[1,2048]{1,0:T(1,128)S(1)}, u32[]{:S(2)}, u32[]{:S(2)}) %collective-permute-start.1) | collective-permute-done | bytes 8224 | tf_op jit(solution)/shard_map/ppermute | solution.py:666
  16.5 0.0 collective-permute-done.refs_1_
  16.5 5.1 %collective-permute-start.5 = (f32[4,2048]{1,0:T(4,128)S(1)}, f32[4,2048]{1,0:T(4,128)S(1)}, u32[]{:S(2)}, u32[]{:S(2)}) collective-permute-start(f32[4,2048]{1,0:T(4,128)S(1)} %join.1.refs_0_), channel_id=1, source_target_pairs={{0,12},{1,13},{2,14},{3,15},{4,8},{5,9},{6,10},{7,11},{8,4},{9,5},... | collective-permute-start | bytes 98312 | tf_op jit(solution)/shard_map/ppermute | solution.py:679
  21.6 1.2 %collective-permute-start.4 = (f32[4,2048]{1,0:T(4,128)S(1)}, f32[4,2048]{1,0:T(4,128)S(1)}, u32[]{:S(2)}, u32[]{:S(2)}) collective-permute-start(f32[4,2048]{1,0:T(4,128)S(1)} %join.1.refs_0_), channel_id=1, source_target_pairs={{0,8},{1,9},{2,10},{3,11},{4,12},{5,13},{6,14},{7,15},{8,0},{9,1},... | collective-permute-start | bytes 98312 | tf_op jit(solution)/shard_map/ppermute | solution.py:679
  22.8 1.0 %collective-permute-start.3 = (f32[4,2048]{1,0:T(4,128)S(1)}, f32[4,2048]{1,0:T(4,128)S(1)}, u32[]{:S(2)}, u32[]{:S(2)}) collective-permute-start(f32[4,2048]{1,0:T(4,128)S(1)} %join.1.refs_0_), channel_id=1, source_target_pairs={{0,4},{1,5},{2,6},{3,7},{4,0},{5,1},{6,2},{7,3},{8,12},{9,13},{10,... | collective-permute-start | bytes 98312 | tf_op jit(solution)/shard_map/ppermute | solution.py:679
  23.8 0.0 copy-done.8
  23.8 0.0 copy-done.9
  23.8 0.0 copy-done.10
  23.8 0.0 copy-done.11
  23.8 2.0 %places.1 = (f32[2896,128]{1,0:T(8,128)S(1)}, s32[1]{0:T(128)}) custom-call(s32[1]{0:T(128)} %bitcast.1.at_ref, s32[1,16384]{1,0:T(1,128)S(1)} %copy-done.9, s32[1,16384]{1,0:T(1,128)S(1)} %copy-done.10, s32[1,16384]{1,0:T(1,128)S(1)} %copy-done.11, f32[24,3072]{1,0:T(8,128)S(1)} %copy-done.8), custom_call_target="tpu_custom_call" | custom-call | flops 1 | bytes 1 | tf_op jit(solution)/shard_map/places/pallas_call | solution.py:689
  25.9 0.0 collective-permute-done.5.refs_3_
  25.9 3.0 %collective-permute-done.4.refs_2_ = f32[4,2048]{1,0:T(4,128)S(1)} collective-permute-done((f32[4,2048]{1,0:T(4,128)S(1)}, f32[4,2048]{1,0:T(4,128)S(1)}, u32[]{:S(2)}, u32[]{:S(2)}) %collective-permute-start.4) | collective-permute-done | bytes 32800 | tf_op jit(solution)/shard_map/ppermute | solution.py:679
  28.8 0.0 collective-permute-done.3.refs_1_
  28.9 0.0 all-to-all-done.in_ref
  28.9 1.0 %scan.1 = f32[16,16,768]{2,1,0:T(8,128)} custom-call(f32[16,24,768]{2,1,0:T(8,128)S(1)} %all-to-all-done.in_ref, f32[2896,128]{1,0:T(8,128)S(1)} %get-tuple-element.29.rest_0_.table_ref, f32[16,2048]{1,0:T(8,128)S(1)} %collect.1.rest_1_.lines_ref), custom_call_target="tpu_custom_call" | custom-call | flops 1 | bytes 1 | tf_op jit(solution)/shard_map/scan/pallas_call | solution.py:728
  29.9 6.9 %all-to-all-start.1 = ((f32[16,16,768]{2,1,0:T(8,128)}), f32[16,16,768]{2,1,0:T(8,128)S(1)}, u32[]{:S(2)}, u32[]{:S(2)}) async-start(f32[16,16,768]{2,1,0:T(8,128)} %scan.1), calls=%async_computation.1 | async-start | bytes 1572864 | tf_op jit(solution)/shard_map/all_to_all | solution.py:737
  36.7 0.0 copy-start.2
  36.8 1.0 %copy-done.2 = f32[1,4,8,3072]{3,2,1,0:T(8,128)S(1)} copy-done((f32[1,4,8,3072]{3,2,1,0:T(8,128)S(1)}, f32[1,4,8,3072]{3,2,1,0:T(8,128)}, u32[]{:S(2)}) %copy-start.2) | copy-done | bytes 393240
  37.7 4.7 %spread.1 = (f32[10,8,3072]{2,1,0:T(8,128)S(1)}, f32[4,8,3072]{2,1,0:T(8,128)}) custom-call(s32[1]{0:T(128)} %get-tuple-element.27.passes_ref, f32[2896,128]{1,0:T(8,128)S(1)} %get-tuple-element.29.rest_0_.table_ref, f32[16,2048]{1,0:T(8,128)S(1)} %collect.1.rest_1_.lines_ref, f32[4,8,3072]{2,1,0:T(8,128)S(1)} %bitcast.17), custom_call_target="tpu_custom_call" | custom-call | flops 1 | bytes 1 | tf_op jit(solution)/shard_map/spread/pallas_call | solution.py:708
  42.4 1.5 %collective-permute-start.8 = (f32[4,8,3072]{2,1,0:T(8,128)}, f32[4,8,3072]{2,1,0:T(8,128)}, u32[]{:S(2)}, u32[]{:S(2)}) collective-permute-start(f32[4,8,3072]{2,1,0:T(8,128)} %get-tuple-element.33), channel_id=1, source_target_pairs={{16,0},{32,16},{48,32},{64,48},{80,64},{96,80},{112,96},{128,112},... | collective-permute-start | bytes 1179656 | tf_op jit(solution)/shard_map/ppermute | solution.py:726
  43.9 5.4 %all-to-all-done.1.back_ref = f32[16,16,768]{2,1,0:T(8,128)S(1)} async-done(((f32[16,16,768]{2,1,0:T(8,128)}), f32[16,16,768]{2,1,0:T(8,128)S(1)}, u32[]{:S(2)}, u32[]{:S(2)}) %all-to-all-start.1) | async-done | bytes 786464 | tf_op jit(solution)/shard_map/all_to_all | solution.py:737
  49.2 1.0 %edges.1 = (f32[40,1536]{1,0:T(8,128)S(1)}, f32[40,1536]{1,0:T(8,128)}) custom-call(f32[16,16,768]{2,1,0:T(8,128)S(1)} %all-to-all-done.1.back_ref, f32[10,8,3072]{2,1,0:T(8,128)S(1)} %get-tuple-element.30.bundle_ref, f32[2896,128]{1,0:T(8,128)S(1)} %get-tuple-element.29.rest_0_.table_ref), custom_call_target="tpu_custom_call" | custom-call | flops 1 | bytes 1 | tf_op jit(solution)/shard_map/edges/pallas_call | solution.py:738
  50.3 2.8 %collective-permute-start.7 = (f32[40,1536]{1,0:T(8,128)}, f32[40,1536]{1,0:T(8,128)}, u32[]{:S(2)}, u32[]{:S(2)}) collective-permute-start(f32[40,1536]{1,0:T(8,128)} %get-tuple-element.32), channel_id=1, source_target_pairs={{1,0},{2,1},{3,2},{4,3},{5,4},{6,5},{7,6},{8,7},{9,8},{10,9},{11,1... | collective-permute-start | bytes 737288 | tf_op jit(solution)/shard_map/ppermute | solution.py:749
  53.0 0.1 collective-permute-start.6
  53.1 0.0 copy-start
  53.1 1.0 %copy-done = f32[1,4,8,3072]{3,2,1,0:T(8,128)S(1)} copy-done((f32[1,4,8,3072]{3,2,1,0:T(8,128)S(1)}, f32[1,4,8,3072]{3,2,1,0:T(8,128)}, u32[]{:S(2)}) %copy-start) | copy-done | bytes 393240
  54.1 0.0 copy-start.4
  54.1 1.0 %copy-done.4 = f32[1,4,8,3072]{3,2,1,0:T(8,128)S(1)} copy-done((f32[1,4,8,3072]{3,2,1,0:T(8,128)S(1)}, f32[1,4,8,3072]{3,2,1,0:T(8,128)}, u32[]{:S(2)}) %copy-start.4) | copy-done | bytes 393240
  55.1 0.0 copy-start.5
  55.1 1.0 %copy-done.5 = f32[1,4,8,3072]{3,2,1,0:T(8,128)S(1)} copy-done((f32[1,4,8,3072]{3,2,1,0:T(8,128)S(1)}, f32[1,4,8,3072]{3,2,1,0:T(8,128)}, u32[]{:S(2)}) %copy-start.5) | copy-done | bytes 393240
  56.1 0.1 fields.1.args_ref
  56.2 0.6 collective-permute-done.8.rm_next_hbm
  56.8 0.8 collective-permute-done.7.above_hbm
  57.6 0.0 collective-permute-done.6.below_hbm
  57.6 0.0 copy-done.15
  57.6 0.0 copy-start.3
  57.6 0.0 copy-start.6
  57.6 0.0 copy-start.7
  57.7 0.0 copy-start.14
  57.7 5.9 %images.1 = (f32[4,8,3072]{2,1,0:T(8,128)S(1)}, f32[4,8,3072]{2,1,0:T(8,128)S(1)}, f32[16,1,1152]{2,1,0:T(1,128)S(1)}) custom-call(s32[1]{0:T(128)} %bitcast.window_ref, s32[1]{0:T(128)} %bitcast.1.at_ref, s32[1]{0:T(128)} %get-tuple-element.27.passes_ref, f32[16,16,768]{2,1,0:T(8,128)S(1)} %all-to-all-done.1.back_ref, ...), custom_call_target="tpu_custom_call" | custom-call | flops 1 | bytes 1 | tf_op jit(solution)/shard_map/images/pallas_call | solution.py:761
  63.6 1.2 %collective-permute-start.9 = (f32[4,8,3072]{2,1,0:T(8,128)S(1)}, f32[4,8,3072]{2,1,0:T(8,128)S(1)}, u32[]{:S(2)}, u32[]{:S(2)}) collective-permute-start(f32[4,8,3072]{2,1,0:T(8,128)S(1)} %get-tuple-element.37), channel_id=1, source_target_pairs={{0,16},{16,32},{32,48},{48,64},{64,80},{80,96},{96,112},{112,128},... | collective-permute-start | bytes 1179656 | tf_op jit(solution)/shard_map/ppermute | solution.py:782
  64.8 14.5 %all_to_all.20.got_ref = f32[16,1,1152]{2,1,0:T(1,128)S(1)} all-to-all(f32[16,1,1152]{2,1,0:T(1,128)S(1)} %get-tuple-element.35), channel_id=1, replica_groups=mesh['tm'=16,'space'=16] {'space'}, dimensions={0} | all-to-all | bytes 147456 | tf_op jit(solution)/shard_map/all_to_all | solution.py:783
  79.3 11.9 %all_to_all.21.sums_ref = f32[16,1,128]{2,1,0:T(1,128)S(1)} all-to-all(f32[16,1,128]{2,1,0:T(1,128)S(1)} %get-tuple-element.36), channel_id=1, replica_groups=mesh['tm'=16,'space'=16] {'tm'}, dimensions={0} | all-to-all | bytes 16384 | tf_op jit(solution)/shard_map/all_to_all | solution.py:793
  91.2 0.0 collective-permute-done.9.image_ref
  91.2 0.0 copy-done.1
  91.2 0.0 copy-done.3
  91.2 0.0 copy-done.6
  91.2 0.0 copy-done.7
  91.3 0.0 copy-done.14
  91.3 2.2 %updates.1 = (f32[4,8,3072]{2,1,0:T(8,128)}, f32[1,1024]{1,0:T(1,128)}, f32[4,8,3072]{2,1,0:T(8,128)}, f32[4,8,3072]{2,1,0:T(8,128)}, f32[1,1024]{1,0:T(1,128)}, /*index=5*/f32[4,8,3072]{2,1,0:T(8,128)}) custom-call(s32[1]{0:T(128)} %bitcast.window_ref, f32[16,1,128]{2,1,0:T(1,128)S(1)} %all_to_all.21.sums_ref, f32[4,8,3072]{2,1,0:T(8,128)S(1)} %bitcast.23, ...), custom_call_target="tpu_custom_call" | custom-call | flops 1 | bytes 1 | tf_op jit(solution)/shard_map/updates/pallas_call | solution.py:796
  (6 shorter events, 0.1 us)
Async XLA Ops:
  3.2 7.8 %copy-start.12 = (f32[1,1024]{1,0:T(1,128)S(1)}, f32[1,1024]{1,0:T(1,128)}, u32[]{:S(2)}) copy-start(f32[1,1024]{1,0:T(1,128)} %ro_ref.3) | copy-start | bytes 12292
  3.2 7.8 %copy-start.13 = (f32[1,1024]{1,0:T(1,128)S(1)}, f32[1,1024]{1,0:T(1,128)}, u32[]{:S(2)}) copy-start(f32[1,1024]{1,0:T(1,128)} %ov_ref.3) | copy-start | bytes 12292
  3.2 20.6 %copy-start.8 = (f32[24,3072]{1,0:T(8,128)S(1)}, f32[24,3072]{1,0:T(8,128)}, u32[]{:S(2)}) copy-start(f32[24,3072]{1,0:T(8,128)} %get-tuple-element.26.rows_ref) | copy-start | bytes 884740
  3.2 20.6 %copy-start.9 = (s32[1,16384]{1,0:T(1,128)S(1)}, s32[1,16384]{1,0:T(1,128)}, u32[]{:S(2)}) copy-start(s32[1,16384]{1,0:T(1,128)} %brick_ref.1) | copy-start | bytes 196612
  3.3 20.5 %copy-start.10 = (s32[1,16384]{1,0:T(1,128)S(1)}, s32[1,16384]{1,0:T(1,128)}, u32[]{:S(2)}) copy-start(s32[1,16384]{1,0:T(1,128)} %cell_ref.1) | copy-start | bytes 196612
  3.3 20.5 %copy-start.11 = (s32[1,16384]{1,0:T(1,128)S(1)}, s32[1,16384]{1,0:T(1,128)}, u32[]{:S(2)}) copy-start(s32[1,16384]{1,0:T(1,128)} %step_ref.1) | copy-start | bytes 196612
  3.3 25.6 %all-to-all-start = ((f32[16,24,768]{2,1,0:T(8,128)}), f32[16,24,768]{2,1,0:T(8,128)S(1)}, u32[]{:S(2)}, u32[]{:S(2)}) async-start(f32[16,24,768]{2,1,0:T(8,128)} %get-tuple-element.28), calls=%async_computation | async-start | bytes 2359296 | tf_op jit(solution)/shard_map/all_to_all | solution.py:652
  11.1 3.9 %collective-permute-start.2 = (f32[1,2048]{1,0:T(1,128)S(1)}, f32[1,2048]{1,0:T(1,128)S(1)}, u32[]{:S(2)}, u32[]{:S(2)}) collective-permute-start(f32[1,2048]{1,0:T(1,128)S(1)} %duals.1.refs_0_), channel_id=1, source_target_pairs={{0,3},{1,2},{2,1},{3,0},{4,7},{5,6},{6,5},{7,4},{8,11},{9,10},{10,... | collective-permute-start | bytes 24584 | tf_op jit(solution)/shard_map/ppermute | solution.py:666
  13.6 2.9 %collective-permute-start.1 = (f32[1,2048]{1,0:T(1,128)S(1)}, f32[1,2048]{1,0:T(1,128)S(1)}, u32[]{:S(2)}, u32[]{:S(2)}) collective-permute-start(f32[1,2048]{1,0:T(1,128)S(1)} %duals.1.refs_0_), channel_id=1, source_target_pairs={{0,2},{1,3},{2,0},{3,1},{4,6},{5,7},{6,4},{7,5},{8,10},{9,11},{10,... | collective-permute-start | bytes 24584 | tf_op jit(solution)/shard_map/ppermute | solution.py:666
  13.6 2.9 %collective-permute-start = (f32[1,2048]{1,0:T(1,128)S(1)}, f32[1,2048]{1,0:T(1,128)S(1)}, u32[]{:S(2)}, u32[]{:S(2)}) collective-permute-start(f32[1,2048]{1,0:T(1,128)S(1)} %duals.1.refs_0_), channel_id=1, source_target_pairs={{0,1},{1,0},{2,3},{3,2},{4,5},{5,4},{6,7},{7,6},{8,9},{9,8},{10,11... | collective-permute-start | bytes 24584 | tf_op jit(solution)/shard_map/ppermute | solution.py:666
  16.5 9.4 %collective-permute-start.5 = (f32[4,2048]{1,0:T(4,128)S(1)}, f32[4,2048]{1,0:T(4,128)S(1)}, u32[]{:S(2)}, u32[]{:S(2)}) collective-permute-start(f32[4,2048]{1,0:T(4,128)S(1)} %join.1.refs_0_), channel_id=1, source_target_pairs={{0,12},{1,13},{2,14},{3,15},{4,8},{5,9},{6,10},{7,11},{8,4},{9,5},... | collective-permute-start | bytes 98312 | tf_op jit(solution)/shard_map/ppermute | solution.py:679
  21.6 7.2 %collective-permute-start.4 = (f32[4,2048]{1,0:T(4,128)S(1)}, f32[4,2048]{1,0:T(4,128)S(1)}, u32[]{:S(2)}, u32[]{:S(2)}) collective-permute-start(f32[4,2048]{1,0:T(4,128)S(1)} %join.1.refs_0_), channel_id=1, source_target_pairs={{0,8},{1,9},{2,10},{3,11},{4,12},{5,13},{6,14},{7,15},{8,0},{9,1},... | collective-permute-start | bytes 98312 | tf_op jit(solution)/shard_map/ppermute | solution.py:679
  22.8 6.1 %collective-permute-start.3 = (f32[4,2048]{1,0:T(4,128)S(1)}, f32[4,2048]{1,0:T(4,128)S(1)}, u32[]{:S(2)}, u32[]{:S(2)}) collective-permute-start(f32[4,2048]{1,0:T(4,128)S(1)} %join.1.refs_0_), channel_id=1, source_target_pairs={{0,4},{1,5},{2,6},{3,7},{4,0},{5,1},{6,2},{7,3},{8,12},{9,13},{10,... | collective-permute-start | bytes 98312 | tf_op jit(solution)/shard_map/ppermute | solution.py:679
  29.9 19.4 %all-to-all-start.1 = ((f32[16,16,768]{2,1,0:T(8,128)}), f32[16,16,768]{2,1,0:T(8,128)S(1)}, u32[]{:S(2)}, u32[]{:S(2)}) async-start(f32[16,16,768]{2,1,0:T(8,128)} %scan.1), calls=%async_computation.1 | async-start | bytes 1572864 | tf_op jit(solution)/shard_map/all_to_all | solution.py:737
  36.7 1.0 %copy-start.2 = (f32[1,4,8,3072]{3,2,1,0:T(8,128)S(1)}, f32[1,4,8,3072]{3,2,1,0:T(8,128)}, u32[]{:S(2)}) copy-start(f32[1,4,8,3072]{3,2,1,0:T(8,128)} %param.23) | copy-start | bytes 1179652
  42.4 14.4 %collective-permute-start.8 = (f32[4,8,3072]{2,1,0:T(8,128)}, f32[4,8,3072]{2,1,0:T(8,128)}, u32[]{:S(2)}, u32[]{:S(2)}) collective-permute-start(f32[4,8,3072]{2,1,0:T(8,128)} %get-tuple-element.33), channel_id=1, source_target_pairs={{16,0},{32,16},{48,32},{64,48},{80,64},{96,80},{112,96},{128,112},... | collective-permute-start | bytes 1179656 | tf_op jit(solution)/shard_map/ppermute | solution.py:726
  50.3 7.3 %collective-permute-start.7 = (f32[40,1536]{1,0:T(8,128)}, f32[40,1536]{1,0:T(8,128)}, u32[]{:S(2)}, u32[]{:S(2)}) collective-permute-start(f32[40,1536]{1,0:T(8,128)} %get-tuple-element.32), channel_id=1, source_target_pairs={{1,0},{2,1},{3,2},{4,3},{5,4},{6,5},{7,6},{8,7},{9,8},{10,9},{11,1... | collective-permute-start | bytes 737288 | tf_op jit(solution)/shard_map/ppermute | solution.py:749
  53.0 4.6 %collective-permute-start.6 = (f32[40,1536]{1,0:T(8,128)S(1)}, f32[40,1536]{1,0:T(8,128)}, u32[]{:S(2)}, u32[]{:S(2)}) collective-permute-start(f32[40,1536]{1,0:T(8,128)S(1)} %get-tuple-element.31.after_ref), channel_id=1, source_target_pairs={{0,1},{1,2},{2,3},{3,4},{4,5},{5,6},{6,7},{7,8},{8,9},{9,10},{10,1... | collective-permute-start | bytes 737288 | tf_op jit(solution)/shard_map/ppermute | solution.py:748
  53.1 1.0 %copy-start = (f32[1,4,8,3072]{3,2,1,0:T(8,128)S(1)}, f32[1,4,8,3072]{3,2,1,0:T(8,128)}, u32[]{:S(2)}) copy-start(f32[1,4,8,3072]{3,2,1,0:T(8,128)} %param.25) | copy-start | bytes 1179652
  54.1 1.0 %copy-start.4 = (f32[1,4,8,3072]{3,2,1,0:T(8,128)S(1)}, f32[1,4,8,3072]{3,2,1,0:T(8,128)}, u32[]{:S(2)}) copy-start(f32[1,4,8,3072]{3,2,1,0:T(8,128)} %param.13) | copy-start | bytes 1179652
  55.1 1.0 %copy-start.5 = (f32[1,4,8,3072]{3,2,1,0:T(8,128)S(1)}, f32[1,4,8,3072]{3,2,1,0:T(8,128)}, u32[]{:S(2)}) copy-start(f32[1,4,8,3072]{3,2,1,0:T(8,128)} %param.14) | copy-start | bytes 1179652
  56.1 1.5 %copy-start.15 = (f32[8,128]{1,0:T(8,128)S(1)}, f32[8,128]{1,0:T(8,128)}, u32[]{:S(2)}) copy-start(f32[8,128]{1,0:T(8,128)} %get-tuple-element.34.square_ref) | copy-start | bytes 12292
  57.6 33.6 %copy-start.1 = (f32[1,4,8,3072]{3,2,1,0:T(8,128)S(1)}, f32[1,4,8,3072]{3,2,1,0:T(8,128)}, u32[]{:S(2)}) copy-start(f32[1,4,8,3072]{3,2,1,0:T(8,128)} %param.25) | copy-start | bytes 1179652
  57.6 33.6 %copy-start.3 = (f32[1,4,8,3072]{3,2,1,0:T(8,128)S(1)}, f32[1,4,8,3072]{3,2,1,0:T(8,128)}, u32[]{:S(2)}) copy-start(f32[1,4,8,3072]{3,2,1,0:T(8,128)} %param.23) | copy-start | bytes 1179652
  57.6 33.6 %copy-start.6 = (f32[1,4,8,3072]{3,2,1,0:T(8,128)S(1)}, f32[1,4,8,3072]{3,2,1,0:T(8,128)}, u32[]{:S(2)}) copy-start(f32[1,4,8,3072]{3,2,1,0:T(8,128)} %param.20) | copy-start | bytes 1179652
  57.6 33.6 %copy-start.7 = (f32[1,4,8,3072]{3,2,1,0:T(8,128)S(1)}, f32[1,4,8,3072]{3,2,1,0:T(8,128)}, u32[]{:S(2)}) copy-start(f32[1,4,8,3072]{3,2,1,0:T(8,128)} %param.22) | copy-start | bytes 1179652
  57.7 33.6 %copy-start.14 = (f32[1,1024]{1,0:T(1,128)S(1)}, f32[1,1024]{1,0:T(1,128)}, u32[]{:S(2)}) copy-start(f32[1,1024]{1,0:T(1,128)} %do_ref.1) | copy-start | bytes 12292
  63.6 27.6 %collective-permute-start.9 = (f32[4,8,3072]{2,1,0:T(8,128)S(1)}, f32[4,8,3072]{2,1,0:T(8,128)S(1)}, u32[]{:S(2)}, u32[]{:S(2)}) collective-permute-start(f32[4,8,3072]{2,1,0:T(8,128)S(1)} %get-tuple-element.37), channel_id=1, source_target_pairs={{0,16},{16,32},{32,48},{48,64},{64,80},{80,96},{96,112},{112,128},... | collective-permute-start | bytes 1179656 | tf_op jit(solution)/shard_map/ppermute | solution.py:782
